TPU v7x, 128 devices: a whole 4x4x4 slice. The times are simulated.
128 devices in a mesh: seqin: 4 (over y), seqout: 8 (over x, core), head: 4 (over z).
Axes of the slice: x: 4, y: 4, z: 4, core: 2. Of those that a mesh axis runs over, the one named last changes fastest.
Arguments:
- queries: bfloat16 [32768, 4096], P(('seqin', 'seqout'), 'head'), may hold values from -6 to 6
- keys: bfloat16 [32768, 4096], P(('seqin', 'seqout'), 'head'), may hold values from -6 to 6
- values: bfloat16 [32768, 4096], P(('seqin', 'seqout'), 'head'), may hold values from -120 to 120
- gain: float32 [4096], P('head'), may hold values from 0.5 to 1.5
- cotangent: bfloat16 [32768, 4096], P(('seqin', 'seqout'), 'head'), may hold values from -6 to 6
Outputs:
- mixed: bfloat16 [32768, 4096], P(('seqin', 'seqout'), 'head')
- grad_queries: bfloat16 [32768, 4096], P(('seqin', 'seqout'), 'head')
- grad_keys: bfloat16 [32768, 4096], P(('seqin', 'seqout'), 'head')
- grad_values: bfloat16 [32768, 4096], P(('seqin', 'seqout'), 'head')
All inputs are finite; a program needn't handle non-finite values.
Results may differ from a plain program's by a relative error of at most 0.0089.
Values sent between devices are 32-bit elements; how exact they have to be, the bound alone decides.
No kernel may reach another device: no remote copies, remote signals or barrier semaphores. Data moves between devices by JAX's collectives and lax.ppermute only.
A program may use at most 192 MiB of HBM per device.

v0:
```python
import functools

import jax
import jax.numpy as jnp
from jax import lax
from jax.experimental import pallas as pl
from jax.experimental.pallas import tpu as pltpu
from jax.sharding import PartitionSpec as P

E = 128
D = 4096
ROWS = 1024
BLOCK = 512
HALF = 256
AUG = E + 8
F32 = jnp.float32
BF16 = jnp.bfloat16
VMEM_LIMIT = 18 * 1024 * 1024


def phi(x):
    xf = x.astype(F32)
    return jnp.where(xf > 0, xf + 1.0, jnp.exp(jnp.minimum(xf, 0.0))).astype(BF16)


def slope(x):
    xf = x.astype(F32)
    return jnp.where(xf > 0, 1.0, jnp.exp(jnp.minimum(xf, 0.0)))


def split(x):
    hi = x.astype(BF16)
    return hi, (x - hi.astype(F32)).astype(BF16)


def dot(a, b, ca=1, cb=0):
    return lax.dot_general(a, b, (((ca,), (cb,)), ((), ())), preferred_element_type=F32)


def iota(shape, dim):
    return lax.broadcasted_iota(jnp.int32, shape, dim)


def column(row):
    return jnp.transpose(jnp.broadcast_to(row, (E, E)))


def columns(at):
    core = lax.rem(lax.axis_index("seqout"), 2)
    return pl.ds(pl.multiple_of(lax.rem(4 * core + at, 8) * E, E), E)


def wide(at):
    return pl.ds(pl.multiple_of(lax.rem(at, 4) * 2 * E, 2 * E), 2 * E)


def each(count, body):
    def step(j, carry):
        body(j)
        return carry

    lax.fori_loop(0, count, step, 0)


def block_sums(fk, v):
    kv = dot(fk, v, 0, 0)
    z = jnp.sum(fk.astype(F32), axis=0, keepdims=True)
    return jnp.concatenate([kv, jnp.broadcast_to(z, (8, E))], axis=0)


def sums_kernel(
    keys_ref, values_ref, queries_ref, cotangent_ref, q_ref, k_ref, v_ref, ct_ref, nd_ref, g_ref, first_ref, last_ref, mask_ref, sems
):
    copies = []
    for i, (src, dst) in enumerate(((keys_ref, k_ref), (values_ref, v_ref), (queries_ref, q_ref), (cotangent_ref, ct_ref))):
        for b in range(2):
            rows = pl.ds(b * BLOCK, BLOCK)
            copies.append(pltpu.make_async_copy(src.at[rows, :], dst.at[rows, :], sems.at[2 * i + b]))
    for i in (0, 2, 1, 3, 4, 5, 6, 7):
        copies[i].start()
    write_masks(mask_ref)
    for b in range(2):
        rows = pl.ds(b * BLOCK, BLOCK)
        copies[b].wait()
        copies[2 + b].wait()

        def one(j):
            cols = columns(j)
            part = block_sums(phi(k_ref[rows, cols]), v_ref[rows, cols])
            if b == 0:
                first_ref[j] = part
            else:
                last_ref[j] = part

        each(8, one)
    for i in (4, 5, 6, 7):
        copies[i].wait()


def intra_kernel(start, count, sent_ref, q_ref, k_ref, v_ref, ct_ref, nd_ref, g_ref, token_ref):
    token_ref[...] = jnp.zeros_like(token_ref)
    tri = iota((HALF, HALF), 0) >= iota((HALF, HALF), 1)
    ones = jnp.ones((BLOCK, E), BF16)

    def one(j):
        cols = columns(start + j)
        for b in range(2):
            rows = pl.ds(b * BLOCK, BLOCK)
            fq, fk = phi(q_ref[rows, cols]), phi(k_ref[rows, cols])
            va = jnp.concatenate([v_ref[rows, cols], ones], axis=1)
            w00 = jnp.where(tri, dot(fq[:HALF], fk[:HALF], 1, 1), 0.0).astype(BF16)
            w10 = dot(fq[HALF:], fk[:HALF], 1, 1).astype(BF16)
            w11 = jnp.where(tri, dot(fq[HALF:], fk[HALF:], 1, 1), 0.0).astype(BF16)
            nd_ref[start + j, pl.ds(b * BLOCK, HALF), :] = dot(w00, va[:HALF])
            nd_ref[start + j, pl.ds(b * BLOCK + HALF, HALF), :] = dot(jnp.concatenate([w10, w11], axis=1), va)

    each(count, one)


def attn_kernel(start, count, gain_ref, st_ref, first_ref, q_ref, k_ref, v_ref, ct_ref, nd_ref, g_ref, sums_ref, sq_acc, pr_acc):
    sq_acc[...] = jnp.zeros_like(sq_acc)
    pr_acc[...] = jnp.zeros_like(pr_acc)

    def one(j):
        cols = columns(start + j)
        for b in range(2):
            rows = pl.ds(b * BLOCK, BLOCK)
            aug = st_ref[j] + first_ref[start + j] if b else st_ref[j]
            s_hi, s_lo = split(aug[:E])
            n_hi, n_lo = split(column(aug[E : E + 1]))
            rhs = jnp.concatenate([jnp.concatenate([s_hi, n_hi], axis=1), jnp.concatenate([s_lo, n_lo], axis=1)], axis=0)
            fq = phi(q_ref[rows, cols])
            nd = nd_ref[start + j, rows, :] + dot(jnp.concatenate([fq, fq], axis=1), rhs)
            inv = 1.0 / nd[:, E:]
            attn = nd[:, :E] * inv
            nd_ref[start + j, rows, :] = jnp.concatenate([attn, inv], axis=1)
            sq_acc[rows, :] += attn * attn
            pr_acc[rows, :] += ct_ref[rows, cols].astype(F32) * gain_ref[:, cols] * attn

    each(count, one)
    for i in range(8):
        rows = pl.ds(i * E, E)
        sums_ref[pl.ds(i, 1), :] = jnp.sum(jnp.transpose(sq_acc[rows, :]), axis=0, keepdims=True)
        sums_ref[pl.ds(8 + i, 1), :] = jnp.sum(jnp.transpose(pr_acc[rows, :]), axis=0, keepdims=True)


def spread(sc_ref, scale_ref, coef_ref):
    for i in range(8):
        rows = pl.ds(i * E, E)
        scale_ref[rows, :] = column(sc_ref[pl.ds(i, 1), :])
        if coef_ref is not None:
            coef_ref[rows, :] = column(sc_ref[pl.ds(8 + i, 1), :])


def grad_kernel(start, count, gain_ref, sc_ref, q_ref, k_ref, v_ref, ct_ref, nd_ref, g_ref, first_ref, last_ref, scale_ref, coef_ref):
    spread(sc_ref, scale_ref, coef_ref)
    lane = iota((BLOCK, E), 1)
    ones = jnp.ones((2 * E, E), BF16)

    def one(j):
        cols = columns(start + j)
        for b in range(2):
            rows = pl.ds(b * BLOCK, BLOCK)
            attn, inv = nd_ref[start + j, rows, :E], nd_ref[start + j, rows, E:]
            weighted = ct_ref[rows, cols].astype(F32) * gain_ref[:, cols]
            d_attn = scale_ref[rows, :] * weighted - attn * coef_ref[rows, :]
            g = (d_attn * inv).astype(BF16)
            p_hi, p_lo = split(d_attn * attn)
            gd = -dot(jnp.concatenate([p_hi, p_lo], axis=1), ones) * inv
            gd_hi, gd_lo = split(gd)
            aug = jnp.where((lane == 0) | (lane == 2), gd_hi, jnp.where(lane == 1, gd_lo, jnp.zeros_like(gd_lo)))
            g_ref.at[lax.div(start + j, 4)][rows, wide(start + j)] = jnp.concatenate([g, aug], axis=1)
            fq = phi(q_ref[rows, cols])
            rev = dot(fq, g, 0, 0)
            rden = jnp.sum(gd * fq.astype(F32), axis=0, keepdims=True)
            part = jnp.concatenate([rev, jnp.broadcast_to(rden, (8, E))], axis=0)
            if b == 0:
                first_ref[j] = part
            else:
                last_ref[j] = part

    each(count, one)


def back_kernel(
    start, count, gain_ref, sc_ref, st_ref, first_ref, sent_ref, q_ref, k_ref, v_ref, ct_ref, nd_ref, g_ref,
    dq_ref, mixed_ref, token_ref, scale_ref, dq_buf, mixed_buf, sems,
):
    token_ref[...] = jnp.zeros_like(token_ref)
    spread(sc_ref, scale_ref, None)
    low = iota((HALF, HALF), 0) >= iota((HALF, HALF), 1)
    up = iota((HALF, HALF), 0) <= iota((HALF, HALF), 1)
    flag = jnp.where(iota((BLOCK, E), 1) < 2, 1.0, 0.0).astype(BF16)
    lane = iota((E, E), 1)

    def copies(j):
        cols = columns(start + j)
        return [
            pltpu.make_async_copy(dq_buf.at[j], dq_ref.at[:, cols], sems.at[0, j]),
            pltpu.make_async_copy(mixed_buf.at[j], mixed_ref.at[:, cols], sems.at[1, j]),
        ]

    def one(j):
        cols = columns(start + j)
        for b in range(2):
            rows = pl.ds(b * BLOCK, BLOCK)
            q, v = q_ref[rows, cols], v_ref[rows, cols]
            fq, fk = phi(q), phi(k_ref[rows, cols])
            ga = g_ref.at[lax.div(start + j, 4)][rows, wide(start + j)]
            g = ga[:, :E]
            va = jnp.concatenate([v, flag], axis=1)
            m00 = jnp.where(low, dot(ga[:HALF], va[:HALF], 1, 1), 0.0).astype(BF16)
            m10 = dot(ga[HALF:], va[:HALF], 1, 1).astype(BF16)
            m11 = jnp.where(low, dot(ga[HALF:], va[HALF:], 1, 1), 0.0).astype(BF16)
            w00 = jnp.where(up, dot(fk[:HALF], fq[:HALF], 1, 1), 0.0).astype(BF16)
            w10 = dot(fk[:HALF], fq[HALF:], 1, 1).astype(BF16)
            w11 = jnp.where(up, dot(fk[HALF:], fq[HALF:], 1, 1), 0.0).astype(BF16)
            at = start % 4 + j
            aug = st_ref[at] + first_ref[start + j] if b else st_ref[at]
            s_hi, s_lo = split(aug[:E])
            n_hi, n_lo = split(column(aug[E : E + 1]))
            naug = jnp.where(lane < 2, n_hi, jnp.where(lane == 2, n_lo, jnp.zeros_like(n_lo)))
            rhs = jnp.concatenate([s_hi, s_lo, naug], axis=1)
            dfq = dot(jnp.concatenate([g, ga], axis=1), rhs, 1, 1)
            dfq = dfq + jnp.concatenate([dot(m00, fk[:HALF]), dot(jnp.concatenate([m10, m11], axis=1), fk)], axis=0)
            dq_buf[j, rows, :] = (dfq * slope(q)).astype(BF16)
            mixed_buf[j, rows, :] = (nd_ref[start + j, rows, :E] * scale_ref[rows, :] * gain_ref[:, cols]).astype(BF16)
            nd_ref[start + j, pl.ds(b * BLOCK, HALF), :E] = dot(jnp.concatenate([m00, m10], axis=0), fq, 0, 0)
            nd_ref[start + j, pl.ds(b * BLOCK + HALF, HALF), :E] = dot(m11, fq[HALF:], 0, 0)
            nd_ref[start + j, pl.ds(b * BLOCK, HALF), E:] = dot(jnp.concatenate([w00, w10], axis=1), g)
            nd_ref[start + j, pl.ds(b * BLOCK + HALF, HALF), E:] = dot(w11, g[HALF:])
        for copy in copies(j):
            copy.start()

    each(count, one)
    for j in range(count):
        for copy in copies(j):
            copy.wait()


def last_kernel(start, count, lt_ref, last_ref, q_ref, k_ref, v_ref, ct_ref, nd_ref, g_ref, gk_ref, gv_ref, gk_buf, gv_buf, sems):

    def copies(j):
        cols = columns(start + j)
        return [
            pltpu.make_async_copy(gk_buf.at[j], gk_ref.at[:, cols], sems.at[0, j]),
            pltpu.make_async_copy(gv_buf.at[j], gv_ref.at[:, cols], sems.at[1, j]),
        ]

    def one(j):
        cols = columns(start + j)
        for b in range(2):
            rows = pl.ds(b * BLOCK, BLOCK)
            k, v = k_ref[rows, cols], v_ref[rows, cols]
            fk = phi(k)
            aug = lt_ref[j] if b else lt_ref[j] + last_ref[start + j]
            l_hi, l_lo = split(aug[:E])
            dfk = dot(jnp.concatenate([v, v], axis=1), jnp.concatenate([l_hi, l_lo], axis=1), 1, 1)
            dfk = dfk + nd_ref[start + j, rows, :E] + aug[E : E + 1]
            dv = dot(jnp.concatenate([fk, fk], axis=1), jnp.concatenate([l_hi, l_lo], axis=0))
            gk_buf[j, rows, :] = (dfk * slope(k)).astype(BF16)
            gv_buf[j, rows, :] = (dv + nd_ref[start + j, rows, E:]).astype(BF16)
        for copy in copies(j):
            copy.start()

    each(count, one)
    for j in range(count):
        for copy in copies(j):
            copy.wait()


def vmem(shape, dtype=F32, into=None):
    return pltpu.VMEM(shape, dtype), into


def hbm(shape, dtype, into=None):
    return pltpu.HBM(shape, dtype), into


def call(kernel, near, far, outs, scratch=(), flops=0):
    arrays = [pltpu.with_memory_space_constraint(a, pltpu.VMEM) for a in near]
    arrays += far
    specs = [pl.BlockSpec(memory_space=pltpu.VMEM)] * len(near) + [pl.BlockSpec(memory_space=pl.ANY)] * len(far)
    first, shapes, out_specs, aliases = len(arrays), [], [], {}
    for i, (shape, into) in enumerate(outs):
        space = pl.ANY if shape.memory_space == pltpu.HBM else pltpu.VMEM
        shapes.append(shape)
        out_specs.append(pl.BlockSpec(memory_space=space))
        if into is not None:
            aliases[len(arrays)] = i
            arrays.append(pltpu.with_memory_space_constraint(into, shape.memory_space))
            specs.append(pl.BlockSpec(memory_space=space))

    def body(*refs):
        bank, nd, *own = refs[len(arrays) :]
        kernel(*refs[:first], *(bank.at[i] for i in range(4)), nd, bank.at[pl.ds(4, 2)], *own)

    return pl.pallas_call(
        body,
        out_shape=shapes,
        in_specs=specs,
        out_specs=out_specs,
        scratch_shapes=list(scratch),
        input_output_aliases=aliases,
        compiler_params=pltpu.CompilerParams(vmem_limit_bytes=VMEM_LIMIT),
        cost_estimate=pl.CostEstimate(flops=flops, bytes_accessed=1 << 20, transcendentals=0),
    )(*arrays)


CORE = [(i, i ^ 1) for i in range(8)]


def swap(x):
    return lax.ppermute(x, "seqout", CORE)


TO, SOURCE, BEFORE, AFTER, LOWER, UPPER, MASKS = 0, 16, 32, 48, 64, 65, 72


def write_masks(mask_ref):
    place = lax.axis_index("seqout")
    x, core = lax.div(place, 2), lax.rem(place, 2)

    def put(at, true):
        mask_ref[pl.ds(at, 1), :] = jnp.full((1, E), jnp.where(true, 1.0, 0.0), F32)

    for k in range(4):
        to = lax.rem(x + k, 4)
        for i in range(4):
            source = lax.rem(x + 4 - i, 4)
            put(TO + 4 * k + i, to == i)
            put(SOURCE + 4 * k + i, lax.rem(x + 4 - k, 4) == i)
            put(BEFORE + 4 * k + i, source < to)
            put(AFTER + 4 * k + i, source > to)
    put(LOWER, core == 0)
    put(UPPER, core == 1)


def keep_where(mask, at, x):
    return jnp.where(mask[at : at + 1] > 0, x, 0.0)


def add(parts):
    return functools.reduce(lambda a, b: a + b, parts)


def scan(sums, mask, reverse, during):
    other = swap(sums[4:])
    total = sums[:4] + other + during[0](sums)
    got = [add([keep_where(mask, TO + 4 * k + h, total[h]) for h in range(4)]) for k in range(4)]
    own = got[0]
    for k in (1, 2, 3):
        got[k] = lax.ppermute(got[k], "seqout", [(i, (i + 2 * k) % 8) for i in range(8)])
    row = got[0] + got[1] + got[2] + got[3] + during[1](own)
    rows = []
    for k in (1, 2, 3):
        pairs = [(i, i - k) if reverse else (i, i + k) for i in range(4)]
        rows.append(lax.ppermute(row, "seqin", [(a, b) for a, b in pairs if 0 <= b < 4]))
    base = rows[0] + rows[1] + rows[2] + during[2](row)
    at = AFTER if reverse else BEFORE
    came = [base + add([keep_where(mask, at + 4 * k + m, got[m]) for m in range(4)]) for k in range(4)]
    for k in (1, 2, 3):
        came[k] = lax.ppermute(came[k], "seqout", [(i, (i + 2 * k) % 8) for i in range(8)])
    zeros = during[3](base)
    out = [add([keep_where(mask, SOURCE + 4 * k + h, came[k]) for k in range(4)]) + zeros for h in range(4)]
    return jnp.stack(out), other


def shards(queries, keys, values, gain, cotangent):
    gain = gain.reshape(1, ROWS)
    shape = (ROWS, ROWS)
    aug = vmem((4, AUG, E))
    token = vmem((8, E))
    acc = pltpu.VMEM((ROWS, E), F32)
    sems = pltpu.SemaphoreType.DMA
    kept = {}
    sizes = {"bank": ((6, ROWS, ROWS), BF16), "nd": ((8, ROWS, 2 * E), F32)}

    def run(kernel, near, far, outs, scratch=(), flops=0):
        held = [vmem(*size, kept.get(name)) for name, size in sizes.items()]
        got = call(kernel, near, [pltpu.with_memory_space_constraint(a, pltpu.HBM) if a.shape == shape else a for a in far], held + outs, scratch, flops)
        kept.update(zip(sizes, got))
        return got[len(sizes) :]

    parts = vmem((8, AUG, E))
    far = [keys, values, queries, cotangent]
    first, last, mask = run(sums_kernel, [], far, [parts, parts, vmem((MASKS, E))], [sems((8,))], 1 << 28)
    sums = first + last

    def intra(start, count):
        def during(sent):
            kernel = functools.partial(intra_kernel, start, count)
            (zeros,) = run(kernel, [], [sent], [token], (), count << 28)
            return zeros[:1]

        return during

    st, other = scan(sums, mask, False, (intra(0, 2), intra(2, 2), intra(4, 2), intra(6, 2)))
    st_keep = st + keep_where(mask, UPPER, other)
    st_send = swap(st + keep_where(mask, LOWER, sums[:4]))

    def attend(start, state):
        kernel = functools.partial(attn_kernel, start, 4)
        near = [gain, state, first]
        return run(kernel, near, [], [vmem((16, E))], (acc, acc), 1 << 28)[0]

    local = attend(0, st_keep)
    local = local + attend(4, st_send)
    far = [lax.ppermute(local, "head", [(i, (i + k) % 4) for i in range(4)]) for k in (1, 2, 3)]
    whole = local + far[0] + far[1] + far[2]
    scale = lax.rsqrt(whole[:8] / D + 1e-06)
    sc = jnp.concatenate([scale, scale**3 * whole[8:] / D], axis=0)

    kernel = functools.partial(grad_kernel, 0, 8)
    back_first, back_last = run(kernel, [gain, sc], [], [parts, parts], (acc, acc), 1 << 29)
    back_sums = back_first + back_last
    dq = mixed = None

    def back(start, count):
        def during(sent):
            nonlocal dq, mixed
            state = st_send if start >= 4 else st_keep
            out = pltpu.VMEM((count, ROWS, E), BF16)
            dq, mixed, zeros = run(
                functools.partial(back_kernel, start, count),
                [gain, sc, state, first], [sent], [hbm(shape, BF16, dq), hbm(shape, BF16, mixed), token],
                (acc, out, out, sems((2, count))), count << 29,
            )
            return zeros[:1]

        return during

    lt, other = scan(back_sums, mask, True, (back(0, 2), back(2, 2), back(4, 2), back(6, 2)))
    lt_keep = lt + keep_where(mask, LOWER, other)
    lt_send = swap(lt + keep_where(mask, UPPER, back_sums[:4]))
    gk = gv = None
    for start, later in ((0, lt_keep), (4, lt_send)):
        out = pltpu.VMEM((4, ROWS, E), BF16)
        gk, gv = run(
            functools.partial(last_kernel, start, 4), [later, back_last], [],
            [hbm(shape, BF16, gk), hbm(shape, BF16, gv)], (out, out, sems((2, 4))), 1 << 28,
        )
    return mixed, dq, gk, gv


def solution(mesh):
    rows = P(("seqin", "seqout"), "head")
    return jax.shard_map(
        shards,
        mesh=mesh,
        in_specs=(rows, rows, rows, P("head"), rows),
        out_specs=(rows, rows, rows, rows),
        check_vma=False,
    )
```

profile of v0, /device:TPU:1, one launch (start us, length us, event | category | flops | bytes accessed | tf_op | source)
XLA Modules:
  0.0 97.1 jit_solution(17504747915296743397)
XLA Ops:
  0.6 6.0 %shard_map.84 = (bf16[6,1024,1024]{2,1,0:T(8,128)(2,1)S(1)}, f32[8,1024,256]{2,1,0:T(8,128)S(1)}, f32[8,136,128]{2,1,0:T(8,128)S(1)}, f32[8,136,128]{2,1,0:T(8,128)S(1)}, f32[72,128]{1,0:T(8,128)S(1)}) custom-call(bf16[1024,1024]{1,0:T(8,128)(2,1)} %refs_0_.1, bf16[1024,1024]{1,0:T(8,128)(2,1)} %refs_1_.1, bf16[1024,1024]{1,0:T(8,128)(2,1)} %refs_2_.1, ...), custom_call_target="tpu_custom_call" | custom-call | flops 268435456 | bytes 1048576 | tf_op jit(solution)/shard_map/pallas_call | solution.py:298
  6.6 0.1 add.428.refs_0_
  6.7 1.5 %collective-permute-start = (f32[4,136,128]{2,1,0:T(8,128)S(1)}, f32[4,136,128]{2,1,0:T(8,128)S(1)}, u32[]{:S(2)}, u32[]{:S(2)}) collective-permute-start(f32[4,136,128]{2,1,0:T(8,128)S(1)} %slice.413), channel_id=1, source_target_pairs={{0,4},{4,0},{8,12},{12,8},{16,20},{20,16},{24,28},{28,24},{1,5},{5... | collective-permute-start | bytes 835592 | tf_op jit(solution)/shard_map/ppermute | solution.py:314
  8.3 1.4 %shard_map.85 = (bf16[6,1024,1024]{2,1,0:T(8,128)(2,1)S(1)}, f32[8,1024,256]{2,1,0:T(8,128)S(1)}, f32[8,128]{1,0:T(8,128)S(1)}) custom-call(f32[8,136,128]{2,1,0:T(8,128)S(1)} %add.428.refs_0_, bf16[6,1024,1024]{2,1,0:T(8,128)(2,1)S(1)} %get-tuple-element.60.refs_1_, ...), custom_call_target="tpu_custom_call", output_to_operand_aliasing={{0}: (1, {}), {1}: (2, {})} | custom-call | flops 536870912 | bytes 1048576 | tf_op jit(solution)/shard_map/pallas_call | solution.py:298
  9.9 1.4 %collective-permute-start.1 = (f32[136,128]{1,0:T(8,128)S(1)}, f32[136,128]{1,0:T(8,128)S(1)}, u32[]{:S(2)}, u32[]{:S(2)}) collective-permute-start(f32[136,128]{1,0:T(8,128)S(1)} %get-tuple-element.138), channel_id=1, source_target_pairs={{0,8},{4,12},{8,16},{12,20},{16,24},{20,28},{24,0},{28,4},{1,9},{5... | collective-permute-start | bytes 208904 | tf_op jit(solution)/shard_map/ppermute | solution.py:353
  11.2 2.5 %collective-permute-start.2 = (f32[136,128]{1,0:T(8,128)S(1)}, f32[136,128]{1,0:T(8,128)S(1)}, u32[]{:S(2)}, u32[]{:S(2)}) collective-permute-start(f32[136,128]{1,0:T(8,128)S(1)} %get-tuple-element.139), channel_id=1, source_target_pairs={{0,16},{4,20},{8,24},{12,28},{16,0},{20,4},{24,8},{28,12},{1,17},{... | collective-permute-start | bytes 208904 | tf_op jit(solution)/shard_map/ppermute | solution.py:353
  13.7 1.2 %collective-permute-start.3 = (f32[136,128]{1,0:T(8,128)S(1)}, f32[136,128]{1,0:T(8,128)S(1)}, u32[]{:S(2)}, u32[]{:S(2)}) collective-permute-start(f32[136,128]{1,0:T(8,128)S(1)} %get-tuple-element.137), channel_id=1, source_target_pairs={{0,24},{4,28},{8,0},{12,4},{16,8},{20,12},{24,16},{28,20},{1,25},{... | collective-permute-start | bytes 208904 | tf_op jit(solution)/shard_map/ppermute | solution.py:353
  14.9 1.4 %shard_map.86 = (bf16[6,1024,1024]{2,1,0:T(8,128)(2,1)S(1)}, f32[8,1024,256]{2,1,0:T(8,128)S(1)}, f32[8,128]{1,0:T(8,128)S(1)}) custom-call(f32[136,128]{1,0:T(8,128)S(1)} %get-tuple-element.136.refs_0_, bf16[6,1024,1024]{2,1,0:T(8,128)(2,1)S(1)} %get-tuple-element.63.refs_1_, ...), custom_call_target="tpu_custom_call", output_to_operand_aliasing={{0}: (1, {}), {1}: (2, {})} | custom-call | flops 536870912 | bytes 1048576 | tf_op jit(solution)/shard_map/pallas_call | solution.py:298
  16.4 1.1 %collective-permute-done.2 = f32[136,128]{1,0:T(8,128)S(1)} collective-permute-done((f32[136,128]{1,0:T(8,128)S(1)}, f32[136,128]{1,0:T(8,128)S(1)}, u32[]{:S(2)}, u32[]{:S(2)}) %collective-permute-start.2) | collective-permute-done | bytes 69664 | tf_op jit(solution)/shard_map/ppermute | solution.py:353
  17.5 4.6 %collective-permute-start.6 = (f32[136,128]{1,0:T(8,128)S(1)}, f32[136,128]{1,0:T(8,128)S(1)}, u32[]{:S(2)}, u32[]{:S(2)}) collective-permute-start(f32[136,128]{1,0:T(8,128)S(1)} %add_add_fusion.13.refs_0_), channel_id=1, source_target_pairs={{0,96},{1,97},{2,98},{3,99},{4,100},{5,101},{6,102},{7,103},{8,104... | collective-permute-start | bytes 208904 | tf_op jit(solution)/shard_map/ppermute | solution.py:358
  22.2 1.3 %collective-permute-start.5 = (f32[136,128]{1,0:T(8,128)S(1)}, f32[136,128]{1,0:T(8,128)S(1)}, u32[]{:S(2)}, u32[]{:S(2)}) collective-permute-start(f32[136,128]{1,0:T(8,128)S(1)} %add_add_fusion.13.refs_0_), channel_id=1, source_target_pairs={{0,64},{32,96},{1,65},{33,97},{2,66},{34,98},{3,67},{35,99},{4,68}... | collective-permute-start | bytes 208904 | tf_op jit(solution)/shard_map/ppermute | solution.py:358
  23.5 2.5 %collective-permute-start.4 = (f32[136,128]{1,0:T(8,128)S(1)}, f32[136,128]{1,0:T(8,128)S(1)}, u32[]{:S(2)}, u32[]{:S(2)}) collective-permute-start(f32[136,128]{1,0:T(8,128)S(1)} %add_add_fusion.13.refs_0_), channel_id=1, source_target_pairs={{0,32},{32,64},{64,96},{1,33},{33,65},{65,97},{2,34},{34,66},{66,9... | collective-permute-start | bytes 208904 | tf_op jit(solution)/shard_map/ppermute | solution.py:358
  26.0 1.4 %shard_map.87 = (bf16[6,1024,1024]{2,1,0:T(8,128)(2,1)S(1)}, f32[8,1024,256]{2,1,0:T(8,128)S(1)}, f32[8,128]{1,0:T(8,128)S(1)}) custom-call(f32[136,128]{1,0:T(8,128)S(1)} %add_add_fusion.13.refs_0_, bf16[6,1024,1024]{2,1,0:T(8,128)(2,1)S(1)} %get-tuple-element.66.refs_1_, ...), custom_call_target="tpu_custom_call", output_to_operand_aliasing={{0}: (1, {}), {1}: (2, {})} | custom-call | flops 536870912 | bytes 1048576 | tf_op jit(solution)/shard_map/pallas_call | solution.py:298
  27.5 0.5 collective-permute-start.7
  28.1 2.8 %collective-permute-start.8 = (f32[136,128]{1,0:T(8,128)S(1)}, f32[136,128]{1,0:T(8,128)S(1)}, u32[]{:S(2)}, u32[]{:S(2)}) collective-permute-start(f32[136,128]{1,0:T(8,128)S(1)} %get-tuple-element.120), channel_id=1, source_target_pairs={{0,16},{4,20},{8,24},{12,28},{16,0},{20,4},{24,8},{28,12},{1,17},{... | collective-permute-start | bytes 208904 | tf_op jit(solution)/shard_map/ppermute | solution.py:363
  30.9 0.9 collective-permute-start.9
  31.8 1.4 %shard_map.88 = (bf16[6,1024,1024]{2,1,0:T(8,128)(2,1)S(1)}, f32[8,1024,256]{2,1,0:T(8,128)S(1)}, f32[8,128]{1,0:T(8,128)S(1)}) custom-call(f32[136,128]{1,0:T(8,128)S(1)} %get-tuple-element.117.refs_0_, bf16[6,1024,1024]{2,1,0:T(8,128)(2,1)S(1)} %get-tuple-element.69.refs_1_, ...), custom_call_target="tpu_custom_call", output_to_operand_aliasing={{0}: (1, {}), {1}: (2, {})} | custom-call | flops 536870912 | bytes 1048576 | tf_op jit(solution)/shard_map/pallas_call | solution.py:298
  33.2 1.1 %collective-permute-done.9 = f32[136,128]{1,0:T(8,128)S(1)} collective-permute-done((f32[136,128]{1,0:T(8,128)S(1)}, f32[136,128]{1,0:T(8,128)S(1)}, u32[]{:S(2)}, u32[]{:S(2)}) %collective-permute-start.9) | collective-permute-done | bytes 69664 | tf_op jit(solution)/shard_map/ppermute | solution.py:363
  34.4 0.1 add_bitcast_fusion.6
  34.5 4.0 %collective-permute-start.10 = (f32[4,136,128]{2,1,0:T(8,128)S(1)}, f32[4,136,128]{2,1,0:T(8,128)S(1)}, u32[]{:S(2)}, u32[]{:S(2)}) collective-permute-start(f32[4,136,128]{2,1,0:T(8,128)S(1)} %get-tuple-element.134), channel_id=1, source_target_pairs={{0,4},{4,0},{8,12},{12,8},{16,20},{20,16},{24,28},{28,24},{1,5},{5... | collective-permute-start | bytes 835592 | tf_op jit(solution)/shard_map/ppermute | solution.py:314
  38.6 2.3 %shard_map.89 = (bf16[6,1024,1024]{2,1,0:T(8,128)(2,1)S(1)}, f32[8,1024,256]{2,1,0:T(8,128)S(1)}, f32[16,128]{1,0:T(8,128)S(1)}) custom-call(f32[1,1024]{1,0:T(1,128)S(1)} %bitcast.245, f32[4,136,128]{2,1,0:T(8,128)S(1)} %get-tuple-element.135.refs_1_.refs_2_, ...), custom_call_target="tpu_custom_call", output_to_operand_aliasing={{0}: (3, {}), {1}: (4, {})} | custom-call | flops 268435456 | bytes 1048576 | tf_op jit(solution)/shard_map/pallas_call | solution.py:298
  40.9 2.2 %shard_map.90 = (bf16[6,1024,1024]{2,1,0:T(8,128)(2,1)S(1)}, f32[8,1024,256]{2,1,0:T(8,128)S(1)}, f32[16,128]{1,0:T(8,128)S(1)}) custom-call(f32[1,1024]{1,0:T(1,128)S(1)} %bitcast.246, f32[4,136,128]{2,1,0:T(8,128)S(1)} %collective-permute-done.10.refs_1_.refs_2_, ...), custom_call_target="tpu_custom_call", output_to_operand_aliasing={{0}: (3, {}), {1}: (4, {})} | custom-call | flops 268435456 | bytes 1048576 | tf_op jit(solution)/shard_map/pallas_call | solution.py:298
  43.1 3.8 %collective-permute-start.13 = (f32[16,128]{1,0:T(8,128)S(1)}, f32[16,128]{1,0:T(8,128)S(1)}, u32[]{:S(2)}, u32[]{:S(2)}) collective-permute-start(f32[16,128]{1,0:T(8,128)S(1)} %add.492), channel_id=1, source_target_pairs={{0,3},{1,0},{2,1},{3,2},{4,7},{5,4},{6,5},{7,6},{8,11},{9,8},{10,9... | collective-permute-start | bytes 24584 | tf_op jit(solution)/shard_map/ppermute | solution.py:409
  47.0 0.7 collective-permute-start.11
  47.7 0.1 collective-permute-done.13
  47.7 3.2 %collective-permute-done.12 = f32[16,128]{1,0:T(8,128)S(1)} collective-permute-done((f32[16,128]{1,0:T(8,128)S(1)}, f32[16,128]{1,0:T(8,128)S(1)}, u32[]{:S(2)}, u32[]{:S(2)}) %collective-permute-start.12) | collective-permute-done | bytes 8224 | tf_op jit(solution)/shard_map/ppermute | solution.py:409
  51.0 8.5 %shard_map.91 = (bf16[6,1024,1024]{2,1,0:T(8,128)(2,1)S(1)}, f32[8,1024,256]{2,1,0:T(8,128)S(1)}, f32[8,136,128]{2,1,0:T(8,128)S(1)}, f32[8,136,128]{2,1,0:T(8,128)S(1)}) custom-call(f32[1,1024]{1,0:T(1,128)S(1)} %bitcast.247, f32[16,128]{1,0:T(8,128)S(1)} %pad_maximum_fusion.2.refs_1_, ...), custom_call_target="tpu_custom_call", output_to_operand_aliasing={{0}: (2, {}), {1}: (3, {})} | custom-call | flops 536870912 | bytes 1048576 | tf_op jit(solution)/shard_map/pallas_call | solution.py:298
  59.5 0.1 add.498.refs_4_
  59.6 1.7 %collective-permute-start.14 = (f32[4,136,128]{2,1,0:T(8,128)S(1)}, f32[4,136,128]{2,1,0:T(8,128)S(1)}, u32[]{:S(2)}, u32[]{:S(2)}) collective-permute-start(f32[4,136,128]{2,1,0:T(8,128)S(1)} %slice.421), channel_id=1, source_target_pairs={{0,4},{4,0},{8,12},{12,8},{16,20},{20,16},{24,28},{28,24},{1,5},{5... | collective-permute-start | bytes 835592 | tf_op jit(solution)/shard_map/ppermute | solution.py:314
  61.4 3.8 %shard_map.92 = (bf16[6,1024,1024]{2,1,0:T(8,128)(2,1)S(1)}, f32[8,1024,256]{2,1,0:T(8,128)S(1)}, bf16[1024,1024]{1,0:T(8,128)(2,1)}, bf16[1024,1024]{1,0:T(8,128)(2,1)}, f32[8,128]{1,0:T(8,128)S(1)}) custom-call(f32[1,1024]{1,0:T(1,128)S(1)} %bitcast.248, f32[16,128]{1,0:T(8,128)S(1)} %pad_maximum_fusion.2.refs_1_, ...), custom_call_target="tpu_custom_call", output_to_operand_aliasing={{0}: (5, {}), {1}: (6, {})} | custom-call | flops 1073741824 | bytes 1048576 | tf_op jit(solution)/shard_map/pallas_call | solution.py:298
  65.4 0.1 collective-permute-start.15
  65.5 2.8 %collective-permute-start.16 = (f32[136,128]{1,0:T(8,128)S(1)}, f32[136,128]{1,0:T(8,128)S(1)}, u32[]{:S(2)}, u32[]{:S(2)}) collective-permute-start(f32[136,128]{1,0:T(8,128)S(1)} %get-tuple-element.133), channel_id=1, source_target_pairs={{0,16},{4,20},{8,24},{12,28},{16,0},{20,4},{24,8},{28,12},{1,17},{... | collective-permute-start | bytes 208904 | tf_op jit(solution)/shard_map/ppermute | solution.py:353
  68.3 0.4 collective-permute-start.17
  68.7 3.8 %shard_map.93 = (bf16[6,1024,1024]{2,1,0:T(8,128)(2,1)S(1)}, f32[8,1024,256]{2,1,0:T(8,128)S(1)}, bf16[1024,1024]{1,0:T(8,128)(2,1)}, bf16[1024,1024]{1,0:T(8,128)(2,1)}, f32[8,128]{1,0:T(8,128)S(1)}) custom-call(f32[1,1024]{1,0:T(1,128)S(1)} %bitcast.249, ...), custom_call_target="tpu_custom_call", output_to_operand_aliasing={{0}: (5, {}), {1}: (6, {}), {2}: (7, {}), {3}: (8, {})} | custom-call | flops 1073741824 | bytes 1048576 | tf_op jit(solution)/shard_map/pallas_call | solution.py:298
  72.7 1.3 %collective-permute-start.20 = (f32[136,128]{1,0:T(8,128)S(1)}, f32[136,128]{1,0:T(8,128)S(1)}, u32[]{:S(2)}, u32[]{:S(2)}) collective-permute-start(f32[136,128]{1,0:T(8,128)S(1)} %add_add_fusion.7.refs_4_), channel_id=1, source_target_pairs={{96,0},{97,1},{98,2},{99,3},{100,4},{101,5},{102,6},{103,7},{104,8... | collective-permute-start | bytes 208904 | tf_op jit(solution)/shard_map/ppermute | solution.py:358
  74.0 1.3 %collective-permute-start.19 = (f32[136,128]{1,0:T(8,128)S(1)}, f32[136,128]{1,0:T(8,128)S(1)}, u32[]{:S(2)}, u32[]{:S(2)}) collective-permute-start(f32[136,128]{1,0:T(8,128)S(1)} %add_add_fusion.7.refs_4_), channel_id=1, source_target_pairs={{64,0},{96,32},{65,1},{97,33},{66,2},{98,34},{67,3},{99,35},{68,4}... | collective-permute-start | bytes 208904 | tf_op jit(solution)/shard_map/ppermute | solution.py:358
  75.3 1.3 %collective-permute-start.18 = (f32[136,128]{1,0:T(8,128)S(1)}, f32[136,128]{1,0:T(8,128)S(1)}, u32[]{:S(2)}, u32[]{:S(2)}) collective-permute-start(f32[136,128]{1,0:T(8,128)S(1)} %add_add_fusion.7.refs_4_), channel_id=1, source_target_pairs={{32,0},{64,32},{96,64},{33,1},{65,33},{97,65},{34,2},{66,34},{98,6... | collective-permute-start | bytes 208904 | tf_op jit(solution)/shard_map/ppermute | solution.py:358
  76.6 3.8 %shard_map.94 = (bf16[6,1024,1024]{2,1,0:T(8,128)(2,1)S(1)}, f32[8,1024,256]{2,1,0:T(8,128)S(1)}, bf16[1024,1024]{1,0:T(8,128)(2,1)}, bf16[1024,1024]{1,0:T(8,128)(2,1)}, f32[8,128]{1,0:T(8,128)S(1)}) custom-call(f32[1,1024]{1,0:T(1,128)S(1)} %bitcast.250, ...), custom_call_target="tpu_custom_call", output_to_operand_aliasing={{0}: (5, {}), {1}: (6, {}), {2}: (7, {}), {3}: (8, {})} | custom-call | flops 1073741824 | bytes 1048576 | tf_op jit(solution)/shard_map/pallas_call | solution.py:298
  80.4 0.2 collective-permute-done.19
  80.7 1.1 %collective-permute-start.21 = (f32[136,128]{1,0:T(8,128)S(1)}, f32[136,128]{1,0:T(8,128)S(1)}, u32[]{:S(2)}, u32[]{:S(2)}) collective-permute-start(f32[136,128]{1,0:T(8,128)S(1)} %get-tuple-element.112), channel_id=1, source_target_pairs={{0,8},{4,12},{8,16},{12,20},{16,24},{20,28},{24,0},{28,4},{1,9},{5... | collective-permute-start | bytes 208904 | tf_op jit(solution)/shard_map/ppermute | solution.py:363
  81.8 2.8 %collective-permute-start.22 = (f32[136,128]{1,0:T(8,128)S(1)}, f32[136,128]{1,0:T(8,128)S(1)}, u32[]{:S(2)}, u32[]{:S(2)}) collective-permute-start(f32[136,128]{1,0:T(8,128)S(1)} %get-tuple-element.118), channel_id=1, source_target_pairs={{0,16},{4,20},{8,24},{12,28},{16,0},{20,4},{24,8},{28,12},{1,17},{... | collective-permute-start | bytes 208904 | tf_op jit(solution)/shard_map/ppermute | solution.py:363
  84.6 0.1 collective-permute-start.23
  84.7 3.8 %shard_map.95 = (bf16[6,1024,1024]{2,1,0:T(8,128)(2,1)S(1)}, f32[8,1024,256]{2,1,0:T(8,128)S(1)}, bf16[1024,1024]{1,0:T(8,128)(2,1)}, bf16[1024,1024]{1,0:T(8,128)(2,1)}, f32[8,128]{1,0:T(8,128)S(1)}) custom-call(f32[1,1024]{1,0:T(1,128)S(1)} %bitcast.251, ...), custom_call_target="tpu_custom_call", output_to_operand_aliasing={{0}: (5, {}), {1}: (6, {}), {2}: (7, {}), {3}: (8, {})} | custom-call | flops 1073741824 | bytes 1048576 | tf_op jit(solution)/shard_map/pallas_call | solution.py:298
  88.6 0.1 add_bitcast_fusion.3
  88.6 0.1 add_bitcast_fusion.2
  88.8 2.8 %collective-permute-start.24 = (f32[4,136,128]{2,1,0:T(8,128)S(1)}, f32[4,136,128]{2,1,0:T(8,128)S(1)}, u32[]{:S(2)}, u32[]{:S(2)}) collective-permute-start(f32[4,136,128]{2,1,0:T(8,128)S(1)} %get-tuple-element.129), channel_id=1, source_target_pairs={{0,4},{4,0},{8,12},{12,8},{16,20},{20,16},{24,28},{28,24},{1,5},{5... | collective-permute-start | bytes 835592 | tf_op jit(solution)/shard_map/ppermute | solution.py:314
  91.6 2.7 %shard_map.96 = (bf16[6,1024,1024]{2,1,0:T(8,128)(2,1)S(1)}, f32[8,1024,256]{2,1,0:T(8,128)S(1)}, bf16[1024,1024]{1,0:T(8,128)(2,1)}, bf16[1024,1024]{1,0:T(8,128)(2,1)}) custom-call(f32[4,136,128]{2,1,0:T(8,128)S(1)} %get-tuple-element.128.refs_0_, f32[8,136,128]{2,1,0:T(8,128)S(1)} %get-tuple-element.81.refs_1_, ...), custom_call_target="tpu_custom_call", output_to_operand_aliasing={{0}: (2, {}), {1}: (3, {})} | custom-call | flops 268435456 | bytes 1048576 | tf_op jit(solution)/shard_map/pallas_call | solution.py:298
  94.3 2.7 %shard_map.97 = (bf16[6,1024,1024]{2,1,0:T(8,128)(2,1)S(1)}, f32[8,1024,256]{2,1,0:T(8,128)S(1)}, bf16[1024,1024]{1,0:T(8,128)(2,1)}, bf16[1024,1024]{1,0:T(8,128)(2,1)}) custom-call(f32[4,136,128]{2,1,0:T(8,128)S(1)} %collective-permute-done.24.refs_0_, ...), custom_call_target="tpu_custom_call", output_to_operand_aliasing={{0}: (2, {}), {1}: (3, {}), {2}: (4, {}), {3}: (5, {})} | custom-call | flops 268435456 | bytes 1048576 | tf_op jit(solution)/shard_map/pallas_call | solution.py:298
  (56 shorter events, 0.9 us)
Async XLA Ops:
  6.7 3.1 %collective-permute-start = (f32[4,136,128]{2,1,0:T(8,128)S(1)}, f32[4,136,128]{2,1,0:T(8,128)S(1)}, u32[]{:S(2)}, u32[]{:S(2)}) collective-permute-start(f32[4,136,128]{2,1,0:T(8,128)S(1)} %slice.413), channel_id=1, source_target_pairs={{0,4},{4,0},{8,12},{12,8},{16,20},{20,16},{24,28},{28,24},{1,5},{5... | collective-permute-start | bytes 835592 | tf_op jit(solution)/shard_map/ppermute | solution.py:314
  9.9 6.5 %collective-permute-start.1 = (f32[136,128]{1,0:T(8,128)S(1)}, f32[136,128]{1,0:T(8,128)S(1)}, u32[]{:S(2)}, u32[]{:S(2)}) collective-permute-start(f32[136,128]{1,0:T(8,128)S(1)} %get-tuple-element.138), channel_id=1, source_target_pairs={{0,8},{4,12},{8,16},{12,20},{16,24},{20,28},{24,0},{28,4},{1,9},{5... | collective-permute-start | bytes 208904 | tf_op jit(solution)/shard_map/ppermute | solution.py:353
  11.2 6.3 %collective-permute-start.2 = (f32[136,128]{1,0:T(8,128)S(1)}, f32[136,128]{1,0:T(8,128)S(1)}, u32[]{:S(2)}, u32[]{:S(2)}) collective-permute-start(f32[136,128]{1,0:T(8,128)S(1)} %get-tuple-element.139), channel_id=1, source_target_pairs={{0,16},{4,20},{8,24},{12,28},{16,0},{20,4},{24,8},{28,12},{1,17},{... | collective-permute-start | bytes 208904 | tf_op jit(solution)/shard_map/ppermute | solution.py:353
  13.7 3.8 %collective-permute-start.3 = (f32[136,128]{1,0:T(8,128)S(1)}, f32[136,128]{1,0:T(8,128)S(1)}, u32[]{:S(2)}, u32[]{:S(2)}) collective-permute-start(f32[136,128]{1,0:T(8,128)S(1)} %get-tuple-element.137), channel_id=1, source_target_pairs={{0,24},{4,28},{8,0},{12,4},{16,8},{20,12},{24,16},{28,20},{1,25},{... | collective-permute-start | bytes 208904 | tf_op jit(solution)/shard_map/ppermute | solution.py:353
  17.5 9.9 %collective-permute-start.6 = (f32[136,128]{1,0:T(8,128)S(1)}, f32[136,128]{1,0:T(8,128)S(1)}, u32[]{:S(2)}, u32[]{:S(2)}) collective-permute-start(f32[136,128]{1,0:T(8,128)S(1)} %add_add_fusion.13.refs_0_), channel_id=1, source_target_pairs={{0,96},{1,97},{2,98},{3,99},{4,100},{5,101},{6,102},{7,103},{8,104... | collective-permute-start | bytes 208904 | tf_op jit(solution)/shard_map/ppermute | solution.py:358
  22.2 5.2 %collective-permute-start.5 = (f32[136,128]{1,0:T(8,128)S(1)}, f32[136,128]{1,0:T(8,128)S(1)}, u32[]{:S(2)}, u32[]{:S(2)}) collective-permute-start(f32[136,128]{1,0:T(8,128)S(1)} %add_add_fusion.13.refs_0_), channel_id=1, source_target_pairs={{0,64},{32,96},{1,65},{33,97},{2,66},{34,98},{3,67},{35,99},{4,68}... | collective-permute-start | bytes 208904 | tf_op jit(solution)/shard_map/ppermute | solution.py:358
  23.5 4.0 %collective-permute-start.4 = (f32[136,128]{1,0:T(8,128)S(1)}, f32[136,128]{1,0:T(8,128)S(1)}, u32[]{:S(2)}, u32[]{:S(2)}) collective-permute-start(f32[136,128]{1,0:T(8,128)S(1)} %add_add_fusion.13.refs_0_), channel_id=1, source_target_pairs={{0,32},{32,64},{64,96},{1,33},{33,65},{65,97},{2,34},{34,66},{66,9... | collective-permute-start | bytes 208904 | tf_op jit(solution)/shard_map/ppermute | solution.py:358
  27.5 5.7 %collective-permute-start.7 = (f32[136,128]{1,0:T(8,128)S(1)}, f32[136,128]{1,0:T(8,128)S(1)}, u32[]{:S(2)}, u32[]{:S(2)}) collective-permute-start(f32[136,128]{1,0:T(8,128)S(1)} %get-tuple-element.116), channel_id=1, source_target_pairs={{0,8},{4,12},{8,16},{12,20},{16,24},{20,28},{24,0},{28,4},{1,9},{5... | collective-permute-start | bytes 208904 | tf_op jit(solution)/shard_map/ppermute | solution.py:363
  28.1 5.2 %collective-permute-start.8 = (f32[136,128]{1,0:T(8,128)S(1)}, f32[136,128]{1,0:T(8,128)S(1)}, u32[]{:S(2)}, u32[]{:S(2)}) collective-permute-start(f32[136,128]{1,0:T(8,128)S(1)} %get-tuple-element.120), channel_id=1, source_target_pairs={{0,16},{4,20},{8,24},{12,28},{16,0},{20,4},{24,8},{28,12},{1,17},{... | collective-permute-start | bytes 208904 | tf_op jit(solution)/shard_map/ppermute | solution.py:363
  30.9 3.5 %collective-permute-start.9 = (f32[136,128]{1,0:T(8,128)S(1)}, f32[136,128]{1,0:T(8,128)S(1)}, u32[]{:S(2)}, u32[]{:S(2)}) collective-permute-start(f32[136,128]{1,0:T(8,128)S(1)} %get-tuple-element.121), channel_id=1, source_target_pairs={{0,24},{4,28},{8,0},{12,4},{16,8},{20,12},{24,16},{28,20},{1,25},{... | collective-permute-start | bytes 208904 | tf_op jit(solution)/shard_map/ppermute | solution.py:363
  31.8 6.8 %copy-start = (f32[1024]{0:T(1024)S(1)}, f32[1024]{0:T(1024)}, u32[]{:S(2)}) copy-start(f32[1024]{0:T(1024)} %param.8) | copy-start | bytes 12292
  34.5 6.3 %collective-permute-start.10 = (f32[4,136,128]{2,1,0:T(8,128)S(1)}, f32[4,136,128]{2,1,0:T(8,128)S(1)}, u32[]{:S(2)}, u32[]{:S(2)}) collective-permute-start(f32[4,136,128]{2,1,0:T(8,128)S(1)} %get-tuple-element.134), channel_id=1, source_target_pairs={{0,4},{4,0},{8,12},{12,8},{16,20},{20,16},{24,28},{28,24},{1,5},{5... | collective-permute-start | bytes 835592 | tf_op jit(solution)/shard_map/ppermute | solution.py:314
  43.1 4.6 %collective-permute-start.13 = (f32[16,128]{1,0:T(8,128)S(1)}, f32[16,128]{1,0:T(8,128)S(1)}, u32[]{:S(2)}, u32[]{:S(2)}) collective-permute-start(f32[16,128]{1,0:T(8,128)S(1)} %add.492), channel_id=1, source_target_pairs={{0,3},{1,0},{2,1},{3,2},{4,7},{5,4},{6,5},{7,6},{8,11},{9,8},{10,9... | collective-permute-start | bytes 24584 | tf_op jit(solution)/shard_map/ppermute | solution.py:409
  47.0 4.0 %collective-permute-start.12 = (f32[16,128]{1,0:T(8,128)S(1)}, f32[16,128]{1,0:T(8,128)S(1)}, u32[]{:S(2)}, u32[]{:S(2)}) collective-permute-start(f32[16,128]{1,0:T(8,128)S(1)} %add.492), channel_id=1, source_target_pairs={{0,2},{1,3},{2,0},{3,1},{4,6},{5,7},{6,4},{7,5},{8,10},{9,11},{10,... | collective-permute-start | bytes 24584 | tf_op jit(solution)/shard_map/ppermute | solution.py:409
  47.0 4.0 %collective-permute-start.11 = (f32[16,128]{1,0:T(8,128)S(1)}, f32[16,128]{1,0:T(8,128)S(1)}, u32[]{:S(2)}, u32[]{:S(2)}) collective-permute-start(f32[16,128]{1,0:T(8,128)S(1)} %add.492), channel_id=1, source_target_pairs={{0,1},{1,2},{2,3},{3,0},{4,5},{5,6},{6,7},{7,4},{8,9},{9,10},{10,1... | collective-permute-start | bytes 24584 | tf_op jit(solution)/shard_map/ppermute | solution.py:409
  59.6 5.6 %collective-permute-start.14 = (f32[4,136,128]{2,1,0:T(8,128)S(1)}, f32[4,136,128]{2,1,0:T(8,128)S(1)}, u32[]{:S(2)}, u32[]{:S(2)}) collective-permute-start(f32[4,136,128]{2,1,0:T(8,128)S(1)} %slice.421), channel_id=1, source_target_pairs={{0,4},{4,0},{8,12},{12,8},{16,20},{20,16},{24,28},{28,24},{1,5},{5... | collective-permute-start | bytes 835592 | tf_op jit(solution)/shard_map/ppermute | solution.py:314
  65.4 7.2 %collective-permute-start.15 = (f32[136,128]{1,0:T(8,128)S(1)}, f32[136,128]{1,0:T(8,128)S(1)}, u32[]{:S(2)}, u32[]{:S(2)}) collective-permute-start(f32[136,128]{1,0:T(8,128)S(1)} %get-tuple-element.132), channel_id=1, source_target_pairs={{0,8},{4,12},{8,16},{12,20},{16,24},{20,28},{24,0},{28,4},{1,9},{5... | collective-permute-start | bytes 208904 | tf_op jit(solution)/shard_map/ppermute | solution.py:353
  65.5 7.1 %collective-permute-start.16 = (f32[136,128]{1,0:T(8,128)S(1)}, f32[136,128]{1,0:T(8,128)S(1)}, u32[]{:S(2)}, u32[]{:S(2)}) collective-permute-start(f32[136,128]{1,0:T(8,128)S(1)} %get-tuple-element.133), channel_id=1, source_target_pairs={{0,16},{4,20},{8,24},{12,28},{16,0},{20,4},{24,8},{28,12},{1,17},{... | collective-permute-start | bytes 208904 | tf_op jit(solution)/shard_map/ppermute | solution.py:353
  68.3 4.3 %collective-permute-start.17 = (f32[136,128]{1,0:T(8,128)S(1)}, f32[136,128]{1,0:T(8,128)S(1)}, u32[]{:S(2)}, u32[]{:S(2)}) collective-permute-start(f32[136,128]{1,0:T(8,128)S(1)} %get-tuple-element.131), channel_id=1, source_target_pairs={{0,24},{4,28},{8,0},{12,4},{16,8},{20,12},{24,16},{28,20},{1,25},{... | collective-permute-start | bytes 208904 | tf_op jit(solution)/shard_map/ppermute | solution.py:353
  72.7 7.7 %collective-permute-start.20 = (f32[136,128]{1,0:T(8,128)S(1)}, f32[136,128]{1,0:T(8,128)S(1)}, u32[]{:S(2)}, u32[]{:S(2)}) collective-permute-start(f32[136,128]{1,0:T(8,128)S(1)} %add_add_fusion.7.refs_4_), channel_id=1, source_target_pairs={{96,0},{97,1},{98,2},{99,3},{100,4},{101,5},{102,6},{103,7},{104,8... | collective-permute-start | bytes 208904 | tf_op jit(solution)/shard_map/ppermute | solution.py:358
  74.0 6.7 %collective-permute-start.19 = (f32[136,128]{1,0:T(8,128)S(1)}, f32[136,128]{1,0:T(8,128)S(1)}, u32[]{:S(2)}, u32[]{:S(2)}) collective-permute-start(f32[136,128]{1,0:T(8,128)S(1)} %add_add_fusion.7.refs_4_), channel_id=1, source_target_pairs={{64,0},{96,32},{65,1},{97,33},{66,2},{98,34},{67,3},{99,35},{68,4}... | collective-permute-start | bytes 208904 | tf_op jit(solution)/shard_map/ppermute | solution.py:358
  75.3 5.4 %collective-permute-start.18 = (f32[136,128]{1,0:T(8,128)S(1)}, f32[136,128]{1,0:T(8,128)S(1)}, u32[]{:S(2)}, u32[]{:S(2)}) collective-permute-start(f32[136,128]{1,0:T(8,128)S(1)} %add_add_fusion.7.refs_4_), channel_id=1, source_target_pairs={{32,0},{64,32},{96,64},{33,1},{65,33},{97,65},{34,2},{66,34},{98,6... | collective-permute-start | bytes 208904 | tf_op jit(solution)/shard_map/ppermute | solution.py:358
  80.7 7.9 %collective-permute-start.21 = (f32[136,128]{1,0:T(8,128)S(1)}, f32[136,128]{1,0:T(8,128)S(1)}, u32[]{:S(2)}, u32[]{:S(2)}) collective-permute-start(f32[136,128]{1,0:T(8,128)S(1)} %get-tuple-element.112), channel_id=1, source_target_pairs={{0,8},{4,12},{8,16},{12,20},{16,24},{20,28},{24,0},{28,4},{1,9},{5... | collective-permute-start | bytes 208904 | tf_op jit(solution)/shard_map/ppermute | solution.py:363
  81.8 6.7 %collective-permute-start.22 = (f32[136,128]{1,0:T(8,128)S(1)}, f32[136,128]{1,0:T(8,128)S(1)}, u32[]{:S(2)}, u32[]{:S(2)}) collective-permute-start(f32[136,128]{1,0:T(8,128)S(1)} %get-tuple-element.118), channel_id=1, source_target_pairs={{0,16},{4,20},{8,24},{12,28},{16,0},{20,4},{24,8},{28,12},{1,17},{... | collective-permute-start | bytes 208904 | tf_op jit(solution)/shard_map/ppermute | solution.py:363
  84.6 4.0 %collective-permute-start.23 = (f32[136,128]{1,0:T(8,128)S(1)}, f32[136,128]{1,0:T(8,128)S(1)}, u32[]{:S(2)}, u32[]{:S(2)}) collective-permute-start(f32[136,128]{1,0:T(8,128)S(1)} %get-tuple-element.119), channel_id=1, source_target_pairs={{0,24},{4,28},{8,0},{12,4},{16,8},{20,12},{24,16},{28,20},{1,25},{... | collective-permute-start | bytes 208904 | tf_op jit(solution)/shard_map/ppermute | solution.py:363
  88.8 5.5 %collective-permute-start.24 = (f32[4,136,128]{2,1,0:T(8,128)S(1)}, f32[4,136,128]{2,1,0:T(8,128)S(1)}, u32[]{:S(2)}, u32[]{:S(2)}) collective-permute-start(f32[4,136,128]{2,1,0:T(8,128)S(1)} %get-tuple-element.129), channel_id=1, source_target_pairs={{0,4},{4,0},{8,12},{12,8},{16,20},{20,16},{24,28},{28,24},{1,5},{5... | collective-permute-start | bytes 835592 | tf_op jit(solution)/shard_map/ppermute | solution.py:314
where the time goes:
time: 97.8 us; the launch traced here: 97.1 us
  Pallas kernels  45.4 us (46%)
  starting transfers between devices  43.5 us (44%)
  waiting for transfers between devices  5.79 us (6%)
  between operations  1.26 us (1%)
  other arithmetic  1.13 us (1%)
    pallas_call x14, Pallas kernels, call(): pl.pallas_call(body, out_shape=shapes, in_specs=specs, out_specs=out_spec...  45.4 us
    ppermute x6, starting transfers between devices, scan(): lax.ppermute(row, 'seqin', [(a, b) for a, b in pairs if 0 <= b < 4])  12.3 us
    ppermute x4, starting transfers between devices, swap(): return lax.ppermute(x, 'seqout', CORE)  10.1 us
    ppermute x6, starting transfers between devices, scan(): lax.ppermute(got[k], 'seqout', [(i, (i + 2 * k) % 8) for i in range(8)])  8.41 us
    ppermute x6, starting transfers between devices, scan(): lax.ppermute(came[k], 'seqout', [(i, (i + 2 * k) % 8) for i in range(8)])  8.19 us
    ppermute x3, starting transfers between devices, shards(): lax.ppermute(local, 'head', [(i, (i + k) % 4) for i in range(4)])  4.53 us
    ppermute x3, waiting for transfers between devices, shards(): lax.ppermute(local, 'head', [(i, (i + k) % 4) for i in range(4)])  3.3 us
  transfers between devices with their start and end apart: 25, of which 5 were waited for; matrix products, arithmetic and copies ran while one was open for 0% of the time, Pallas kernels for 27%

commit v1 on v0

v1 whole, which is shorter than its diff:
```python
import functools

import jax
import jax.numpy as jnp
from jax import lax
from jax.experimental import pallas as pl
from jax.experimental.pallas import tpu as pltpu
from jax.sharding import PartitionSpec as P

E = 128
D = 4096
ROWS = 1024
BLOCK = 512
HALF = 256
AUG = E + 8
F32 = jnp.float32
BF16 = jnp.bfloat16
VMEM_LIMIT = 16 * 1024 * 1024
UNROLL = 2
ORDER = (2, 1, 3)
USE = (0, 2, 1, 3)
ROW_ORDER = (1, 3, 2)


def phi(x):
    xf = x.astype(F32)
    return jnp.where(xf > 0, xf + 1.0, jnp.exp(xf)).astype(BF16)


def slope(x):
    xf = x.astype(F32)
    return jnp.where(xf > 0, 1.0, jnp.exp(xf))


def split(x):
    hi = x.astype(BF16)
    return hi, (x - hi.astype(F32)).astype(BF16)


def dot(a, b, ca=1, cb=0):
    return lax.dot_general(a, b, (((ca,), (cb,)), ((), ())), preferred_element_type=F32)


def iota(shape, dim):
    return lax.broadcasted_iota(jnp.int32, shape, dim)


def column(row):
    return jnp.transpose(jnp.broadcast_to(row, (E, E)))


def columns(at):
    core = lax.rem(lax.axis_index("seqout"), 2)
    return pl.ds(pl.multiple_of(lax.rem(4 * core + at, 8) * E, E), E)


def each(count, body):
    def step(j, carry):
        body(j)
        return carry

    lax.fori_loop(0, count, step, 0, unroll=UNROLL)


def block_sums(fk, v):
    kv = dot(fk, v, 0, 0)
    z = jnp.sum(fk.astype(F32), axis=0, keepdims=True)
    return jnp.concatenate([kv, jnp.broadcast_to(z, (8, E))], axis=0)


def sums_kernel(
    keys_ref, values_ref, queries_ref, cotangent_ref, q_ref, k_ref, v_ref, ct_ref, fq_ref, fk_ref, nd_ref, gr_ref, g_ref, first_ref, last_ref, mask_ref, sems
):
    half = ROWS // 2
    near = pl.ds(pl.multiple_of(half * lax.rem(lax.axis_index("seqout"), 2), half), half)
    away = pl.ds(pl.multiple_of(half - half * lax.rem(lax.axis_index("seqout"), 2), half), half)
    top, bottom = pl.ds(0, BLOCK), pl.ds(BLOCK, BLOCK)
    copies = []
    for at in ((top, near), (top, away), (bottom, slice(None))):
        for src, dst in ((keys_ref, k_ref), (values_ref, v_ref)):
            copies.append(pltpu.make_async_copy(src.at[at], dst.at[at], sems.at[len(copies)]))
    for src, dst in ((queries_ref, q_ref), (cotangent_ref, ct_ref)):
        copies.append(pltpu.make_async_copy(src, dst, sems.at[len(copies)]))
    for copy in copies:
        copy.start()
    write_masks(mask_ref)
    for step in range(4):
        b = step // 2
        rows = pl.ds(b * BLOCK, BLOCK)
        if step < 3:
            copies[2 * step].wait()
            copies[2 * step + 1].wait()

        def group(i):
            done = []
            for j in (4 * (step % 2) + 2 * i, 4 * (step % 2) + 2 * i + 1):
                cols = columns(j)
                fk = phi(k_ref[rows, cols])
                done.append((j, cols, fk, block_sums(fk, v_ref[rows, cols])))
            for j, cols, fk, part in done:
                fk_ref[rows, cols] = fk
                (last_ref if b else first_ref)[j] = part

        each(2, group)
    for copy in copies[6:]:
        copy.wait()


def intra_kernel(start, count, sent_ref, q_ref, k_ref, v_ref, ct_ref, fq_ref, fk_ref, nd_ref, gr_ref, g_ref, token_ref):
    token_ref[...] = jnp.zeros_like(token_ref)
    tri = iota((HALF, HALF), 0) >= iota((HALF, HALF), 1)
    ones = jnp.ones((BLOCK, E), BF16)

    def one(j):
        cols = columns(start + j)
        done = []
        for b in range(2):
            rows = pl.ds(b * BLOCK, BLOCK)
            fq, fk = phi(q_ref[rows, cols]), fk_ref[rows, cols]
            done.append((rows, fq))
            va = jnp.concatenate([v_ref[rows, cols], ones], axis=1)
            w00 = jnp.where(tri, dot(fq[:HALF], fk[:HALF], 1, 1), 0.0).astype(BF16)
            w10 = dot(fq[HALF:], fk[:HALF], 1, 1).astype(BF16)
            w11 = jnp.where(tri, dot(fq[HALF:], fk[HALF:], 1, 1), 0.0).astype(BF16)
            nd_ref[start + j, pl.ds(b * BLOCK, HALF), :] = dot(w00, va[:HALF])
            nd_ref[start + j, pl.ds(b * BLOCK + HALF, HALF), :] = dot(jnp.concatenate([w10, w11], axis=1), va)
        for rows, fq in done:
            fq_ref[rows, cols] = fq

    each(count, one)


def attn_kernel(start, count, gain_ref, st_ref, first_ref, q_ref, k_ref, v_ref, ct_ref, fq_ref, fk_ref, nd_ref, gr_ref, g_ref, sums_ref, sq_acc, pr_acc):
    sq_acc[...] = jnp.zeros_like(sq_acc)
    pr_acc[...] = jnp.zeros_like(pr_acc)

    def pair(i):
        for b in range(2):
            rows = pl.ds(b * BLOCK, BLOCK)
            squares, products = [], []
            for j in (2 * i, 2 * i + 1):
                cols = columns(start + j)
                aug = st_ref[j] + first_ref[start + j] if b else st_ref[j]
                s_hi, s_lo = split(aug[:E])
                n_hi, n_lo = split(column(aug[E : E + 1]))
                rhs = jnp.concatenate([jnp.concatenate([s_hi, n_hi], axis=1), jnp.concatenate([s_lo, n_lo], axis=1)], axis=0)
                fq = fq_ref[rows, cols]
                nd = nd_ref[start + j, rows, :] + dot(jnp.concatenate([fq, fq], axis=1), rhs)
                inv = 1.0 / nd[:, E:]
                attn = nd[:, :E] * inv
                nd_ref[start + j, rows, :] = jnp.concatenate([attn, inv], axis=1)
                squares.append(attn * attn)
                products.append(ct_ref[rows, cols].astype(F32) * gain_ref[:, cols] * attn)
            sq_acc[rows, :] += squares[0] + squares[1]
            pr_acc[rows, :] += products[0] + products[1]

    each(count // 2, pair)
    for i in range(8):
        rows = pl.ds(i * E, E)
        sums_ref[pl.ds(i, 1), :] = jnp.sum(jnp.transpose(sq_acc[rows, :]), axis=0, keepdims=True)
        sums_ref[pl.ds(8 + i, 1), :] = jnp.sum(jnp.transpose(pr_acc[rows, :]), axis=0, keepdims=True)


def spread(sc_ref, scale_ref, coef_ref):
    for i in range(8):
        rows = pl.ds(i * E, E)
        scale_ref[rows, :] = column(sc_ref[pl.ds(i, 1), :])
        if coef_ref is not None:
            coef_ref[rows, :] = column(sc_ref[pl.ds(8 + i, 1), :])


def rows_kernel(gain_ref, sent_ref, q_ref, k_ref, v_ref, ct_ref, fq_ref, fk_ref, nd_ref, gr_ref, g_ref, p_ref, s_ref):
    ones = jnp.ones((8, 2 * E), BF16)

    def row_sums(x):
        hi, lo = split(x)
        return dot(ones, jnp.concatenate([hi, lo], axis=1), 1, 1)[0:1]

    def one(j):
        cols = columns(j)
        for b in range(2):
            rows = pl.ds(b * BLOCK, BLOCK)
            attn, inv = nd_ref[j, rows, :E], nd_ref[j, rows, E:]
            wi = ct_ref[rows, cols].astype(F32) * gain_ref[:, cols] * inv
            ai = attn * inv
            p, s = row_sums(wi * attn), row_sums(ai * attn)
            gr_ref[j, rows, :] = wi
            nd_ref[j, rows, E:] = ai
            for i in range(4):
                p_ref[j, pl.ds(4 * b + i, 1), :] = p[:, i * E : (i + 1) * E]
                s_ref[j, pl.ds(4 * b + i, 1), :] = s[:, i * E : (i + 1) * E]

    each(8, one)


def grad_kernel(
    gain_ref, sc_ref, p_ref, s_ref, q_ref, k_ref, v_ref, ct_ref, fq_ref, fk_ref, nd_ref, gr_ref, g_ref, first_ref, last_ref, gd_ref, scale_ref, coef_ref
):
    spread(sc_ref, scale_ref, coef_ref)

    def group(i):
        done = []
        for j in (2 * i, 2 * i + 1):
            cols = columns(j)
            gd = sc_ref[8:16, :] * s_ref[j] - sc_ref[0:8, :] * p_ref[j]
            hi = gd.astype(BF16).astype(F32)
            for b in range(2):
                rows = pl.ds(b * BLOCK, BLOCK)
                g = (scale_ref[rows, :] * gr_ref[j, rows, :] - coef_ref[rows, :] * nd_ref[j, rows, E:]).astype(BF16)
                pieces = [jnp.concatenate([x[4 * b + i : 4 * b + i + 1] for i in range(4)], axis=1) for x in (hi, gd - hi)]
                pieces.append(jnp.zeros((14, BLOCK), F32))
                fq = fq_ref[rows, cols]
                rden = dot(jnp.concatenate(pieces, axis=0).astype(BF16), fq)
                rden = jnp.broadcast_to(rden[0:1] + rden[1:2], (8, E))
                done.append((j, b, rows, g, jnp.concatenate([dot(fq, g, 0, 0), rden], axis=0)))
            gd_ref[j] = gd
        for j, b, rows, g, part in done:
            g_ref[rows, pl.ds(pl.multiple_of(j * E, E), E)] = g
            (last_ref if b else first_ref)[j] = part

    each(4, group)


def back_kernel(
    start, count, gain_ref, sc_ref, st_ref, first_ref, gd_ref, sent_ref, q_ref, k_ref, v_ref, ct_ref, fq_ref, fk_ref, nd_ref, gr_ref, g_ref,
    dq_ref, mixed_ref, token_ref, scale_ref, dq_buf, mixed_buf, sems,
):
    token_ref[...] = jnp.zeros_like(token_ref)
    spread(sc_ref, scale_ref, None)
    low = iota((HALF, HALF), 0) >= iota((HALF, HALF), 1)
    up = iota((HALF, HALF), 0) <= iota((HALF, HALF), 1)

    def copies(j):
        cols = columns(start + j)
        return [
            pltpu.make_async_copy(dq_buf.at[j], dq_ref.at[:, cols], sems.at[0, j]),
            pltpu.make_async_copy(mixed_buf.at[j], mixed_ref.at[:, cols], sems.at[1, j]),
        ]

    def one(j):
        cols = columns(start + j)
        for b in range(2):
            rows = pl.ds(b * BLOCK, BLOCK)
            v, fq, fk = v_ref[rows, cols], fq_ref[rows, cols], fk_ref[rows, cols]
            g = g_ref[rows, pl.ds(pl.multiple_of((start + j) * E, E), E)]
            gd = jnp.concatenate([column(gd_ref[start + j, pl.ds(4 * b + i, 1), :]) for i in range(4)], axis=0)
            add0, add1 = (jnp.concatenate([x, x], axis=1) for x in (gd[:HALF], gd[HALF:]))
            m00 = jnp.where(low, dot(g[:HALF], v[:HALF], 1, 1) + add0, 0.0).astype(BF16)
            m10 = (dot(g[HALF:], v[:HALF], 1, 1) + add1).astype(BF16)
            m11 = jnp.where(low, dot(g[HALF:], v[HALF:], 1, 1) + add1, 0.0).astype(BF16)
            w00 = jnp.where(up, dot(fk[:HALF], fq[:HALF], 1, 1), 0.0).astype(BF16)
            w10 = dot(fk[:HALF], fq[HALF:], 1, 1).astype(BF16)
            w11 = jnp.where(up, dot(fk[HALF:], fq[HALF:], 1, 1), 0.0).astype(BF16)
            at = start % 4 + j
            aug = st_ref[at] + first_ref[start + j] if b else st_ref[at]
            s_hi, s_lo = split(aug[:E])
            rhs = jnp.concatenate([s_hi, s_lo], axis=1)
            dfq = dot(jnp.concatenate([g, g], axis=1), rhs, 1, 1) + gd * aug[E : E + 1]
            dfq = dfq + jnp.concatenate([dot(m00, fk[:HALF]), dot(jnp.concatenate([m10, m11], axis=1), fk)], axis=0)
            dq_buf[j, rows, :] = (dfq * slope(q_ref[rows, cols])).astype(BF16)
            mixed_buf[j, rows, :] = (nd_ref[start + j, rows, :E] * scale_ref[rows, :] * gain_ref[:, cols]).astype(BF16)
            nd_ref[start + j, pl.ds(b * BLOCK, HALF), :E] = dot(jnp.concatenate([m00, m10], axis=0), fq, 0, 0)
            nd_ref[start + j, pl.ds(b * BLOCK + HALF, HALF), :E] = dot(m11, fq[HALF:], 0, 0)
            nd_ref[start + j, pl.ds(b * BLOCK, HALF), E:] = dot(jnp.concatenate([w00, w10], axis=1), g)
            nd_ref[start + j, pl.ds(b * BLOCK + HALF, HALF), E:] = dot(w11, g[HALF:])
        for copy in copies(j):
            copy.start()

    each(count, one)
    for j in range(count):
        for copy in copies(j):
            copy.wait()


def last_kernel(start, count, lt_ref, last_ref, q_ref, k_ref, v_ref, ct_ref, fq_ref, fk_ref, nd_ref, gr_ref, g_ref, gk_ref, gv_ref, gk_buf, gv_buf, sems):

    def copies(j):
        cols = columns(start + j)
        return [
            pltpu.make_async_copy(gk_buf.at[j], gk_ref.at[:, cols], sems.at[0, j]),
            pltpu.make_async_copy(gv_buf.at[j], gv_ref.at[:, cols], sems.at[1, j]),
        ]

    def group(i):
        for j in (2 * i, 2 * i + 1):
            cols = columns(start + j)
            for b in range(2):
                rows = pl.ds(b * BLOCK, BLOCK)
                v, fk = v_ref[rows, cols], fk_ref[rows, cols]
                aug = lt_ref[j] if b else lt_ref[j] + last_ref[start + j]
                l_hi, l_lo = split(aug[:E])
                dfk = dot(jnp.concatenate([v, v], axis=1), jnp.concatenate([l_hi, l_lo], axis=1), 1, 1)
                dfk = dfk + nd_ref[start + j, rows, :E] + aug[E : E + 1]
                dv = dot(jnp.concatenate([fk, fk], axis=1), jnp.concatenate([l_hi, l_lo], axis=0))
                gk_buf[j, rows, :] = (dfk * slope(k_ref[rows, cols])).astype(BF16)
                gv_buf[j, rows, :] = (dv + nd_ref[start + j, rows, E:]).astype(BF16)
        for j in (2 * i, 2 * i + 1):
            for copy in copies(j):
                copy.start()

    for i in range(count // 2):
        group(i)
    for j in range(count):
        for copy in copies(j):
            copy.wait()


def vmem(shape, dtype=F32, into=None):
    return pltpu.VMEM(shape, dtype), into


def hbm(shape, dtype, into=None):
    return pltpu.HBM(shape, dtype), into


def call(kernel, near, far, outs, scratch=(), flops=0):
    arrays = [pltpu.with_memory_space_constraint(a, pltpu.VMEM) for a in near]
    arrays += far
    specs = [pl.BlockSpec(memory_space=pltpu.VMEM)] * len(near) + [pl.BlockSpec(memory_space=pl.ANY)] * len(far)
    first, shapes, out_specs, aliases = len(arrays), [], [], {}
    for i, (shape, into) in enumerate(outs):
        space = pl.ANY if shape.memory_space == pltpu.HBM else pltpu.VMEM
        shapes.append(shape)
        out_specs.append(pl.BlockSpec(memory_space=space))
        if into is not None:
            aliases[len(arrays)] = i
            arrays.append(pltpu.with_memory_space_constraint(into, shape.memory_space))
            specs.append(pl.BlockSpec(memory_space=space))

    def body(*refs):
        bank, nd, gr, *own = refs[len(arrays) :]
        kernel(*refs[:first], *(bank.at[i] for i in range(6)), nd, gr, bank.at[6], *own)

    return pl.pallas_call(
        body,
        out_shape=shapes,
        in_specs=specs,
        out_specs=out_specs,
        scratch_shapes=list(scratch),
        input_output_aliases=aliases,
        compiler_params=pltpu.CompilerParams(vmem_limit_bytes=VMEM_LIMIT),
        cost_estimate=pl.CostEstimate(flops=flops, bytes_accessed=1 << 20, transcendentals=0),
    )(*arrays)


CORE = [(i, i ^ 1) for i in range(8)]


def send_x(x, k):
    return lax.ppermute(x, "seqout", [(i, (i + 2 * k) % 8) for i in range(8)])


def send_y(x, k):
    return lax.ppermute(x, "seqin", [(i, (i + k) % 4) for i in range(4)])


def swap(x):
    return lax.ppermute(x, "seqout", CORE)


TO, SOURCE, BEFORE, AFTER, LOWER, UPPER, ROW_BEFORE, ROW_AFTER, MASKS = 0, 16, 32, 48, 64, 65, 66, 70, 80


def write_masks(mask_ref):
    place = lax.axis_index("seqout")
    x, core = lax.div(place, 2), lax.rem(place, 2)

    def put(at, true):
        mask_ref[pl.ds(at, 1), :] = jnp.full((1, E), jnp.where(true, 1.0, 0.0), F32)

    for k in range(4):
        to = lax.rem(x + k, 4)
        for i in range(4):
            source = lax.rem(x + 4 - i, 4)
            put(TO + 4 * k + i, to == i)
            put(SOURCE + 4 * k + i, lax.rem(x + 4 - k, 4) == i)
            put(BEFORE + 4 * k + i, source < to)
            put(AFTER + 4 * k + i, source > to)
    y = lax.axis_index("seqin")
    for k in range(4):
        put(ROW_BEFORE + k, y >= k)
        put(ROW_AFTER + k, y < 4 - k)
    put(LOWER, core == 0)
    put(UPPER, core == 1)


def keep_where(mask, at, x):
    return jnp.where(mask[at : at + 1] > 0, x, 0.0)


def add(parts):
    return functools.reduce(lambda a, b: a + b, parts)


def scan(sums, mask, reverse, during):
    other = swap(sums[4:])
    total = sums[:4] + other + during[0](sums)
    got = {k: add([keep_where(mask, TO + 4 * k + h, total[h]) for h in range(4)]) for k in (*ORDER, 0)}
    own = got[0]
    for k in ORDER:
        got[k] = send_x(got[k], k)
    row = add([got[k] for k in USE]) + during[1](own)
    rows = []
    for k in ROW_ORDER:
        came = send_y(row, -k if reverse else k)
        rows.append(keep_where(mask, (ROW_AFTER if reverse else ROW_BEFORE) + k, came))
    base = rows[0] + rows[1] + rows[2] + during[2](row)
    at = AFTER if reverse else BEFORE
    came = {k: base + add([keep_where(mask, at + 4 * k + m, got[m]) for m in USE]) for k in (*ORDER, 0)}
    for k in ORDER:
        came[k] = send_x(came[k], k)
    zeros = during[3](base)
    out = [add([keep_where(mask, SOURCE + 4 * k + h, came[k]) for k in USE]) + zeros for h in range(4)]
    return jnp.stack(out), other


def shards(queries, keys, values, gain, cotangent):
    gain = gain.reshape(1, ROWS)
    shape = (ROWS, ROWS)
    aug = vmem((4, AUG, E))
    token = vmem((8, E))
    acc = pltpu.VMEM((ROWS, E), F32)
    sems = pltpu.SemaphoreType.DMA
    kept = {}
    sizes = {"bank": ((7, ROWS, ROWS), BF16), "nd": ((8, ROWS, 2 * E), F32), "gr": ((8, ROWS, E), F32)}

    def run(kernel, near, far, outs, scratch=(), flops=0):
        held = [vmem(*size, kept.get(name)) for name, size in sizes.items()]
        got = call(kernel, near, [pltpu.with_memory_space_constraint(a, pltpu.HBM) if a.shape == shape else a for a in far], held + outs, scratch, flops)
        kept.update(zip(sizes, got))
        return got[len(sizes) :]

    parts = vmem((8, AUG, E))
    far = [keys, values, queries, cotangent]
    first, last, mask = run(sums_kernel, [], far, [parts, parts, vmem((MASKS, E))], [sems((8,))], 1 << 28)
    sums = first + last

    def intra(start, count):
        def during(sent):
            kernel = functools.partial(intra_kernel, start, count)
            (zeros,) = run(kernel, [], [sent], [token], (), count << 28)
            return zeros[:1]

        return during

    st, other = scan(sums, mask, False, (intra(0, 2), intra(2, 2), intra(4, 2), intra(6, 2)))
    st_keep = st + keep_where(mask, UPPER, other)
    st_send = swap(st + keep_where(mask, LOWER, sums[:4]))

    def attend(start, state):
        kernel = functools.partial(attn_kernel, start, 4)
        near = [gain, state, first]
        return run(kernel, near, [], [vmem((16, E))], (acc, acc), 1 << 28)[0]

    local = attend(0, st_keep)
    local = local + attend(4, st_send)
    per_head = vmem((8, 8, E))
    p, s = run(rows_kernel, [gain], [local], [per_head, per_head], (), 1 << 28)
    far = [lax.ppermute(local, "head", [(i, (i + k) % 4) for i in range(4)]) for k in (1, 3, 2)]
    whole = local + far[0] + far[1] + far[2]
    scale = lax.rsqrt(whole[:8] / D + 1e-06)
    sc = jnp.concatenate([scale, scale**3 * whole[8:] / D], axis=0)

    back_first, back_last, gd = run(grad_kernel, [gain, sc, p, s], [], [parts, parts, per_head], (acc, acc), 1 << 29)
    back_sums = back_first + back_last
    dq = mixed = None

    def back(start, count):
        def during(sent):
            nonlocal dq, mixed
            state = st_send if start >= 4 else st_keep
            out = pltpu.VMEM((count, ROWS, E), BF16)
            dq, mixed, zeros = run(
                functools.partial(back_kernel, start, count),
                [gain, sc, state, first, gd], [sent], [hbm(shape, BF16, dq), hbm(shape, BF16, mixed), token],
                (acc, out, out, sems((2, count))), count << 29,
            )
            return zeros[:1]

        return during

    lt, other = scan(back_sums, mask, True, (back(0, 2), back(2, 2), back(4, 2), back(6, 2)))
    lt_keep = lt + keep_where(mask, LOWER, other)
    lt_send = swap(lt + keep_where(mask, UPPER, back_sums[:4]))
    gk = gv = None
    for start, later in ((0, lt_keep), (4, lt_send)):
        out = pltpu.VMEM((4, ROWS, E), BF16)
        gk, gv = run(
            functools.partial(last_kernel, start, 4), [later, back_last], [],
            [hbm(shape, BF16, gk), hbm(shape, BF16, gv)], (out, out, sems((2, 4))), 1 << 28,
        )
    return mixed, dq, gk, gv


def solution(mesh):
    rows = P(("seqin", "seqout"), "head")
    return jax.shard_map(
        shards,
        mesh=mesh,
        in_specs=(rows, rows, rows, P("head"), rows),
        out_specs=(rows, rows, rows, rows),
        check_vma=False,
    )
```

time: 97.8 us -> 84.1 us (0.86)
  Pallas kernels: 45.4 us -> 35.4 us
  starting transfers between devices: 43.5 us -> 40.5 us
    pallas_call x14 -> x15, Pallas kernels: 45.4 us -> 35.4 us  [call(): pl.pallas_call(body, out_shape=shapes, in_specs=specs, out_specs=out_spec...]
    ppermute x18, starting transfers between devices: 28.9 us -> 23.8 us  [the longest x12 16.2 us: send_x(): return lax.ppermute(x, 'seqout', [(i, (i + 2 * k) % 8) for i in range(8)])]
    ppermute x3, waiting for transfers between devices: 3.3 us -> 0.02 us  [shards(): lax.ppermute(local, 'head', [(i, (i + k) % 4) for i in range(4)])]
    ppermute x18, waiting for transfers between devices: 2.47 us -> 5.54 us  [the longest x6 3.11 us: send_y(): return lax.ppermute(x, 'seqin', [(i, (i + k) % 4) for i in range(4)])]
    ppermute x4, starting transfers between devices: 10.1 us -> 11.6 us  [swap(): return lax.ppermute(x, 'seqout', CORE)]
  transfers between devices with their start and end apart: 25 -> 25, of which waited for: 5 -> 7; matrix products, arithmetic and copies ran while one was open for 0% -> 0% of each run, Pallas kernels for 27% -> 29%
where the time goes in v1:
time: 84.1 us; the launch traced here: 84 us
  starting transfers between devices  40.5 us (48%)
  Pallas kernels  35.4 us (42%)
  waiting for transfers between devices  5.58 us (7%)
  between operations  1.22 us (1%)
  other arithmetic  1.14 us (1%)
    pallas_call x15, Pallas kernels, call(): pl.pallas_call(body, out_shape=shapes, in_specs=specs, out_specs=out_spec...  35.4 us
    ppermute x12, starting transfers between devices, send_x(): return lax.ppermute(x, 'seqout', [(i, (i + 2 * k) % 8) for i in range(8)])  16.2 us
    ppermute x4, starting transfers between devices, swap(): return lax.ppermute(x, 'seqout', CORE)  11.6 us
    ppermute x6, starting transfers between devices, send_y(): return lax.ppermute(x, 'seqin', [(i, (i + k) % 4) for i in range(4)])  7.63 us
    ppermute x3, starting transfers between devices, shards(): lax.ppermute(local, 'head', [(i, (i + k) % 4) for i in range(4)])  5.14 us
    ppermute x6, waiting for transfers between devices, send_y(): return lax.ppermute(x, 'seqin', [(i, (i + k) % 4) for i in range(4)])  3.11 us
    ppermute x12, waiting for transfers between devices, send_x(): return lax.ppermute(x, 'seqout', [(i, (i + 2 * k) % 8) for i in range(8)])  2.43 us
  transfers between devices with their start and end apart: 25, of which 7 were waited for; matrix products, arithmetic and copies ran while one was open for 0% of the time, Pallas kernels for 29%

profile of v1, /device:TPU:1, one launch (start us, length us, event | category | flops | bytes accessed | tf_op | source)
XLA Modules:
  0.0 84.0 jit_solution(7136135476707642979)
XLA Ops:
  0.6 4.3 %shard_map.84 = (bf16[7,1024,1024]{2,1,0:T(8,128)(2,1)S(1)}, f32[8,1024,256]{2,1,0:T(8,128)S(1)}, f32[8,1024,128]{2,1,0:T(8,128)S(1)}, f32[8,136,128]{2,1,0:T(8,...) custom-call(bf16[1024,1024]{1,0:T(8,128)(2,1)} %refs_0_.1, bf16[1024,1024]{1,0:T(8,128)(2,1)} %refs_1_.1, ...), custom_call_target="tpu_custom_call" | custom-call | flops 268435456 | bytes 1048576 | tf_op jit(solution)/shard_map/pallas_call | solution.py:334
  5.1 1.5 %collective-permute-start = (f32[4,136,128]{2,1,0:T(8,128)S(1)}, f32[4,136,128]{2,1,0:T(8,128)S(1)}, u32[]{:S(2)}, u32[]{:S(2)}) collective-permute-start(f32[4,136,128]{2,1,0:T(8,128)S(1)} %slice.437), channel_id=1, source_target_pairs={{0,4},{4,0},{8,12},{12,8},{16,20},{20,16},{24,28},{28,24},{1,5},{5... | collective-permute-start | bytes 835592 | tf_op jit(solution)/shard_map/ppermute | solution.py:358
  6.6 1.2 %shard_map.85 = (bf16[7,1024,1024]{2,1,0:T(8,128)(2,1)S(1)}, f32[8,1024,256]{2,1,0:T(8,128)S(1)}, f32[8,1024,128]{2,1,0:T(8,128)S(1)}, f32[8,128]{1,0:T(8,128)S(1)}) custom-call(f32[8,136,128]{2,1,0:T(8,128)S(1)} %add.428.refs_0_, bf16[7,1024,1024]{2,1,0:T(8,128)(2,1)S(1)} %get-tuple-element.79.refs_1_, ...), custom_call_target="tpu_custom_call", output_to_operand_aliasing={{0}: (1, {}), {1}: (2, {}), {2}: (3, {})} | custom-call | flops 536870912 | bytes 1048576 | tf_op jit(solution)/shard_map/pallas_call | solution.py:334
  7.9 2.9 %collective-permute-start.1 = (f32[136,128]{1,0:T(8,128)S(1)}, f32[136,128]{1,0:T(8,128)S(1)}, u32[]{:S(2)}, u32[]{:S(2)}) collective-permute-start(f32[136,128]{1,0:T(8,128)S(1)} %get-tuple-element.176), channel_id=1, source_target_pairs={{0,16},{4,20},{8,24},{12,28},{16,0},{20,4},{24,8},{28,12},{1,17},{... | collective-permute-start | bytes 208904 | tf_op jit(solution)/shard_map/ppermute | solution.py:350
  10.8 0.3 collective-permute-start.2
  11.2 2.4 %collective-permute-start.3 = (f32[136,128]{1,0:T(8,128)S(1)}, f32[136,128]{1,0:T(8,128)S(1)}, u32[]{:S(2)}, u32[]{:S(2)}) collective-permute-start(f32[136,128]{1,0:T(8,128)S(1)} %get-tuple-element.175), channel_id=1, source_target_pairs={{0,24},{4,28},{8,0},{12,4},{16,8},{20,12},{24,16},{28,20},{1,25},{... | collective-permute-start | bytes 208904 | tf_op jit(solution)/shard_map/ppermute | solution.py:350
  13.6 1.1 %shard_map.86 = (bf16[7,1024,1024]{2,1,0:T(8,128)(2,1)S(1)}, f32[8,1024,256]{2,1,0:T(8,128)S(1)}, f32[8,1024,128]{2,1,0:T(8,128)S(1)}, f32[8,128]{1,0:T(8,128)S(1)}) custom-call(f32[136,128]{1,0:T(8,128)S(1)} %get-tuple-element.174.refs_0_, ...), custom_call_target="tpu_custom_call", output_to_operand_aliasing={{0}: (1, {}), {1}: (2, {}), {2}: (3, {})} | custom-call | flops 536870912 | bytes 1048576 | tf_op jit(solution)/shard_map/pallas_call | solution.py:334
  14.8 0.4 collective-permute-done.2
  15.2 3.0 %collective-permute-start.6 = (f32[136,128]{1,0:T(8,128)S(1)}, f32[136,128]{1,0:T(8,128)S(1)}, u32[]{:S(2)}, u32[]{:S(2)}) collective-permute-start(f32[136,128]{1,0:T(8,128)S(1)} %add_add_fusion.13.refs_0_), channel_id=1, source_target_pairs={{0,64},{32,96},{64,0},{96,32},{1,65},{33,97},{65,1},{97,33},{2,66}... | collective-permute-start | bytes 208904 | tf_op jit(solution)/shard_map/ppermute | solution.py:354
  18.2 0.8 collective-permute-start.5
  19.0 0.7 collective-permute-start.4
  19.7 1.1 %shard_map.87 = (bf16[7,1024,1024]{2,1,0:T(8,128)(2,1)S(1)}, f32[8,1024,256]{2,1,0:T(8,128)S(1)}, f32[8,1024,128]{2,1,0:T(8,128)S(1)}, f32[8,128]{1,0:T(8,128)S(1)}) custom-call(f32[136,128]{1,0:T(8,128)S(1)} %add_add_fusion.13.refs_0_, ...), custom_call_target="tpu_custom_call", output_to_operand_aliasing={{0}: (1, {}), {1}: (2, {}), {2}: (3, {})} | custom-call | flops 536870912 | bytes 1048576 | tf_op jit(solution)/shard_map/pallas_call | solution.py:334
  20.9 0.5 collective-permute-done.5
  21.4 2.1 %collective-permute-done.4 = f32[136,128]{1,0:T(8,128)S(1)} collective-permute-done((f32[136,128]{1,0:T(8,128)S(1)}, f32[136,128]{1,0:T(8,128)S(1)}, u32[]{:S(2)}, u32[]{:S(2)}) %collective-permute-start.4) | collective-permute-done | bytes 69664 | tf_op jit(solution)/shard_map/ppermute | solution.py:354
  23.6 1.5 %collective-permute-start.7 = (f32[136,128]{1,0:T(8,128)S(1)}, f32[136,128]{1,0:T(8,128)S(1)}, u32[]{:S(2)}, u32[]{:S(2)}) collective-permute-start(f32[136,128]{1,0:T(8,128)S(1)} %get-tuple-element.154), channel_id=1, source_target_pairs={{0,16},{4,20},{8,24},{12,28},{16,0},{20,4},{24,8},{28,12},{1,17},{... | collective-permute-start | bytes 208904 | tf_op jit(solution)/shard_map/ppermute | solution.py:350
  25.1 2.1 %collective-permute-start.8 = (f32[136,128]{1,0:T(8,128)S(1)}, f32[136,128]{1,0:T(8,128)S(1)}, u32[]{:S(2)}, u32[]{:S(2)}) collective-permute-start(f32[136,128]{1,0:T(8,128)S(1)} %get-tuple-element.158), channel_id=1, source_target_pairs={{0,8},{4,12},{8,16},{12,20},{16,24},{20,28},{24,0},{28,4},{1,9},{5... | collective-permute-start | bytes 208904 | tf_op jit(solution)/shard_map/ppermute | solution.py:350
  27.2 0.7 collective-permute-start.9
  27.9 1.1 %shard_map.88 = (bf16[7,1024,1024]{2,1,0:T(8,128)(2,1)S(1)}, f32[8,1024,256]{2,1,0:T(8,128)S(1)}, f32[8,1024,128]{2,1,0:T(8,128)S(1)}, f32[8,128]{1,0:T(8,128)S(1)}) custom-call(f32[136,128]{1,0:T(8,128)S(1)} %get-tuple-element.155.refs_0_, ...), custom_call_target="tpu_custom_call", output_to_operand_aliasing={{0}: (1, {}), {1}: (2, {}), {2}: (3, {})} | custom-call | flops 536870912 | bytes 1048576 | tf_op jit(solution)/shard_map/pallas_call | solution.py:334
  29.1 0.5 collective-permute-done.8
  29.6 0.8 collective-permute-done.9
  30.6 5.4 %collective-permute-start.10 = (f32[4,136,128]{2,1,0:T(8,128)S(1)}, f32[4,136,128]{2,1,0:T(8,128)S(1)}, u32[]{:S(2)}, u32[]{:S(2)}) collective-permute-start(f32[4,136,128]{2,1,0:T(8,128)S(1)} %get-tuple-element.172), channel_id=1, source_target_pairs={{0,4},{4,0},{8,12},{12,8},{16,20},{20,16},{24,28},{28,24},{1,5},{5... | collective-permute-start | bytes 835592 | tf_op jit(solution)/shard_map/ppermute | solution.py:358
  36.1 1.3 %shard_map.89 = (bf16[7,1024,1024]{2,1,0:T(8,128)(2,1)S(1)}, f32[8,1024,256]{2,1,0:T(8,128)S(1)}, f32[8,1024,128]{2,1,0:T(8,128)S(1)}, f32[16,128]{1,0:T(8,128)S(1)}) custom-call(f32[1,1024]{1,0:T(1,128)S(1)} %bitcast.257, f32[4,136,128]{2,1,0:T(8,128)S(1)} %get-tuple-element.173.refs_1_.refs_2_, ...), custom_call_target="tpu_custom_call", output_to_operand_aliasing={{0}: (3, {}), {1}: (4, {}), {2}: (5, {})} | custom-call | flops 268435456 | bytes 1048576 | tf_op jit(solution)/shard_map/pallas_call | solution.py:334
  37.4 1.3 %shard_map.90 = (bf16[7,1024,1024]{2,1,0:T(8,128)(2,1)S(1)}, f32[8,1024,256]{2,1,0:T(8,128)S(1)}, f32[8,1024,128]{2,1,0:T(8,128)S(1)}, f32[16,128]{1,0:T(8,128)S(1)}) custom-call(f32[1,1024]{1,0:T(1,128)S(1)} %bitcast.258, f32[4,136,128]{2,1,0:T(8,128)S(1)} %collective-permute-done.10.refs_1_.refs_2_, ...), custom_call_target="tpu_custom_call", output_to_operand_aliasing={{0}: (3, {}), {1}: (4, {}), {2}: (5, {})} | custom-call | flops 268435456 | bytes 1048576 | tf_op jit(solution)/shard_map/pallas_call | solution.py:334
  38.8 3.7 %collective-permute-start.13 = (f32[16,128]{1,0:T(8,128)S(1)}, f32[16,128]{1,0:T(8,128)S(1)}, u32[]{:S(2)}, u32[]{:S(2)}) collective-permute-start(f32[16,128]{1,0:T(8,128)S(1)} %add.492.refs_1_), channel_id=1, source_target_pairs={{0,2},{1,3},{2,0},{3,1},{4,6},{5,7},{6,4},{7,5},{8,10},{9,11},{10,... | collective-permute-start | bytes 24584 | tf_op jit(solution)/shard_map/ppermute | solution.py:459
  42.4 0.4 collective-permute-start.12
  42.9 1.0 %collective-permute-start.11 = (f32[16,128]{1,0:T(8,128)S(1)}, f32[16,128]{1,0:T(8,128)S(1)}, u32[]{:S(2)}, u32[]{:S(2)}) collective-permute-start(f32[16,128]{1,0:T(8,128)S(1)} %add.492.refs_1_), channel_id=1, source_target_pairs={{0,1},{1,2},{2,3},{3,0},{4,5},{5,6},{6,7},{7,4},{8,9},{9,10},{10,1... | collective-permute-start | bytes 24584 | tf_op jit(solution)/shard_map/ppermute | solution.py:459
  43.9 2.8 %shard_map.91 = (bf16[7,1024,1024]{2,1,0:T(8,128)(2,1)S(1)}, f32[8,1024,256]{2,1,0:T(8,128)S(1)}, f32[8,1024,128]{2,1,0:T(8,128)S(1)}, f32[8,8,128]{2,1,0:T(8,128)S(1)}, f32[8,8,128]{2,1,0:T(8,128)S(1)}) custom-call(f32[1,1024]{1,0:T(1,128)S(1)} %bitcast.259, ...), custom_call_target="tpu_custom_call", output_to_operand_aliasing={{0}: (2, {}), {1}: (3, {}), {2}: (4, {})} | custom-call | flops 268435456 | bytes 1048576 | tf_op jit(solution)/shard_map/pallas_call | solution.py:334
  46.8 2.8 %shard_map.92 = (bf16[7,1024,1024]{2,1,0:T(8,128)(2,1)S(1)}, f32[8,1024,256]{2,1,0:T(8,128)S(1)}, f32[8,1024,128]{2,1,0:T(8,128)S(1)}, f32[8,136,128]{2,1,0:T(8,...) custom-call(f32[1,1024]{1,0:T(1,128)S(1)} %bitcast.260, ...), custom_call_target="tpu_custom_call", output_to_operand_aliasing={{0}: (4, {}), {1}: (5, {}), {2}: (6, {})} | custom-call | flops 536870912 | bytes 1048576 | tf_op jit(solution)/shard_map/pallas_call | solution.py:334
  49.6 0.1 add.498.refs_5_
  49.7 1.8 %collective-permute-start.14 = (f32[4,136,128]{2,1,0:T(8,128)S(1)}, f32[4,136,128]{2,1,0:T(8,128)S(1)}, u32[]{:S(2)}, u32[]{:S(2)}) collective-permute-start(f32[4,136,128]{2,1,0:T(8,128)S(1)} %slice.445), channel_id=1, source_target_pairs={{0,4},{4,0},{8,12},{12,8},{16,20},{20,16},{24,28},{28,24},{1,5},{5... | collective-permute-start | bytes 835592 | tf_op jit(solution)/shard_map/ppermute | solution.py:358
  51.5 3.4 %shard_map.93 = (bf16[7,1024,1024]{2,1,0:T(8,128)(2,1)S(1)}, f32[8,1024,256]{2,1,0:T(8,128)S(1)}, f32[8,1024,128]{2,1,0:T(8,128)S(1)}, bf16[1024,1024]{1,0:T(8,1...) custom-call(f32[1,1024]{1,0:T(1,128)S(1)} %bitcast.261, ...), custom_call_target="tpu_custom_call", output_to_operand_aliasing={{0}: (6, {}), {1}: (7, {}), {2}: (8, {})} | custom-call | flops 1073741824 | bytes 1048576 | tf_op jit(solution)/shard_map/pallas_call | solution.py:334
  55.1 0.4 collective-permute-start.15
  55.5 1.8 %collective-permute-start.16 = (f32[136,128]{1,0:T(8,128)S(1)}, f32[136,128]{1,0:T(8,128)S(1)}, u32[]{:S(2)}, u32[]{:S(2)}) collective-permute-start(f32[136,128]{1,0:T(8,128)S(1)} %get-tuple-element.171), channel_id=1, source_target_pairs={{0,8},{4,12},{8,16},{12,20},{16,24},{20,28},{24,0},{28,4},{1,9},{5... | collective-permute-start | bytes 208904 | tf_op jit(solution)/shard_map/ppermute | solution.py:350
  57.3 0.9 %collective-permute-start.17 = (f32[136,128]{1,0:T(8,128)S(1)}, f32[136,128]{1,0:T(8,128)S(1)}, u32[]{:S(2)}, u32[]{:S(2)}) collective-permute-start(f32[136,128]{1,0:T(8,128)S(1)} %get-tuple-element.169), channel_id=1, source_target_pairs={{0,24},{4,28},{8,0},{12,4},{16,8},{20,12},{24,16},{28,20},{1,25},{... | collective-permute-start | bytes 208904 | tf_op jit(solution)/shard_map/ppermute | solution.py:350
  58.2 3.4 %shard_map.94 = (bf16[7,1024,1024]{2,1,0:T(8,128)(2,1)S(1)}, f32[8,1024,256]{2,1,0:T(8,128)S(1)}, f32[8,1024,128]{2,1,0:T(8,128)S(1)}, bf16[1024,1024]{1,0:T(8,1...) custom-call(f32[1,1024]{1,0:T(1,128)S(1)} %bitcast.262, ...), custom_call_target="tpu_custom_call", output_to_operand_aliasing={{0}: (6, {}), {1}: (7, {}), {2}: (8, {}), {3}: (9, {}), {4}... | custom-call | flops 1073741824 | bytes 1048576 | tf_op jit(solution)/shard_map/pallas_call | solution.py:334
  61.6 0.7 collective-permute-done.16
  62.3 0.5 collective-permute-start.20
  62.8 0.1 collective-permute-start.19
  62.9 2.6 %collective-permute-start.18 = (f32[136,128]{1,0:T(8,128)S(1)}, f32[136,128]{1,0:T(8,128)S(1)}, u32[]{:S(2)}, u32[]{:S(2)}) collective-permute-start(f32[136,128]{1,0:T(8,128)S(1)} %add_add_fusion.7.refs_5_), channel_id=1, source_target_pairs={{0,96},{32,0},{64,32},{96,64},{1,97},{33,1},{65,33},{97,65},{2,98}... | collective-permute-start | bytes 208904 | tf_op jit(solution)/shard_map/ppermute | solution.py:354
  65.5 3.4 %shard_map.95 = (bf16[7,1024,1024]{2,1,0:T(8,128)(2,1)S(1)}, f32[8,1024,256]{2,1,0:T(8,128)S(1)}, f32[8,1024,128]{2,1,0:T(8,128)S(1)}, bf16[1024,1024]{1,0:T(8,1...) custom-call(f32[1,1024]{1,0:T(1,128)S(1)} %bitcast.263, ...), custom_call_target="tpu_custom_call", output_to_operand_aliasing={{0}: (6, {}), {1}: (7, {}), {2}: (8, {}), {3}: (9, {}), {4}... | custom-call | flops 1073741824 | bytes 1048576 | tf_op jit(solution)/shard_map/pallas_call | solution.py:334
  68.9 0.5 collective-permute-done.19
  69.4 0.4 collective-permute-start.21
  69.8 0.8 collective-permute-start.22
  70.6 1.9 %collective-permute-start.23 = (f32[136,128]{1,0:T(8,128)S(1)}, f32[136,128]{1,0:T(8,128)S(1)}, u32[]{:S(2)}, u32[]{:S(2)}) collective-permute-start(f32[136,128]{1,0:T(8,128)S(1)} %get-tuple-element.157), channel_id=1, source_target_pairs={{0,24},{4,28},{8,0},{12,4},{16,8},{20,12},{24,16},{28,20},{1,25},{... | collective-permute-start | bytes 208904 | tf_op jit(solution)/shard_map/ppermute | solution.py:350
  72.6 3.4 %shard_map.96 = (bf16[7,1024,1024]{2,1,0:T(8,128)(2,1)S(1)}, f32[8,1024,256]{2,1,0:T(8,128)S(1)}, f32[8,1024,128]{2,1,0:T(8,128)S(1)}, bf16[1024,1024]{1,0:T(8,1...) custom-call(f32[1,1024]{1,0:T(1,128)S(1)} %bitcast.264, ...), custom_call_target="tpu_custom_call", output_to_operand_aliasing={{0}: (6, {}), {1}: (7, {}), {2}: (8, {}), {3}: (9, {}), {4}... | custom-call | flops 1073741824 | bytes 1048576 | tf_op jit(solution)/shard_map/pallas_call | solution.py:334
  76.2 2.9 %collective-permute-start.24 = (f32[4,136,128]{2,1,0:T(8,128)S(1)}, f32[4,136,128]{2,1,0:T(8,128)S(1)}, u32[]{:S(2)}, u32[]{:S(2)}) collective-permute-start(f32[4,136,128]{2,1,0:T(8,128)S(1)} %get-tuple-element.167), channel_id=1, source_target_pairs={{0,4},{4,0},{8,12},{12,8},{16,20},{20,16},{24,28},{28,24},{1,5},{5... | collective-permute-start | bytes 835592 | tf_op jit(solution)/shard_map/ppermute | solution.py:358
  79.0 2.4 %shard_map.97 = (bf16[7,1024,1024]{2,1,0:T(8,128)(2,1)S(1)}, f32[8,1024,256]{2,1,0:T(8,128)S(1)}, f32[8,1024,128]{2,1,0:T(8,128)S(1)}, bf16[1024,1024]{1,0:T(8,128)(2,1)}, bf16[1024,1024]{1,0:T(8,128)(2,1)}) custom-call(f32[4,136,128]{2,1,0:T(8,128)S(1)} %get-tuple-element.166.refs_0_, ...), custom_call_target="tpu_custom_call", output_to_operand_aliasing={{0}: (2, {}), {1}: (3, {}), {2}: (4, {})} | custom-call | flops 268435456 | bytes 1048576 | tf_op jit(solution)/shard_map/pallas_call | solution.py:334
  81.4 2.4 %shard_map.98 = (bf16[7,1024,1024]{2,1,0:T(8,128)(2,1)S(1)}, f32[8,1024,256]{2,1,0:T(8,128)S(1)}, f32[8,1024,128]{2,1,0:T(8,128)S(1)}, bf16[1024,1024]{1,0:T(8,128)(2,1)}, bf16[1024,1024]{1,0:T(8,128)(2,1)}) custom-call(f32[4,136,128]{2,1,0:T(8,128)S(1)} %collective-permute-done.24.ref, ...), custom_call_target="tpu_custom_call", output_to_operand_aliasing={{0}: (2, {}), {1}: (3, {}), {2}: (4, {}), {3}: (5, {}), {4}... | custom-call | flops 268435456 | bytes 1048576 | tf_op jit(solution)/shard_map/pallas_call | solution.py:334
  (57 shorter events, 1.2 us)
Async XLA Ops:
  5.1 2.8 %collective-permute-start = (f32[4,136,128]{2,1,0:T(8,128)S(1)}, f32[4,136,128]{2,1,0:T(8,128)S(1)}, u32[]{:S(2)}, u32[]{:S(2)}) collective-permute-start(f32[4,136,128]{2,1,0:T(8,128)S(1)} %slice.437), channel_id=1, source_target_pairs={{0,4},{4,0},{8,12},{12,8},{16,20},{20,16},{24,28},{28,24},{1,5},{5... | collective-permute-start | bytes 835592 | tf_op jit(solution)/shard_map/ppermute | solution.py:358
  7.9 6.8 %collective-permute-start.1 = (f32[136,128]{1,0:T(8,128)S(1)}, f32[136,128]{1,0:T(8,128)S(1)}, u32[]{:S(2)}, u32[]{:S(2)}) collective-permute-start(f32[136,128]{1,0:T(8,128)S(1)} %get-tuple-element.176), channel_id=1, source_target_pairs={{0,16},{4,20},{8,24},{12,28},{16,0},{20,4},{24,8},{28,12},{1,17},{... | collective-permute-start | bytes 208904 | tf_op jit(solution)/shard_map/ppermute | solution.py:350
  10.8 4.4 %collective-permute-start.2 = (f32[136,128]{1,0:T(8,128)S(1)}, f32[136,128]{1,0:T(8,128)S(1)}, u32[]{:S(2)}, u32[]{:S(2)}) collective-permute-start(f32[136,128]{1,0:T(8,128)S(1)} %get-tuple-element.177), channel_id=1, source_target_pairs={{0,8},{4,12},{8,16},{12,20},{16,24},{20,28},{24,0},{28,4},{1,9},{5... | collective-permute-start | bytes 208904 | tf_op jit(solution)/shard_map/ppermute | solution.py:350
  11.2 4.0 %collective-permute-start.3 = (f32[136,128]{1,0:T(8,128)S(1)}, f32[136,128]{1,0:T(8,128)S(1)}, u32[]{:S(2)}, u32[]{:S(2)}) collective-permute-start(f32[136,128]{1,0:T(8,128)S(1)} %get-tuple-element.175), channel_id=1, source_target_pairs={{0,24},{4,28},{8,0},{12,4},{16,8},{20,12},{24,16},{28,20},{1,25},{... | collective-permute-start | bytes 208904 | tf_op jit(solution)/shard_map/ppermute | solution.py:350
  15.2 5.6 %collective-permute-start.6 = (f32[136,128]{1,0:T(8,128)S(1)}, f32[136,128]{1,0:T(8,128)S(1)}, u32[]{:S(2)}, u32[]{:S(2)}) collective-permute-start(f32[136,128]{1,0:T(8,128)S(1)} %add_add_fusion.13.refs_0_), channel_id=1, source_target_pairs={{0,64},{32,96},{64,0},{96,32},{1,65},{33,97},{65,1},{97,33},{2,66}... | collective-permute-start | bytes 208904 | tf_op jit(solution)/shard_map/ppermute | solution.py:354
  18.2 3.2 %collective-permute-start.5 = (f32[136,128]{1,0:T(8,128)S(1)}, f32[136,128]{1,0:T(8,128)S(1)}, u32[]{:S(2)}, u32[]{:S(2)}) collective-permute-start(f32[136,128]{1,0:T(8,128)S(1)} %add_add_fusion.13.refs_0_), channel_id=1, source_target_pairs={{0,96},{32,0},{64,32},{96,64},{1,97},{33,1},{65,33},{97,65},{2,98}... | collective-permute-start | bytes 208904 | tf_op jit(solution)/shard_map/ppermute | solution.py:354
  19.0 4.5 %collective-permute-start.4 = (f32[136,128]{1,0:T(8,128)S(1)}, f32[136,128]{1,0:T(8,128)S(1)}, u32[]{:S(2)}, u32[]{:S(2)}) collective-permute-start(f32[136,128]{1,0:T(8,128)S(1)} %add_add_fusion.13.refs_0_), channel_id=1, source_target_pairs={{0,32},{32,64},{64,96},{96,0},{1,33},{33,65},{65,97},{97,1},{2,34}... | collective-permute-start | bytes 208904 | tf_op jit(solution)/shard_map/ppermute | solution.py:354
  23.6 5.5 %collective-permute-start.7 = (f32[136,128]{1,0:T(8,128)S(1)}, f32[136,128]{1,0:T(8,128)S(1)}, u32[]{:S(2)}, u32[]{:S(2)}) collective-permute-start(f32[136,128]{1,0:T(8,128)S(1)} %get-tuple-element.154), channel_id=1, source_target_pairs={{0,16},{4,20},{8,24},{12,28},{16,0},{20,4},{24,8},{28,12},{1,17},{... | collective-permute-start | bytes 208904 | tf_op jit(solution)/shard_map/ppermute | solution.py:350
  25.1 4.4 %collective-permute-start.8 = (f32[136,128]{1,0:T(8,128)S(1)}, f32[136,128]{1,0:T(8,128)S(1)}, u32[]{:S(2)}, u32[]{:S(2)}) collective-permute-start(f32[136,128]{1,0:T(8,128)S(1)} %get-tuple-element.158), channel_id=1, source_target_pairs={{0,8},{4,12},{8,16},{12,20},{16,24},{20,28},{24,0},{28,4},{1,9},{5... | collective-permute-start | bytes 208904 | tf_op jit(solution)/shard_map/ppermute | solution.py:350
  27.2 3.2 %collective-permute-start.9 = (f32[136,128]{1,0:T(8,128)S(1)}, f32[136,128]{1,0:T(8,128)S(1)}, u32[]{:S(2)}, u32[]{:S(2)}) collective-permute-start(f32[136,128]{1,0:T(8,128)S(1)} %get-tuple-element.159), channel_id=1, source_target_pairs={{0,24},{4,28},{8,0},{12,4},{16,8},{20,12},{24,16},{28,20},{1,25},{... | collective-permute-start | bytes 208904 | tf_op jit(solution)/shard_map/ppermute | solution.py:350
  27.9 8.2 %copy-start = (f32[1024]{0:T(1024)S(1)}, f32[1024]{0:T(1024)}, u32[]{:S(2)}) copy-start(f32[1024]{0:T(1024)} %param.8) | copy-start | bytes 12292
  30.6 6.8 %collective-permute-start.10 = (f32[4,136,128]{2,1,0:T(8,128)S(1)}, f32[4,136,128]{2,1,0:T(8,128)S(1)}, u32[]{:S(2)}, u32[]{:S(2)}) collective-permute-start(f32[4,136,128]{2,1,0:T(8,128)S(1)} %get-tuple-element.172), channel_id=1, source_target_pairs={{0,4},{4,0},{8,12},{12,8},{16,20},{20,16},{24,28},{28,24},{1,5},{5... | collective-permute-start | bytes 835592 | tf_op jit(solution)/shard_map/ppermute | solution.py:358
  38.8 8.0 %collective-permute-start.13 = (f32[16,128]{1,0:T(8,128)S(1)}, f32[16,128]{1,0:T(8,128)S(1)}, u32[]{:S(2)}, u32[]{:S(2)}) collective-permute-start(f32[16,128]{1,0:T(8,128)S(1)} %add.492.refs_1_), channel_id=1, source_target_pairs={{0,2},{1,3},{2,0},{3,1},{4,6},{5,7},{6,4},{7,5},{8,10},{9,11},{10,... | collective-permute-start | bytes 24584 | tf_op jit(solution)/shard_map/ppermute | solution.py:459
  42.4 4.3 %collective-permute-start.12 = (f32[16,128]{1,0:T(8,128)S(1)}, f32[16,128]{1,0:T(8,128)S(1)}, u32[]{:S(2)}, u32[]{:S(2)}) collective-permute-start(f32[16,128]{1,0:T(8,128)S(1)} %add.492.refs_1_), channel_id=1, source_target_pairs={{0,3},{1,0},{2,1},{3,2},{4,7},{5,4},{6,5},{7,6},{8,11},{9,8},{10,9... | collective-permute-start | bytes 24584 | tf_op jit(solution)/shard_map/ppermute | solution.py:459
  42.9 3.9 %collective-permute-start.11 = (f32[16,128]{1,0:T(8,128)S(1)}, f32[16,128]{1,0:T(8,128)S(1)}, u32[]{:S(2)}, u32[]{:S(2)}) collective-permute-start(f32[16,128]{1,0:T(8,128)S(1)} %add.492.refs_1_), channel_id=1, source_target_pairs={{0,1},{1,2},{2,3},{3,0},{4,5},{5,6},{6,7},{7,4},{8,9},{9,10},{10,1... | collective-permute-start | bytes 24584 | tf_op jit(solution)/shard_map/ppermute | solution.py:459
  49.7 5.2 %collective-permute-start.14 = (f32[4,136,128]{2,1,0:T(8,128)S(1)}, f32[4,136,128]{2,1,0:T(8,128)S(1)}, u32[]{:S(2)}, u32[]{:S(2)}) collective-permute-start(f32[4,136,128]{2,1,0:T(8,128)S(1)} %slice.445), channel_id=1, source_target_pairs={{0,4},{4,0},{8,12},{12,8},{16,20},{20,16},{24,28},{28,24},{1,5},{5... | collective-permute-start | bytes 835592 | tf_op jit(solution)/shard_map/ppermute | solution.py:358
  55.1 6.5 %collective-permute-start.15 = (f32[136,128]{1,0:T(8,128)S(1)}, f32[136,128]{1,0:T(8,128)S(1)}, u32[]{:S(2)}, u32[]{:S(2)}) collective-permute-start(f32[136,128]{1,0:T(8,128)S(1)} %get-tuple-element.170), channel_id=1, source_target_pairs={{0,16},{4,20},{8,24},{12,28},{16,0},{20,4},{24,8},{28,12},{1,17},{... | collective-permute-start | bytes 208904 | tf_op jit(solution)/shard_map/ppermute | solution.py:350
  55.5 6.8 %collective-permute-start.16 = (f32[136,128]{1,0:T(8,128)S(1)}, f32[136,128]{1,0:T(8,128)S(1)}, u32[]{:S(2)}, u32[]{:S(2)}) collective-permute-start(f32[136,128]{1,0:T(8,128)S(1)} %get-tuple-element.171), channel_id=1, source_target_pairs={{0,8},{4,12},{8,16},{12,20},{16,24},{20,28},{24,0},{28,4},{1,9},{5... | collective-permute-start | bytes 208904 | tf_op jit(solution)/shard_map/ppermute | solution.py:350
  57.3 5.0 %collective-permute-start.17 = (f32[136,128]{1,0:T(8,128)S(1)}, f32[136,128]{1,0:T(8,128)S(1)}, u32[]{:S(2)}, u32[]{:S(2)}) collective-permute-start(f32[136,128]{1,0:T(8,128)S(1)} %get-tuple-element.169), channel_id=1, source_target_pairs={{0,24},{4,28},{8,0},{12,4},{16,8},{20,12},{24,16},{28,20},{1,25},{... | collective-permute-start | bytes 208904 | tf_op jit(solution)/shard_map/ppermute | solution.py:350
  62.3 6.5 %collective-permute-start.20 = (f32[136,128]{1,0:T(8,128)S(1)}, f32[136,128]{1,0:T(8,128)S(1)}, u32[]{:S(2)}, u32[]{:S(2)}) collective-permute-start(f32[136,128]{1,0:T(8,128)S(1)} %add_add_fusion.7.refs_5_), channel_id=1, source_target_pairs={{0,64},{32,96},{64,0},{96,32},{1,65},{33,97},{65,1},{97,33},{2,66}... | collective-permute-start | bytes 208904 | tf_op jit(solution)/shard_map/ppermute | solution.py:354
  62.8 6.5 %collective-permute-start.19 = (f32[136,128]{1,0:T(8,128)S(1)}, f32[136,128]{1,0:T(8,128)S(1)}, u32[]{:S(2)}, u32[]{:S(2)}) collective-permute-start(f32[136,128]{1,0:T(8,128)S(1)} %add_add_fusion.7.refs_5_), channel_id=1, source_target_pairs={{0,32},{32,64},{64,96},{96,0},{1,33},{33,65},{65,97},{97,1},{2,34}... | collective-permute-start | bytes 208904 | tf_op jit(solution)/shard_map/ppermute | solution.py:354
  62.9 6.4 %collective-permute-start.18 = (f32[136,128]{1,0:T(8,128)S(1)}, f32[136,128]{1,0:T(8,128)S(1)}, u32[]{:S(2)}, u32[]{:S(2)}) collective-permute-start(f32[136,128]{1,0:T(8,128)S(1)} %add_add_fusion.7.refs_5_), channel_id=1, source_target_pairs={{0,96},{32,0},{64,32},{96,64},{1,97},{33,1},{65,33},{97,65},{2,98}... | collective-permute-start | bytes 208904 | tf_op jit(solution)/shard_map/ppermute | solution.py:354
  69.4 6.6 %collective-permute-start.21 = (f32[136,128]{1,0:T(8,128)S(1)}, f32[136,128]{1,0:T(8,128)S(1)}, u32[]{:S(2)}, u32[]{:S(2)}) collective-permute-start(f32[136,128]{1,0:T(8,128)S(1)} %get-tuple-element.150), channel_id=1, source_target_pairs={{0,16},{4,20},{8,24},{12,28},{16,0},{20,4},{24,8},{28,12},{1,17},{... | collective-permute-start | bytes 208904 | tf_op jit(solution)/shard_map/ppermute | solution.py:350
  69.8 6.2 %collective-permute-start.22 = (f32[136,128]{1,0:T(8,128)S(1)}, f32[136,128]{1,0:T(8,128)S(1)}, u32[]{:S(2)}, u32[]{:S(2)}) collective-permute-start(f32[136,128]{1,0:T(8,128)S(1)} %get-tuple-element.156), channel_id=1, source_target_pairs={{0,8},{4,12},{8,16},{12,20},{16,24},{20,28},{24,0},{28,4},{1,9},{5... | collective-permute-start | bytes 208904 | tf_op jit(solution)/shard_map/ppermute | solution.py:350
  70.6 5.4 %collective-permute-start.23 = (f32[136,128]{1,0:T(8,128)S(1)}, f32[136,128]{1,0:T(8,128)S(1)}, u32[]{:S(2)}, u32[]{:S(2)}) collective-permute-start(f32[136,128]{1,0:T(8,128)S(1)} %get-tuple-element.157), channel_id=1, source_target_pairs={{0,24},{4,28},{8,0},{12,4},{16,8},{20,12},{24,16},{28,20},{1,25},{... | collective-permute-start | bytes 208904 | tf_op jit(solution)/shard_map/ppermute | solution.py:350
  76.2 5.2 %collective-permute-start.24 = (f32[4,136,128]{2,1,0:T(8,128)S(1)}, f32[4,136,128]{2,1,0:T(8,128)S(1)}, u32[]{:S(2)}, u32[]{:S(2)}) collective-permute-start(f32[4,136,128]{2,1,0:T(8,128)S(1)} %get-tuple-element.167), channel_id=1, source_target_pairs={{0,4},{4,0},{8,12},{12,8},{16,20},{20,16},{24,28},{28,24},{1,5},{5... | collective-permute-start | bytes 835592 | tf_op jit(solution)/shard_map/ppermute | solution.py:358

commit v2 on v1

--- a/solution.py
+++ b/solution.py
@@ -59,7 +59,7 @@
         body(j)
         return carry
 
-    lax.fori_loop(0, count, step, 0, unroll=UNROLL)
+    lax.fori_loop(0, count, step, 0, unroll=3 if count == 3 else UNROLL)
 
 
 def block_sums(fk, v):
@@ -69,7 +69,7 @@
 
 
 def sums_kernel(
-    keys_ref, values_ref, queries_ref, cotangent_ref, q_ref, k_ref, v_ref, ct_ref, fq_ref, fk_ref, nd_ref, gr_ref, g_ref, first_ref, last_ref, mask_ref, sems
+    keys_ref, values_ref, queries_ref, cotangent_ref, q_ref, k_ref, v_ref, ct_ref, fq_ref, fk_ref, nd_ref, gr_ref, wt_ref, g_ref, first_ref, last_ref, mask_ref, sems
 ):
     half = ROWS // 2
     near = pl.ds(pl.multiple_of(half * lax.rem(lax.axis_index("seqout"), 2), half), half)
@@ -106,9 +106,10 @@
         copy.wait()
 
 
-def intra_kernel(start, count, sent_ref, q_ref, k_ref, v_ref, ct_ref, fq_ref, fk_ref, nd_ref, gr_ref, g_ref, token_ref):
+def intra_kernel(start, count, sent_ref, q_ref, k_ref, v_ref, ct_ref, fq_ref, fk_ref, nd_ref, gr_ref, wt_ref, g_ref, token_ref):
     token_ref[...] = jnp.zeros_like(token_ref)
     tri = iota((HALF, HALF), 0) >= iota((HALF, HALF), 1)
+    up = iota((HALF, HALF), 0) <= iota((HALF, HALF), 1)
     ones = jnp.ones((BLOCK, E), BF16)
 
     def one(j):
@@ -118,6 +119,9 @@
             rows = pl.ds(b * BLOCK, BLOCK)
             fq, fk = phi(q_ref[rows, cols]), fk_ref[rows, cols]
             done.append((rows, fq))
+            wt_ref[start + j, b, pl.ds(0, HALF), :] = jnp.where(up, dot(fk[:HALF], fq[:HALF], 1, 1), 0.0).astype(BF16)
+            wt_ref[start + j, b, pl.ds(HALF, HALF), :] = dot(fk[:HALF], fq[HALF:], 1, 1).astype(BF16)
+            wt_ref[start + j, b, pl.ds(2 * HALF, HALF), :] = jnp.where(up, dot(fk[HALF:], fq[HALF:], 1, 1), 0.0).astype(BF16)
             va = jnp.concatenate([v_ref[rows, cols], ones], axis=1)
             w00 = jnp.where(tri, dot(fq[:HALF], fk[:HALF], 1, 1), 0.0).astype(BF16)
             w10 = dot(fq[HALF:], fk[:HALF], 1, 1).astype(BF16)
@@ -130,7 +134,7 @@
     each(count, one)
 
 
-def attn_kernel(start, count, gain_ref, st_ref, first_ref, q_ref, k_ref, v_ref, ct_ref, fq_ref, fk_ref, nd_ref, gr_ref, g_ref, sums_ref, sq_acc, pr_acc):
+def attn_kernel(start, count, gain_ref, st_ref, first_ref, q_ref, k_ref, v_ref, ct_ref, fq_ref, fk_ref, nd_ref, gr_ref, wt_ref, g_ref, sums_ref, sq_acc, pr_acc):
     sq_acc[...] = jnp.zeros_like(sq_acc)
     pr_acc[...] = jnp.zeros_like(pr_acc)
 
@@ -169,7 +173,7 @@
             coef_ref[rows, :] = column(sc_ref[pl.ds(8 + i, 1), :])
 
 
-def rows_kernel(gain_ref, sent_ref, q_ref, k_ref, v_ref, ct_ref, fq_ref, fk_ref, nd_ref, gr_ref, g_ref, p_ref, s_ref):
+def rows_kernel(gain_ref, sent_ref, q_ref, k_ref, v_ref, ct_ref, fq_ref, fk_ref, nd_ref, gr_ref, wt_ref, g_ref, p_ref, s_ref):
     ones = jnp.ones((8, 2 * E), BF16)
 
     def row_sums(x):
@@ -194,7 +198,7 @@
 
 
 def grad_kernel(
-    gain_ref, sc_ref, p_ref, s_ref, q_ref, k_ref, v_ref, ct_ref, fq_ref, fk_ref, nd_ref, gr_ref, g_ref, first_ref, last_ref, gd_ref, scale_ref, coef_ref
+    gain_ref, sc_ref, p_ref, s_ref, q_ref, k_ref, v_ref, ct_ref, fq_ref, fk_ref, nd_ref, gr_ref, wt_ref, g_ref, first_ref, last_ref, gd_ref, scale_ref, coef_ref
 ):
     spread(sc_ref, scale_ref, coef_ref)
 
@@ -222,13 +226,12 @@
 
 
 def back_kernel(
-    start, count, gain_ref, sc_ref, st_ref, first_ref, gd_ref, sent_ref, q_ref, k_ref, v_ref, ct_ref, fq_ref, fk_ref, nd_ref, gr_ref, g_ref,
+    start, count, gain_ref, sc_ref, st_ref, first_ref, gd_ref, sent_ref, q_ref, k_ref, v_ref, ct_ref, fq_ref, fk_ref, nd_ref, gr_ref, wt_ref, g_ref,
     dq_ref, mixed_ref, token_ref, scale_ref, dq_buf, mixed_buf, sems,
 ):
     token_ref[...] = jnp.zeros_like(token_ref)
     spread(sc_ref, scale_ref, None)
     low = iota((HALF, HALF), 0) >= iota((HALF, HALF), 1)
-    up = iota((HALF, HALF), 0) <= iota((HALF, HALF), 1)
 
     def copies(j):
         cols = columns(start + j)
@@ -248,11 +251,8 @@
             m00 = jnp.where(low, dot(g[:HALF], v[:HALF], 1, 1) + add0, 0.0).astype(BF16)
             m10 = (dot(g[HALF:], v[:HALF], 1, 1) + add1).astype(BF16)
             m11 = jnp.where(low, dot(g[HALF:], v[HALF:], 1, 1) + add1, 0.0).astype(BF16)
-            w00 = jnp.where(up, dot(fk[:HALF], fq[:HALF], 1, 1), 0.0).astype(BF16)
-            w10 = dot(fk[:HALF], fq[HALF:], 1, 1).astype(BF16)
-            w11 = jnp.where(up, dot(fk[HALF:], fq[HALF:], 1, 1), 0.0).astype(BF16)
-            at = start % 4 + j
-            aug = st_ref[at] + first_ref[start + j] if b else st_ref[at]
+            w00, w10, w11 = (wt_ref[start + j, b, pl.ds(i * HALF, HALF), :] for i in range(3))
+            aug = st_ref[start + j] + first_ref[start + j] if b else st_ref[start + j]
             s_hi, s_lo = split(aug[:E])
             rhs = jnp.concatenate([s_hi, s_lo], axis=1)
             dfq = dot(jnp.concatenate([g, g], axis=1), rhs, 1, 1) + gd * aug[E : E + 1]
@@ -272,7 +272,7 @@
             copy.wait()
 
 
-def last_kernel(start, count, lt_ref, last_ref, q_ref, k_ref, v_ref, ct_ref, fq_ref, fk_ref, nd_ref, gr_ref, g_ref, gk_ref, gv_ref, gk_buf, gv_buf, sems):
+def last_kernel(start, count, lt_ref, last_ref, q_ref, k_ref, v_ref, ct_ref, fq_ref, fk_ref, nd_ref, gr_ref, wt_ref, g_ref, gk_ref, gv_ref, gk_buf, gv_buf, sems):
 
     def copies(j):
         cols = columns(start + j)
@@ -328,8 +328,8 @@
             specs.append(pl.BlockSpec(memory_space=space))
 
     def body(*refs):
-        bank, nd, gr, *own = refs[len(arrays) :]
-        kernel(*refs[:first], *(bank.at[i] for i in range(6)), nd, gr, bank.at[6], *own)
+        bank, nd, gr, wt, *own = refs[len(arrays) :]
+        kernel(*refs[:first], *(bank.at[i] for i in range(6)), nd, gr, wt, bank.at[6], *own)
 
     return pl.pallas_call(
         body,
@@ -394,22 +394,22 @@
 
 def scan(sums, mask, reverse, during):
     other = swap(sums[4:])
-    total = sums[:4] + other + during[0](sums)
+    total = sums[:4] + other
     got = {k: add([keep_where(mask, TO + 4 * k + h, total[h]) for h in range(4)]) for k in (*ORDER, 0)}
     own = got[0]
     for k in ORDER:
         got[k] = send_x(got[k], k)
-    row = add([got[k] for k in USE]) + during[1](own)
+    row = add([got[k] for k in USE]) + during[0](own)
     rows = []
     for k in ROW_ORDER:
         came = send_y(row, -k if reverse else k)
         rows.append(keep_where(mask, (ROW_AFTER if reverse else ROW_BEFORE) + k, came))
-    base = rows[0] + rows[1] + rows[2] + during[2](row)
+    base = rows[0] + rows[1] + rows[2] + during[1](row)
     at = AFTER if reverse else BEFORE
     came = {k: base + add([keep_where(mask, at + 4 * k + m, got[m]) for m in USE]) for k in (*ORDER, 0)}
     for k in ORDER:
         came[k] = send_x(came[k], k)
-    zeros = during[3](base)
+    zeros = during[2](base)
     out = [add([keep_where(mask, SOURCE + 4 * k + h, came[k]) for k in USE]) + zeros for h in range(4)]
     return jnp.stack(out), other
 
@@ -423,6 +423,7 @@
     sems = pltpu.SemaphoreType.DMA
     kept = {}
     sizes = {"bank": ((7, ROWS, ROWS), BF16), "nd": ((8, ROWS, 2 * E), F32), "gr": ((8, ROWS, E), F32)}
+    sizes |= {"wt": ((8, 2, 3 * HALF, HALF), BF16)}
 
     def run(kernel, near, far, outs, scratch=(), flops=0):
         held = [vmem(*size, kept.get(name)) for name, size in sizes.items()]
@@ -443,7 +444,7 @@
 
         return during
 
-    st, other = scan(sums, mask, False, (intra(0, 2), intra(2, 2), intra(4, 2), intra(6, 2)))
+    st, other = scan(sums, mask, False, (intra(0, 3), intra(3, 3), intra(6, 2)))
     st_keep = st + keep_where(mask, UPPER, other)
     st_send = swap(st + keep_where(mask, LOWER, sums[:4]))
 
@@ -464,22 +465,22 @@
     back_first, back_last, gd = run(grad_kernel, [gain, sc, p, s], [], [parts, parts, per_head], (acc, acc), 1 << 29)
     back_sums = back_first + back_last
     dq = mixed = None
+    states = jnp.concatenate([st_keep, st_send])
 
     def back(start, count):
         def during(sent):
             nonlocal dq, mixed
-            state = st_send if start >= 4 else st_keep
             out = pltpu.VMEM((count, ROWS, E), BF16)
             dq, mixed, zeros = run(
                 functools.partial(back_kernel, start, count),
-                [gain, sc, state, first, gd], [sent], [hbm(shape, BF16, dq), hbm(shape, BF16, mixed), token],
+                [gain, sc, states, first, gd], [sent], [hbm(shape, BF16, dq), hbm(shape, BF16, mixed), token],
                 (acc, out, out, sems((2, count))), count << 29,
             )
             return zeros[:1]
 
         return during
 
-    lt, other = scan(back_sums, mask, True, (back(0, 2), back(2, 2), back(4, 2), back(6, 2)))
+    lt, other = scan(back_sums, mask, True, (back(0, 3), back(3, 3), back(6, 2)))
     lt_keep = lt + keep_where(mask, LOWER, other)
     lt_send = swap(lt + keep_where(mask, UPPER, back_sums[:4]))
     gk = gv = None

time: 84.1 us -> 83.1 us (0.988)
  waiting for transfers between devices: 5.58 us -> 4.47 us
    ppermute x4, waiting for transfers between devices: 0.01 us -> 2.23 us  [swap(): return lax.ppermute(x, 'seqout', CORE)]
    ppermute x6, waiting for transfers between devices: 3.11 us -> 1.36 us  [send_y(): return lax.ppermute(x, 'seqin', [(i, (i + k) % 4) for i in range(4)])]
    ppermute x12, waiting for transfers between devices: 2.43 us -> 0.86 us  [send_x(): return lax.ppermute(x, 'seqout', [(i, (i + 2 * k) % 8) for i in range(8)])]
    pallas_call x15 -> x13, Pallas kernels: 35.4 us -> 35 us  [call(): pl.pallas_call(body, out_shape=shapes, in_specs=specs, out_specs=out_spec...]
  transfers between devices with their start and end apart: 25 -> 25, of which waited for: 7 -> 5; matrix products, arithmetic and copies ran while one was open for 0% -> 0% of each run, Pallas kernels for 29% -> 29%
where the time goes in v2:
time: 83.1 us; the launch traced here: 83 us
  starting transfers between devices  41.1 us (49%)
  Pallas kernels  35 us (42%)
  waiting for transfers between devices  4.47 us (5%)
  between operations  1.24 us (1%)
  other arithmetic  1.15 us (1%)
    pallas_call x13, Pallas kernels, call(): pl.pallas_call(body, out_shape=shapes, in_specs=specs, out_specs=out_spec...  35 us
    ppermute x12, starting transfers between devices, send_x(): return lax.ppermute(x, 'seqout', [(i, (i + 2 * k) % 8) for i in range(8)])  16.6 us
    ppermute x4, starting transfers between devices, swap(): return lax.ppermute(x, 'seqout', CORE)  11.8 us
    ppermute x6, starting transfers between devices, send_y(): return lax.ppermute(x, 'seqin', [(i, (i + k) % 4) for i in range(4)])  7.62 us
    ppermute x3, starting transfers between devices, shards(): lax.ppermute(local, 'head', [(i, (i + k) % 4) for i in range(4)])  5.13 us
    ppermute x4, waiting for transfers between devices, swap(): return lax.ppermute(x, 'seqout', CORE)  2.23 us
  transfers between devices with their start and end apart: 25, of which 5 were waited for; matrix products, arithmetic and copies ran while one was open for 0% of the time, Pallas kernels for 29%

profile of v2, /device:TPU:1, one launch (start us, length us, event | category | flops | bytes accessed | tf_op | source)
XLA Modules:
  0.0 83.0 jit_solution(9802082119362626481)
XLA Ops:
  0.6 4.3 %shard_map.84 = (bf16[7,1024,1024]{2,1,0:T(8,128)(2,1)S(1)}, f32[8,1024,256]{2,1,0:T(8,128)S(1)}, f32[8,1024,128]{2,1,0:T(8,128)S(1)}, bf16[8,2,768,256]{3,2,1,0...) custom-call(bf16[1024,1024]{1,0:T(8,128)(2,1)} %refs_0_.1, ...), custom_call_target="tpu_custom_call" | custom-call | flops 268435456 | bytes 1048576 | tf_op jit(solution)/shard_map/pallas_call | solution.py:334
  5.0 1.5 %collective-permute-start = (f32[4,136,128]{2,1,0:T(8,128)S(1)}, f32[4,136,128]{2,1,0:T(8,128)S(1)}, u32[]{:S(2)}, u32[]{:S(2)}) collective-permute-start(f32[4,136,128]{2,1,0:T(8,128)S(1)} %slice.429), channel_id=1, source_target_pairs={{0,4},{4,0},{8,12},{12,8},{16,20},{20,16},{24,28},{28,24},{1,5},{5... | collective-permute-start | bytes 835592 | tf_op jit(solution)/shard_map/ppermute | solution.py:358
  6.6 1.1 %collective-permute-done = f32[4,136,128]{2,1,0:T(8,128)S(1)} collective-permute-done((f32[4,136,128]{2,1,0:T(8,128)S(1)}, f32[4,136,128]{2,1,0:T(8,128)S(1)}, u32[]{:S(2)}, u32[]{:S(2)}) %collective-permute-start) | collective-permute-done | bytes 278560 | tf_op jit(solution)/shard_map/ppermute | solution.py:358
  7.8 2.9 %collective-permute-start.1 = (f32[136,128]{1,0:T(8,128)S(1)}, f32[136,128]{1,0:T(8,128)S(1)}, u32[]{:S(2)}, u32[]{:S(2)}) collective-permute-start(f32[136,128]{1,0:T(8,128)S(1)} %get-tuple-element.180), channel_id=1, source_target_pairs={{0,16},{4,20},{8,24},{12,28},{16,0},{20,4},{24,8},{28,12},{1,17},{... | collective-permute-start | bytes 208904 | tf_op jit(solution)/shard_map/ppermute | solution.py:350
  10.7 0.3 collective-permute-start.2
  11.1 2.4 %collective-permute-start.3 = (f32[136,128]{1,0:T(8,128)S(1)}, f32[136,128]{1,0:T(8,128)S(1)}, u32[]{:S(2)}, u32[]{:S(2)}) collective-permute-start(f32[136,128]{1,0:T(8,128)S(1)} %get-tuple-element.179), channel_id=1, source_target_pairs={{0,24},{4,28},{8,0},{12,4},{16,8},{20,12},{24,16},{28,20},{1,25},{... | collective-permute-start | bytes 208904 | tf_op jit(solution)/shard_map/ppermute | solution.py:350
  13.5 2.3 %shard_map.85 = (bf16[7,1024,1024]{2,1,0:T(8,128)(2,1)S(1)}, f32[8,1024,256]{2,1,0:T(8,128)S(1)}, f32[8,1024,128]{2,1,0:T(8,128)S(1)}, bf16[8,2,768,256]{3,2,1,0:T(8,128)(2,1)S(1)}, f32[8,128]{1,0:T(8,128)S(1)}) custom-call(f32[136,128]{1,0:T(8,128)S(1)} %get-tuple-element.178.refs_0_, ...), custom_call_target="tpu_custom_call", output_to_operand_aliasing={{0}: (1, {}), {1}: (2, {}), {2}: (3, {}), {3}: (4, {})} | custom-call | flops 805306368 | bytes 1048576 | tf_op jit(solution)/shard_map/pallas_call | solution.py:334
  15.9 3.0 %collective-permute-start.6 = (f32[136,128]{1,0:T(8,128)S(1)}, f32[136,128]{1,0:T(8,128)S(1)}, u32[]{:S(2)}, u32[]{:S(2)}) collective-permute-start(f32[136,128]{1,0:T(8,128)S(1)} %add_add_fusion.11.refs_0_), channel_id=1, source_target_pairs={{0,64},{32,96},{64,0},{96,32},{1,65},{33,97},{65,1},{97,33},{2,66}... | collective-permute-start | bytes 208904 | tf_op jit(solution)/shard_map/ppermute | solution.py:354
  18.9 0.8 collective-permute-start.5
  19.7 0.7 collective-permute-start.4
  20.4 2.3 %shard_map.86 = (bf16[7,1024,1024]{2,1,0:T(8,128)(2,1)S(1)}, f32[8,1024,256]{2,1,0:T(8,128)S(1)}, f32[8,1024,128]{2,1,0:T(8,128)S(1)}, bf16[8,2,768,256]{3,2,1,0:T(8,128)(2,1)S(1)}, f32[8,128]{1,0:T(8,128)S(1)}) custom-call(f32[136,128]{1,0:T(8,128)S(1)} %add_add_fusion.11.refs_0_, ...), custom_call_target="tpu_custom_call", output_to_operand_aliasing={{0}: (1, {}), {1}: (2, {}), {2}: (3, {}), {3}: (4, {})} | custom-call | flops 805306368 | bytes 1048576 | tf_op jit(solution)/shard_map/pallas_call | solution.py:334
  22.7 1.3 %collective-permute-done.4 = f32[136,128]{1,0:T(8,128)S(1)} collective-permute-done((f32[136,128]{1,0:T(8,128)S(1)}, f32[136,128]{1,0:T(8,128)S(1)}, u32[]{:S(2)}, u32[]{:S(2)}) %collective-permute-start.4) | collective-permute-done | bytes 69664 | tf_op jit(solution)/shard_map/ppermute | solution.py:354
  24.1 0.9 %collective-permute-start.7 = (f32[136,128]{1,0:T(8,128)S(1)}, f32[136,128]{1,0:T(8,128)S(1)}, u32[]{:S(2)}, u32[]{:S(2)}) collective-permute-start(f32[136,128]{1,0:T(8,128)S(1)} %get-tuple-element.158), channel_id=1, source_target_pairs={{0,16},{4,20},{8,24},{12,28},{16,0},{20,4},{24,8},{28,12},{1,17},{... | collective-permute-start | bytes 208904 | tf_op jit(solution)/shard_map/ppermute | solution.py:350
  25.0 2.1 %collective-permute-start.8 = (f32[136,128]{1,0:T(8,128)S(1)}, f32[136,128]{1,0:T(8,128)S(1)}, u32[]{:S(2)}, u32[]{:S(2)}) collective-permute-start(f32[136,128]{1,0:T(8,128)S(1)} %get-tuple-element.162), channel_id=1, source_target_pairs={{0,8},{4,12},{8,16},{12,20},{16,24},{20,28},{24,0},{28,4},{1,9},{5... | collective-permute-start | bytes 208904 | tf_op jit(solution)/shard_map/ppermute | solution.py:350
  27.1 0.7 collective-permute-start.9
  27.8 1.6 %shard_map.87 = (bf16[7,1024,1024]{2,1,0:T(8,128)(2,1)S(1)}, f32[8,1024,256]{2,1,0:T(8,128)S(1)}, f32[8,1024,128]{2,1,0:T(8,128)S(1)}, bf16[8,2,768,256]{3,2,1,0:T(8,128)(2,1)S(1)}, f32[8,128]{1,0:T(8,128)S(1)}) custom-call(f32[136,128]{1,0:T(8,128)S(1)} %get-tuple-element.159.refs_0_, ...), custom_call_target="tpu_custom_call", output_to_operand_aliasing={{0}: (1, {}), {1}: (2, {}), {2}: (3, {}), {3}: (4, {})} | custom-call | flops 536870912 | bytes 1048576 | tf_op jit(solution)/shard_map/pallas_call | solution.py:334
  29.4 0.2 collective-permute-done.8
  29.6 0.7 collective-permute-done.9
  30.3 0.1 add_bitcast_fusion.7
  30.3 0.1 add_bitcast_fusion.6
  30.4 0.1 select_add_fusion.2
  30.5 5.4 %collective-permute-start.10 = (f32[4,136,128]{2,1,0:T(8,128)S(1)}, f32[4,136,128]{2,1,0:T(8,128)S(1)}, u32[]{:S(2)}, u32[]{:S(2)}) collective-permute-start(f32[4,136,128]{2,1,0:T(8,128)S(1)} %get-tuple-element.176), channel_id=1, source_target_pairs={{0,4},{4,0},{8,12},{12,8},{16,20},{20,16},{24,28},{28,24},{1,5},{5... | collective-permute-start | bytes 835592 | tf_op jit(solution)/shard_map/ppermute | solution.py:358
  35.8 1.3 %shard_map.88 = (bf16[7,1024,1024]{2,1,0:T(8,128)(2,1)S(1)}, f32[8,1024,256]{2,1,0:T(8,128)S(1)}, f32[8,1024,128]{2,1,0:T(8,128)S(1)}, bf16[8,2,768,256]{3,2,1,0:T(8,128)(2,1)S(1)}, f32[16,128]{1,0:T(8,128)S(1)}) custom-call(f32[1,1024]{1,0:T(1,128)S(1)} %bitcast.253, ...), custom_call_target="tpu_custom_call", output_to_operand_aliasing={{0}: (3, {}), {1}: (4, {}), {2}: (5, {}), {3}: (6, {})} | custom-call | flops 268435456 | bytes 1048576 | tf_op jit(solution)/shard_map/pallas_call | solution.py:334
  37.2 1.4 %shard_map.89 = (bf16[7,1024,1024]{2,1,0:T(8,128)(2,1)S(1)}, f32[8,1024,256]{2,1,0:T(8,128)S(1)}, f32[8,1024,128]{2,1,0:T(8,128)S(1)}, bf16[8,2,768,256]{3,2,1,0:T(8,128)(2,1)S(1)}, f32[16,128]{1,0:T(8,128)S(1)}) custom-call(f32[1,1024]{1,0:T(1,128)S(1)} %bitcast.254, ...), custom_call_target="tpu_custom_call", output_to_operand_aliasing={{0}: (3, {}), {1}: (4, {}), {2}: (5, {}), {3}: (6, {})} | custom-call | flops 268435456 | bytes 1048576 | tf_op jit(solution)/shard_map/pallas_call | solution.py:334
  38.5 3.7 %collective-permute-start.13 = (f32[16,128]{1,0:T(8,128)S(1)}, f32[16,128]{1,0:T(8,128)S(1)}, u32[]{:S(2)}, u32[]{:S(2)}) collective-permute-start(f32[16,128]{1,0:T(8,128)S(1)} %add.469.refs_1_), channel_id=1, source_target_pairs={{0,2},{1,3},{2,0},{3,1},{4,6},{5,7},{6,4},{7,5},{8,10},{9,11},{10,... | collective-permute-start | bytes 24584 | tf_op jit(solution)/shard_map/ppermute | solution.py:460
  42.2 0.4 collective-permute-start.12
  42.7 1.0 %collective-permute-start.11 = (f32[16,128]{1,0:T(8,128)S(1)}, f32[16,128]{1,0:T(8,128)S(1)}, u32[]{:S(2)}, u32[]{:S(2)}) collective-permute-start(f32[16,128]{1,0:T(8,128)S(1)} %add.469.refs_1_), channel_id=1, source_target_pairs={{0,1},{1,2},{2,3},{3,0},{4,5},{5,6},{6,7},{7,4},{8,9},{9,10},{10,1... | collective-permute-start | bytes 24584 | tf_op jit(solution)/shard_map/ppermute | solution.py:460
  43.7 2.8 %shard_map.90 = (bf16[7,1024,1024]{2,1,0:T(8,128)(2,1)S(1)}, f32[8,1024,256]{2,1,0:T(8,128)S(1)}, f32[8,1024,128]{2,1,0:T(8,128)S(1)}, bf16[8,2,768,256]{3,2,1,0...) custom-call(f32[1,1024]{1,0:T(1,128)S(1)} %bitcast.255, ...), custom_call_target="tpu_custom_call", output_to_operand_aliasing={{0}: (2, {}), {1}: (3, {}), {2}: (4, {}), {3}: (5, {})} | custom-call | flops 268435456 | bytes 1048576 | tf_op jit(solution)/shard_map/pallas_call | solution.py:334
  46.6 2.8 %shard_map.91 = (bf16[7,1024,1024]{2,1,0:T(8,128)(2,1)S(1)}, f32[8,1024,256]{2,1,0:T(8,128)S(1)}, f32[8,1024,128]{2,1,0:T(8,128)S(1)}, bf16[8,2,768,256]{3,2,1,0...) custom-call(f32[1,1024]{1,0:T(1,128)S(1)} %bitcast.256, ...), custom_call_target="tpu_custom_call", output_to_operand_aliasing={{0}: (4, {}), {1}: (5, {}), {2}: (6, {}), {3}: (7, {})} | custom-call | flops 536870912 | bytes 1048576 | tf_op jit(solution)/shard_map/pallas_call | solution.py:334
  49.5 1.8 %collective-permute-start.14 = (f32[4,136,128]{2,1,0:T(8,128)S(1)}, f32[4,136,128]{2,1,0:T(8,128)S(1)}, u32[]{:S(2)}, u32[]{:S(2)}) collective-permute-start(f32[4,136,128]{2,1,0:T(8,128)S(1)} %slice.437), channel_id=1, source_target_pairs={{0,4},{4,0},{8,12},{12,8},{16,20},{20,16},{24,28},{28,24},{1,5},{5... | collective-permute-start | bytes 835592 | tf_op jit(solution)/shard_map/ppermute | solution.py:358
  51.4 1.1 %collective-permute-done.14 = f32[4,136,128]{2,1,0:T(8,128)S(1)} collective-permute-done((f32[4,136,128]{2,1,0:T(8,128)S(1)}, f32[4,136,128]{2,1,0:T(8,128)S(1)}, u32[]{:S(2)}, u32[]{:S(2)}) %collective-permute-start.14) | collective-permute-done | bytes 278560 | tf_op jit(solution)/shard_map/ppermute | solution.py:358
  52.6 0.4 collective-permute-start.15
  53.0 1.8 %collective-permute-start.16 = (f32[136,128]{1,0:T(8,128)S(1)}, f32[136,128]{1,0:T(8,128)S(1)}, u32[]{:S(2)}, u32[]{:S(2)}) collective-permute-start(f32[136,128]{1,0:T(8,128)S(1)} %get-tuple-element.175), channel_id=1, source_target_pairs={{0,8},{4,12},{8,16},{12,20},{16,24},{20,28},{24,0},{28,4},{1,9},{5... | collective-permute-start | bytes 208904 | tf_op jit(solution)/shard_map/ppermute | solution.py:350
  54.8 0.9 %collective-permute-start.17 = (f32[136,128]{1,0:T(8,128)S(1)}, f32[136,128]{1,0:T(8,128)S(1)}, u32[]{:S(2)}, u32[]{:S(2)}) collective-permute-start(f32[136,128]{1,0:T(8,128)S(1)} %get-tuple-element.173), channel_id=1, source_target_pairs={{0,24},{4,28},{8,0},{12,4},{16,8},{20,12},{24,16},{28,20},{1,25},{... | collective-permute-start | bytes 208904 | tf_op jit(solution)/shard_map/ppermute | solution.py:350
  55.7 4.2 %shard_map.92 = (bf16[7,1024,1024]{2,1,0:T(8,128)(2,1)S(1)}, f32[8,1024,256]{2,1,0:T(8,128)S(1)}, f32[8,1024,128]{2,1,0:T(8,128)S(1)}, bf16[8,2,768,256]{3,2,1,0...) custom-call(f32[1,1024]{1,0:T(1,128)S(1)} %bitcast.257, ...), custom_call_target="tpu_custom_call", output_to_operand_aliasing={{0}: (6, {}), {1}: (7, {}), {2}: (8, {}), {3}: (9, {})} | custom-call | flops 1610612736 | bytes 1048576 | tf_op jit(solution)/shard_map/pallas_call | solution.py:334
  60.0 0.5 collective-permute-start.20
  60.5 0.2 collective-permute-start.19
  60.6 2.5 %collective-permute-start.18 = (f32[136,128]{1,0:T(8,128)S(1)}, f32[136,128]{1,0:T(8,128)S(1)}, u32[]{:S(2)}, u32[]{:S(2)}) collective-permute-start(f32[136,128]{1,0:T(8,128)S(1)} %add_add_fusion.5.refs_5_), channel_id=1, source_target_pairs={{0,96},{32,0},{64,32},{96,64},{1,97},{33,1},{65,33},{97,65},{2,98}... | collective-permute-start | bytes 208904 | tf_op jit(solution)/shard_map/ppermute | solution.py:354
  63.1 4.2 %shard_map.93 = (bf16[7,1024,1024]{2,1,0:T(8,128)(2,1)S(1)}, f32[8,1024,256]{2,1,0:T(8,128)S(1)}, f32[8,1024,128]{2,1,0:T(8,128)S(1)}, bf16[8,2,768,256]{3,2,1,0...) custom-call(f32[1,1024]{1,0:T(1,128)S(1)} %bitcast.258, ...), custom_call_target="tpu_custom_call", output_to_operand_aliasing={{0}: (6, {}), {1}: (7, {}), {2}: (8, {}), {3}: (9, {}), {4}... | custom-call | flops 1610612736 | bytes 1048576 | tf_op jit(solution)/shard_map/pallas_call | solution.py:334
  67.4 1.5 %collective-permute-start.21 = (f32[136,128]{1,0:T(8,128)S(1)}, f32[136,128]{1,0:T(8,128)S(1)}, u32[]{:S(2)}, u32[]{:S(2)}) collective-permute-start(f32[136,128]{1,0:T(8,128)S(1)} %get-tuple-element.154), channel_id=1, source_target_pairs={{0,16},{4,20},{8,24},{12,28},{16,0},{20,4},{24,8},{28,12},{1,17},{... | collective-permute-start | bytes 208904 | tf_op jit(solution)/shard_map/ppermute | solution.py:350
  69.0 0.1 collective-permute-start.22
  69.1 2.7 %collective-permute-start.23 = (f32[136,128]{1,0:T(8,128)S(1)}, f32[136,128]{1,0:T(8,128)S(1)}, u32[]{:S(2)}, u32[]{:S(2)}) collective-permute-start(f32[136,128]{1,0:T(8,128)S(1)} %get-tuple-element.161), channel_id=1, source_target_pairs={{0,24},{4,28},{8,0},{12,4},{16,8},{20,12},{24,16},{28,20},{1,25},{... | collective-permute-start | bytes 208904 | tf_op jit(solution)/shard_map/ppermute | solution.py:350
  71.7 3.0 %shard_map.94 = (bf16[7,1024,1024]{2,1,0:T(8,128)(2,1)S(1)}, f32[8,1024,256]{2,1,0:T(8,128)S(1)}, f32[8,1024,128]{2,1,0:T(8,128)S(1)}, bf16[8,2,768,256]{3,2,1,0...) custom-call(f32[1,1024]{1,0:T(1,128)S(1)} %bitcast.259, ...), custom_call_target="tpu_custom_call", output_to_operand_aliasing={{0}: (6, {}), {1}: (7, {}), {2}: (8, {}), {3}: (9, {}), {4}... | custom-call | flops 1073741824 | bytes 1048576 | tf_op jit(solution)/shard_map/pallas_call | solution.py:334
  74.8 0.1 add_bitcast_fusion.3
  74.8 0.1 add_bitcast_fusion.2
  75.0 3.1 %collective-permute-start.24 = (f32[4,136,128]{2,1,0:T(8,128)S(1)}, f32[4,136,128]{2,1,0:T(8,128)S(1)}, u32[]{:S(2)}, u32[]{:S(2)}) collective-permute-start(f32[4,136,128]{2,1,0:T(8,128)S(1)} %get-tuple-element.171), channel_id=1, source_target_pairs={{0,4},{4,0},{8,12},{12,8},{16,20},{20,16},{24,28},{28,24},{1,5},{5... | collective-permute-start | bytes 835592 | tf_op jit(solution)/shard_map/ppermute | solution.py:358
  78.1 2.3 %shard_map.95 = (bf16[7,1024,1024]{2,1,0:T(8,128)(2,1)S(1)}, f32[8,1024,256]{2,1,0:T(8,128)S(1)}, f32[8,1024,128]{2,1,0:T(8,128)S(1)}, bf16[8,2,768,256]{3,2,1,0...) custom-call(f32[4,136,128]{2,1,0:T(8,128)S(1)} %get-tuple-element.17, ...), custom_call_target="tpu_custom_call", output_to_operand_aliasing={{0}: (2, {}), {1}: (3, {}), {2}: (4, {}), {3}: (5, {})} | custom-call | flops 268435456 | bytes 1048576 | tf_op jit(solution)/shard_map/pallas_call | solution.py:334
  80.4 2.4 %shard_map.96 = (bf16[7,1024,1024]{2,1,0:T(8,128)(2,1)S(1)}, f32[8,1024,256]{2,1,0:T(8,128)S(1)}, f32[8,1024,128]{2,1,0:T(8,128)S(1)}, bf16[8,2,768,256]{3,2,1,0...) custom-call(f32[4,136,128]{2,1,0:T(8,128)S(1)} %collective-permute-d, ...), custom_call_target="tpu_custom_call", output_to_operand_aliasing={{0}: (2, {}), {1}: (3, {}), {2}: (4, {}), {3}: (5, {}), {4}... | custom-call | flops 268435456 | bytes 1048576 | tf_op jit(solution)/shard_map/pallas_call | solution.py:334
  (54 shorter events, 0.9 us)
Async XLA Ops:
  5.0 2.7 %collective-permute-start = (f32[4,136,128]{2,1,0:T(8,128)S(1)}, f32[4,136,128]{2,1,0:T(8,128)S(1)}, u32[]{:S(2)}, u32[]{:S(2)}) collective-permute-start(f32[4,136,128]{2,1,0:T(8,128)S(1)} %slice.429), channel_id=1, source_target_pairs={{0,4},{4,0},{8,12},{12,8},{16,20},{20,16},{24,28},{28,24},{1,5},{5... | collective-permute-start | bytes 835592 | tf_op jit(solution)/shard_map/ppermute | solution.py:358
  7.8 8.0 %collective-permute-start.1 = (f32[136,128]{1,0:T(8,128)S(1)}, f32[136,128]{1,0:T(8,128)S(1)}, u32[]{:S(2)}, u32[]{:S(2)}) collective-permute-start(f32[136,128]{1,0:T(8,128)S(1)} %get-tuple-element.180), channel_id=1, source_target_pairs={{0,16},{4,20},{8,24},{12,28},{16,0},{20,4},{24,8},{28,12},{1,17},{... | collective-permute-start | bytes 208904 | tf_op jit(solution)/shard_map/ppermute | solution.py:350
  10.7 5.1 %collective-permute-start.2 = (f32[136,128]{1,0:T(8,128)S(1)}, f32[136,128]{1,0:T(8,128)S(1)}, u32[]{:S(2)}, u32[]{:S(2)}) collective-permute-start(f32[136,128]{1,0:T(8,128)S(1)} %get-tuple-element.181), channel_id=1, source_target_pairs={{0,8},{4,12},{8,16},{12,20},{16,24},{20,28},{24,0},{28,4},{1,9},{5... | collective-permute-start | bytes 208904 | tf_op jit(solution)/shard_map/ppermute | solution.py:350
  11.1 4.8 %collective-permute-start.3 = (f32[136,128]{1,0:T(8,128)S(1)}, f32[136,128]{1,0:T(8,128)S(1)}, u32[]{:S(2)}, u32[]{:S(2)}) collective-permute-start(f32[136,128]{1,0:T(8,128)S(1)} %get-tuple-element.179), channel_id=1, source_target_pairs={{0,24},{4,28},{8,0},{12,4},{16,8},{20,12},{24,16},{28,20},{1,25},{... | collective-permute-start | bytes 208904 | tf_op jit(solution)/shard_map/ppermute | solution.py:350
  15.9 6.8 %collective-permute-start.6 = (f32[136,128]{1,0:T(8,128)S(1)}, f32[136,128]{1,0:T(8,128)S(1)}, u32[]{:S(2)}, u32[]{:S(2)}) collective-permute-start(f32[136,128]{1,0:T(8,128)S(1)} %add_add_fusion.11.refs_0_), channel_id=1, source_target_pairs={{0,64},{32,96},{64,0},{96,32},{1,65},{33,97},{65,1},{97,33},{2,66}... | collective-permute-start | bytes 208904 | tf_op jit(solution)/shard_map/ppermute | solution.py:354
  18.9 3.8 %collective-permute-start.5 = (f32[136,128]{1,0:T(8,128)S(1)}, f32[136,128]{1,0:T(8,128)S(1)}, u32[]{:S(2)}, u32[]{:S(2)}) collective-permute-start(f32[136,128]{1,0:T(8,128)S(1)} %add_add_fusion.11.refs_0_), channel_id=1, source_target_pairs={{0,96},{32,0},{64,32},{96,64},{1,97},{33,1},{65,33},{97,65},{2,98}... | collective-permute-start | bytes 208904 | tf_op jit(solution)/shard_map/ppermute | solution.py:354
  19.7 4.4 %collective-permute-start.4 = (f32[136,128]{1,0:T(8,128)S(1)}, f32[136,128]{1,0:T(8,128)S(1)}, u32[]{:S(2)}, u32[]{:S(2)}) collective-permute-start(f32[136,128]{1,0:T(8,128)S(1)} %add_add_fusion.11.refs_0_), channel_id=1, source_target_pairs={{0,32},{32,64},{64,96},{96,0},{1,33},{33,65},{65,97},{97,1},{2,34}... | collective-permute-start | bytes 208904 | tf_op jit(solution)/shard_map/ppermute | solution.py:354
  24.1 5.3 %collective-permute-start.7 = (f32[136,128]{1,0:T(8,128)S(1)}, f32[136,128]{1,0:T(8,128)S(1)}, u32[]{:S(2)}, u32[]{:S(2)}) collective-permute-start(f32[136,128]{1,0:T(8,128)S(1)} %get-tuple-element.158), channel_id=1, source_target_pairs={{0,16},{4,20},{8,24},{12,28},{16,0},{20,4},{24,8},{28,12},{1,17},{... | collective-permute-start | bytes 208904 | tf_op jit(solution)/shard_map/ppermute | solution.py:350
  25.0 4.6 %collective-permute-start.8 = (f32[136,128]{1,0:T(8,128)S(1)}, f32[136,128]{1,0:T(8,128)S(1)}, u32[]{:S(2)}, u32[]{:S(2)}) collective-permute-start(f32[136,128]{1,0:T(8,128)S(1)} %get-tuple-element.162), channel_id=1, source_target_pairs={{0,8},{4,12},{8,16},{12,20},{16,24},{20,28},{24,0},{28,4},{1,9},{5... | collective-permute-start | bytes 208904 | tf_op jit(solution)/shard_map/ppermute | solution.py:350
  27.1 3.2 %collective-permute-start.9 = (f32[136,128]{1,0:T(8,128)S(1)}, f32[136,128]{1,0:T(8,128)S(1)}, u32[]{:S(2)}, u32[]{:S(2)}) collective-permute-start(f32[136,128]{1,0:T(8,128)S(1)} %get-tuple-element.163), channel_id=1, source_target_pairs={{0,24},{4,28},{8,0},{12,4},{16,8},{20,12},{24,16},{28,20},{1,25},{... | collective-permute-start | bytes 208904 | tf_op jit(solution)/shard_map/ppermute | solution.py:350
  27.8 8.0 %copy-start = (f32[1024]{0:T(1024)S(1)}, f32[1024]{0:T(1024)}, u32[]{:S(2)}) copy-start(f32[1024]{0:T(1024)} %param.8) | copy-start | bytes 12292
  30.5 6.7 %collective-permute-start.10 = (f32[4,136,128]{2,1,0:T(8,128)S(1)}, f32[4,136,128]{2,1,0:T(8,128)S(1)}, u32[]{:S(2)}, u32[]{:S(2)}) collective-permute-start(f32[4,136,128]{2,1,0:T(8,128)S(1)} %get-tuple-element.176), channel_id=1, source_target_pairs={{0,4},{4,0},{8,12},{12,8},{16,20},{20,16},{24,28},{28,24},{1,5},{5... | collective-permute-start | bytes 835592 | tf_op jit(solution)/shard_map/ppermute | solution.py:358
  38.5 8.0 %collective-permute-start.13 = (f32[16,128]{1,0:T(8,128)S(1)}, f32[16,128]{1,0:T(8,128)S(1)}, u32[]{:S(2)}, u32[]{:S(2)}) collective-permute-start(f32[16,128]{1,0:T(8,128)S(1)} %add.469.refs_1_), channel_id=1, source_target_pairs={{0,2},{1,3},{2,0},{3,1},{4,6},{5,7},{6,4},{7,5},{8,10},{9,11},{10,... | collective-permute-start | bytes 24584 | tf_op jit(solution)/shard_map/ppermute | solution.py:460
  42.2 4.3 %collective-permute-start.12 = (f32[16,128]{1,0:T(8,128)S(1)}, f32[16,128]{1,0:T(8,128)S(1)}, u32[]{:S(2)}, u32[]{:S(2)}) collective-permute-start(f32[16,128]{1,0:T(8,128)S(1)} %add.469.refs_1_), channel_id=1, source_target_pairs={{0,3},{1,0},{2,1},{3,2},{4,7},{5,4},{6,5},{7,6},{8,11},{9,8},{10,9... | collective-permute-start | bytes 24584 | tf_op jit(solution)/shard_map/ppermute | solution.py:460
  42.7 3.9 %collective-permute-start.11 = (f32[16,128]{1,0:T(8,128)S(1)}, f32[16,128]{1,0:T(8,128)S(1)}, u32[]{:S(2)}, u32[]{:S(2)}) collective-permute-start(f32[16,128]{1,0:T(8,128)S(1)} %add.469.refs_1_), channel_id=1, source_target_pairs={{0,1},{1,2},{2,3},{3,0},{4,5},{5,6},{6,7},{7,4},{8,9},{9,10},{10,1... | collective-permute-start | bytes 24584 | tf_op jit(solution)/shard_map/ppermute | solution.py:460
  49.5 3.0 %collective-permute-start.14 = (f32[4,136,128]{2,1,0:T(8,128)S(1)}, f32[4,136,128]{2,1,0:T(8,128)S(1)}, u32[]{:S(2)}, u32[]{:S(2)}) collective-permute-start(f32[4,136,128]{2,1,0:T(8,128)S(1)} %slice.437), channel_id=1, source_target_pairs={{0,4},{4,0},{8,12},{12,8},{16,20},{20,16},{24,28},{28,24},{1,5},{5... | collective-permute-start | bytes 835592 | tf_op jit(solution)/shard_map/ppermute | solution.py:358
  52.6 7.3 %collective-permute-start.15 = (f32[136,128]{1,0:T(8,128)S(1)}, f32[136,128]{1,0:T(8,128)S(1)}, u32[]{:S(2)}, u32[]{:S(2)}) collective-permute-start(f32[136,128]{1,0:T(8,128)S(1)} %get-tuple-element.174), channel_id=1, source_target_pairs={{0,16},{4,20},{8,24},{12,28},{16,0},{20,4},{24,8},{28,12},{1,17},{... | collective-permute-start | bytes 208904 | tf_op jit(solution)/shard_map/ppermute | solution.py:350
  53.0 6.9 %collective-permute-start.16 = (f32[136,128]{1,0:T(8,128)S(1)}, f32[136,128]{1,0:T(8,128)S(1)}, u32[]{:S(2)}, u32[]{:S(2)}) collective-permute-start(f32[136,128]{1,0:T(8,128)S(1)} %get-tuple-element.175), channel_id=1, source_target_pairs={{0,8},{4,12},{8,16},{12,20},{16,24},{20,28},{24,0},{28,4},{1,9},{5... | collective-permute-start | bytes 208904 | tf_op jit(solution)/shard_map/ppermute | solution.py:350
  54.8 5.1 %collective-permute-start.17 = (f32[136,128]{1,0:T(8,128)S(1)}, f32[136,128]{1,0:T(8,128)S(1)}, u32[]{:S(2)}, u32[]{:S(2)}) collective-permute-start(f32[136,128]{1,0:T(8,128)S(1)} %get-tuple-element.173), channel_id=1, source_target_pairs={{0,24},{4,28},{8,0},{12,4},{16,8},{20,12},{24,16},{28,20},{1,25},{... | collective-permute-start | bytes 208904 | tf_op jit(solution)/shard_map/ppermute | solution.py:350
  60.0 7.4 %collective-permute-start.20 = (f32[136,128]{1,0:T(8,128)S(1)}, f32[136,128]{1,0:T(8,128)S(1)}, u32[]{:S(2)}, u32[]{:S(2)}) collective-permute-start(f32[136,128]{1,0:T(8,128)S(1)} %add_add_fusion.5.refs_5_), channel_id=1, source_target_pairs={{0,64},{32,96},{64,0},{96,32},{1,65},{33,97},{65,1},{97,33},{2,66}... | collective-permute-start | bytes 208904 | tf_op jit(solution)/shard_map/ppermute | solution.py:354
  60.5 6.9 %collective-permute-start.19 = (f32[136,128]{1,0:T(8,128)S(1)}, f32[136,128]{1,0:T(8,128)S(1)}, u32[]{:S(2)}, u32[]{:S(2)}) collective-permute-start(f32[136,128]{1,0:T(8,128)S(1)} %add_add_fusion.5.refs_5_), channel_id=1, source_target_pairs={{0,32},{32,64},{64,96},{96,0},{1,33},{33,65},{65,97},{97,1},{2,34}... | collective-permute-start | bytes 208904 | tf_op jit(solution)/shard_map/ppermute | solution.py:354
  60.6 6.7 %collective-permute-start.18 = (f32[136,128]{1,0:T(8,128)S(1)}, f32[136,128]{1,0:T(8,128)S(1)}, u32[]{:S(2)}, u32[]{:S(2)}) collective-permute-start(f32[136,128]{1,0:T(8,128)S(1)} %add_add_fusion.5.refs_5_), channel_id=1, source_target_pairs={{0,96},{32,0},{64,32},{96,64},{1,97},{33,1},{65,33},{97,65},{2,98}... | collective-permute-start | bytes 208904 | tf_op jit(solution)/shard_map/ppermute | solution.py:354
  67.4 7.3 %collective-permute-start.21 = (f32[136,128]{1,0:T(8,128)S(1)}, f32[136,128]{1,0:T(8,128)S(1)}, u32[]{:S(2)}, u32[]{:S(2)}) collective-permute-start(f32[136,128]{1,0:T(8,128)S(1)} %get-tuple-element.154), channel_id=1, source_target_pairs={{0,16},{4,20},{8,24},{12,28},{16,0},{20,4},{24,8},{28,12},{1,17},{... | collective-permute-start | bytes 208904 | tf_op jit(solution)/shard_map/ppermute | solution.py:350
  69.0 5.8 %collective-permute-start.22 = (f32[136,128]{1,0:T(8,128)S(1)}, f32[136,128]{1,0:T(8,128)S(1)}, u32[]{:S(2)}, u32[]{:S(2)}) collective-permute-start(f32[136,128]{1,0:T(8,128)S(1)} %get-tuple-element.160), channel_id=1, source_target_pairs={{0,8},{4,12},{8,16},{12,20},{16,24},{20,28},{24,0},{28,4},{1,9},{5... | collective-permute-start | bytes 208904 | tf_op jit(solution)/shard_map/ppermute | solution.py:350
  69.1 5.7 %collective-permute-start.23 = (f32[136,128]{1,0:T(8,128)S(1)}, f32[136,128]{1,0:T(8,128)S(1)}, u32[]{:S(2)}, u32[]{:S(2)}) collective-permute-start(f32[136,128]{1,0:T(8,128)S(1)} %get-tuple-element.161), channel_id=1, source_target_pairs={{0,24},{4,28},{8,0},{12,4},{16,8},{20,12},{24,16},{28,20},{1,25},{... | collective-permute-start | bytes 208904 | tf_op jit(solution)/shard_map/ppermute | solution.py:350
  75.0 5.5 %collective-permute-start.24 = (f32[4,136,128]{2,1,0:T(8,128)S(1)}, f32[4,136,128]{2,1,0:T(8,128)S(1)}, u32[]{:S(2)}, u32[]{:S(2)}) collective-permute-start(f32[4,136,128]{2,1,0:T(8,128)S(1)} %get-tuple-element.171), channel_id=1, source_target_pairs={{0,4},{4,0},{8,12},{12,8},{16,20},{20,16},{24,28},{28,24},{1,5},{5... | collective-permute-start | bytes 835592 | tf_op jit(solution)/shard_map/ppermute | solution.py:358

commit v3 on v2

--- a/solution.py
+++ b/solution.py
@@ -16,7 +16,7 @@
 F32 = jnp.float32
 BF16 = jnp.bfloat16
 VMEM_LIMIT = 16 * 1024 * 1024
-UNROLL = 2
+UNROLL = 4
 ORDER = (2, 1, 3)
 USE = (0, 2, 1, 3)
 ROW_ORDER = (1, 3, 2)
@@ -59,7 +59,7 @@
         body(j)
         return carry
 
-    lax.fori_loop(0, count, step, 0, unroll=3 if count == 3 else UNROLL)
+    lax.fori_loop(0, count, step, 0, unroll=3 if count == 3 else min(count, UNROLL))
 
 
 def block_sums(fk, v):
@@ -394,22 +394,22 @@
 
 def scan(sums, mask, reverse, during):
     other = swap(sums[4:])
-    total = sums[:4] + other
+    total = sums[:4] + other + during[0](sums)
     got = {k: add([keep_where(mask, TO + 4 * k + h, total[h]) for h in range(4)]) for k in (*ORDER, 0)}
     own = got[0]
     for k in ORDER:
         got[k] = send_x(got[k], k)
-    row = add([got[k] for k in USE]) + during[0](own)
+    row = add([got[k] for k in USE]) + during[1](own)
     rows = []
     for k in ROW_ORDER:
         came = send_y(row, -k if reverse else k)
         rows.append(keep_where(mask, (ROW_AFTER if reverse else ROW_BEFORE) + k, came))
-    base = rows[0] + rows[1] + rows[2] + during[1](row)
+    base = rows[0] + rows[1] + rows[2] + during[2](row)
     at = AFTER if reverse else BEFORE
     came = {k: base + add([keep_where(mask, at + 4 * k + m, got[m]) for m in USE]) for k in (*ORDER, 0)}
     for k in ORDER:
         came[k] = send_x(came[k], k)
-    zeros = during[2](base)
+    zeros = during[3](base)
     out = [add([keep_where(mask, SOURCE + 4 * k + h, came[k]) for k in USE]) + zeros for h in range(4)]
     return jnp.stack(out), other
 
@@ -444,7 +444,7 @@
 
         return during
 
-    st, other = scan(sums, mask, False, (intra(0, 3), intra(3, 3), intra(6, 2)))
+    st, other = scan(sums, mask, False, (intra(0, 2), intra(2, 2), intra(4, 2), intra(6, 2)))
     st_keep = st + keep_where(mask, UPPER, other)
     st_send = swap(st + keep_where(mask, LOWER, sums[:4]))
 
@@ -480,7 +480,7 @@
 
         return during
 
-    lt, other = scan(back_sums, mask, True, (back(0, 3), back(3, 3), back(6, 2)))
+    lt, other = scan(back_sums, mask, True, (back(0, 1), back(1, 2), back(3, 3), back(6, 2)))
     lt_keep = lt + keep_where(mask, LOWER, other)
     lt_send = swap(lt + keep_where(mask, UPPER, back_sums[:4]))
     gk = gv = None

time: 83.1 us -> 82.6 us (level)
    ppermute x4, waiting for transfers between devices: 2.23 us -> 0.01 us  [swap(): return lax.ppermute(x, 'seqout', CORE)]
    ppermute x12, waiting for transfers between devices: 0.86 us -> 1.88 us  [send_x(): return lax.ppermute(x, 'seqout', [(i, (i + 2 * k) % 8) for i in range(8)])]
    pallas_call x13 -> x15, Pallas kernels: 35 us -> 35.4 us  [call(): pl.pallas_call(body, out_shape=shapes, in_specs=specs, out_specs=out_spec...]
  transfers between devices with their start and end apart: 25 -> 25, of which waited for: 5 -> 6; matrix products, arithmetic and copies ran while one was open for 0% -> 0% of each run, Pallas kernels for 29% -> 30%
where the time goes in v3:
time: 82.6 us; the launch traced here: 82.5 us
  starting transfers between devices  40.6 us (49%)
  Pallas kernels  35.4 us (43%)
  waiting for transfers between devices  4.05 us (5%)
  between operations  1.25 us (2%)
  other arithmetic  1.19 us (1%)
    pallas_call x15, Pallas kernels, call(): pl.pallas_call(body, out_shape=shapes, in_specs=specs, out_specs=out_spec...  35.4 us
    ppermute x12, starting transfers between devices, send_x(): return lax.ppermute(x, 'seqout', [(i, (i + 2 * k) % 8) for i in range(8)])  16.3 us
    ppermute x4, starting transfers between devices, swap(): return lax.ppermute(x, 'seqout', CORE)  11.7 us
    ppermute x6, starting transfers between devices, send_y(): return lax.ppermute(x, 'seqin', [(i, (i + k) % 4) for i in range(4)])  7.43 us
    ppermute x3, starting transfers between devices, shards(): lax.ppermute(local, 'head', [(i, (i + k) % 4) for i in range(4)])  5.15 us
    ppermute x6, waiting for transfers between devices, send_y(): return lax.ppermute(x, 'seqin', [(i, (i + k) % 4) for i in range(4)])  2.06 us
    ppermute x12, waiting for transfers between devices, send_x(): return lax.ppermute(x, 'seqout', [(i, (i + 2 * k) % 8) for i in range(8)])  1.88 us
  transfers between devices with their start and end apart: 25, of which 6 were waited for; matrix products, arithmetic and copies ran while one was open for 0% of the time, Pallas kernels for 30%

profile of v3, /device:TPU:1, one launch (start us, length us, event | category | flops | bytes accessed | tf_op | source)
XLA Modules:
  0.0 82.5 jit_solution(17254504325103934659)
XLA Ops:
  0.6 4.3 %shard_map.84 = (bf16[7,1024,1024]{2,1,0:T(8,128)(2,1)S(1)}, f32[8,1024,256]{2,1,0:T(8,128)S(1)}, f32[8,1024,128]{2,1,0:T(8,128)S(1)}, bf16[8,2,768,256]{3,2,1,0...) custom-call(bf16[1024,1024]{1,0:T(8,128)(2,1)} %refs_0_.1, ...), custom_call_target="tpu_custom_call" | custom-call | flops 268435456 | bytes 1048576 | tf_op jit(solution)/shard_map/pallas_call | solution.py:334
  5.0 0.1 add.428.refs_0_
  5.1 1.5 %collective-permute-start = (f32[4,136,128]{2,1,0:T(8,128)S(1)}, f32[4,136,128]{2,1,0:T(8,128)S(1)}, u32[]{:S(2)}, u32[]{:S(2)}) collective-permute-start(f32[4,136,128]{2,1,0:T(8,128)S(1)} %slice.437), channel_id=1, source_target_pairs={{0,4},{4,0},{8,12},{12,8},{16,20},{20,16},{24,28},{28,24},{1,5},{5... | collective-permute-start | bytes 835592 | tf_op jit(solution)/shard_map/ppermute | solution.py:358
  6.6 1.6 %shard_map.85 = (bf16[7,1024,1024]{2,1,0:T(8,128)(2,1)S(1)}, f32[8,1024,256]{2,1,0:T(8,128)S(1)}, f32[8,1024,128]{2,1,0:T(8,128)S(1)}, bf16[8,2,768,256]{3,2,1,0:T(8,128)(2,1)S(1)}, f32[8,128]{1,0:T(8,128)S(1)}) custom-call(f32[8,136,128]{2,1,0:T(8,128)S(1)} %add.428.refs_0_, ...), custom_call_target="tpu_custom_call", output_to_operand_aliasing={{0}: (1, {}), {1}: (2, {}), {2}: (3, {}), {3}: (4, {})} | custom-call | flops 536870912 | bytes 1048576 | tf_op jit(solution)/shard_map/pallas_call | solution.py:334
  8.4 2.9 %collective-permute-start.1 = (f32[136,128]{1,0:T(8,128)S(1)}, f32[136,128]{1,0:T(8,128)S(1)}, u32[]{:S(2)}, u32[]{:S(2)}) collective-permute-start(f32[136,128]{1,0:T(8,128)S(1)} %get-tuple-element.204), channel_id=1, source_target_pairs={{0,16},{4,20},{8,24},{12,28},{16,0},{20,4},{24,8},{28,12},{1,17},{... | collective-permute-start | bytes 208904 | tf_op jit(solution)/shard_map/ppermute | solution.py:350
  11.3 0.3 collective-permute-start.2
  11.7 2.4 %collective-permute-start.3 = (f32[136,128]{1,0:T(8,128)S(1)}, f32[136,128]{1,0:T(8,128)S(1)}, u32[]{:S(2)}, u32[]{:S(2)}) collective-permute-start(f32[136,128]{1,0:T(8,128)S(1)} %get-tuple-element.203), channel_id=1, source_target_pairs={{0,24},{4,28},{8,0},{12,4},{16,8},{20,12},{24,16},{28,20},{1,25},{... | collective-permute-start | bytes 208904 | tf_op jit(solution)/shard_map/ppermute | solution.py:350
  14.1 1.6 %shard_map.86 = (bf16[7,1024,1024]{2,1,0:T(8,128)(2,1)S(1)}, f32[8,1024,256]{2,1,0:T(8,128)S(1)}, f32[8,1024,128]{2,1,0:T(8,128)S(1)}, bf16[8,2,768,256]{3,2,1,0:T(8,128)(2,1)S(1)}, f32[8,128]{1,0:T(8,128)S(1)}) custom-call(f32[136,128]{1,0:T(8,128)S(1)} %get-tuple-element.202.refs_0_, ...), custom_call_target="tpu_custom_call", output_to_operand_aliasing={{0}: (1, {}), {1}: (2, {}), {2}: (3, {}), {3}: (4, {})} | custom-call | flops 536870912 | bytes 1048576 | tf_op jit(solution)/shard_map/pallas_call | solution.py:334
  15.8 3.0 %collective-permute-start.6 = (f32[136,128]{1,0:T(8,128)S(1)}, f32[136,128]{1,0:T(8,128)S(1)}, u32[]{:S(2)}, u32[]{:S(2)}) collective-permute-start(f32[136,128]{1,0:T(8,128)S(1)} %add_add_fusion.13.refs_0_), channel_id=1, source_target_pairs={{0,64},{32,96},{64,0},{96,32},{1,65},{33,97},{65,1},{97,33},{2,66}... | collective-permute-start | bytes 208904 | tf_op jit(solution)/shard_map/ppermute | solution.py:354
  18.8 0.8 collective-permute-start.5
  19.5 0.7 collective-permute-start.4
  20.2 1.6 %shard_map.87 = (bf16[7,1024,1024]{2,1,0:T(8,128)(2,1)S(1)}, f32[8,1024,256]{2,1,0:T(8,128)S(1)}, f32[8,1024,128]{2,1,0:T(8,128)S(1)}, bf16[8,2,768,256]{3,2,1,0:T(8,128)(2,1)S(1)}, f32[8,128]{1,0:T(8,128)S(1)}) custom-call(f32[136,128]{1,0:T(8,128)S(1)} %add_add_fusion.13.refs_0_, ...), custom_call_target="tpu_custom_call", output_to_operand_aliasing={{0}: (1, {}), {1}: (2, {}), {2}: (3, {}), {3}: (4, {})} | custom-call | flops 536870912 | bytes 1048576 | tf_op jit(solution)/shard_map/pallas_call | solution.py:334
  21.9 0.4 collective-permute-done.5
  22.2 1.7 %collective-permute-done.4 = f32[136,128]{1,0:T(8,128)S(1)} collective-permute-done((f32[136,128]{1,0:T(8,128)S(1)}, f32[136,128]{1,0:T(8,128)S(1)}, u32[]{:S(2)}, u32[]{:S(2)}) %collective-permute-start.4) | collective-permute-done | bytes 69664 | tf_op jit(solution)/shard_map/ppermute | solution.py:354
  24.0 1.6 %collective-permute-start.7 = (f32[136,128]{1,0:T(8,128)S(1)}, f32[136,128]{1,0:T(8,128)S(1)}, u32[]{:S(2)}, u32[]{:S(2)}) collective-permute-start(f32[136,128]{1,0:T(8,128)S(1)} %get-tuple-element.182), channel_id=1, source_target_pairs={{0,16},{4,20},{8,24},{12,28},{16,0},{20,4},{24,8},{28,12},{1,17},{... | collective-permute-start | bytes 208904 | tf_op jit(solution)/shard_map/ppermute | solution.py:350
  25.6 2.0 %collective-permute-start.8 = (f32[136,128]{1,0:T(8,128)S(1)}, f32[136,128]{1,0:T(8,128)S(1)}, u32[]{:S(2)}, u32[]{:S(2)}) collective-permute-start(f32[136,128]{1,0:T(8,128)S(1)} %get-tuple-element.186), channel_id=1, source_target_pairs={{0,8},{4,12},{8,16},{12,20},{16,24},{20,28},{24,0},{28,4},{1,9},{5... | collective-permute-start | bytes 208904 | tf_op jit(solution)/shard_map/ppermute | solution.py:350
  27.6 0.8 collective-permute-start.9
  28.4 1.6 %shard_map.88 = (bf16[7,1024,1024]{2,1,0:T(8,128)(2,1)S(1)}, f32[8,1024,256]{2,1,0:T(8,128)S(1)}, f32[8,1024,128]{2,1,0:T(8,128)S(1)}, bf16[8,2,768,256]{3,2,1,0:T(8,128)(2,1)S(1)}, f32[8,128]{1,0:T(8,128)S(1)}) custom-call(f32[136,128]{1,0:T(8,128)S(1)} %get-tuple-element.183.refs_0_, ...), custom_call_target="tpu_custom_call", output_to_operand_aliasing={{0}: (1, {}), {1}: (2, {}), {2}: (3, {}), {3}: (4, {})} | custom-call | flops 536870912 | bytes 1048576 | tf_op jit(solution)/shard_map/pallas_call | solution.py:334
  30.1 0.7 collective-permute-done.9
  30.8 0.1 add_bitcast_fusion.6
  31.0 5.1 %collective-permute-start.10 = (f32[4,136,128]{2,1,0:T(8,128)S(1)}, f32[4,136,128]{2,1,0:T(8,128)S(1)}, u32[]{:S(2)}, u32[]{:S(2)}) collective-permute-start(f32[4,136,128]{2,1,0:T(8,128)S(1)} %get-tuple-element.200), channel_id=1, source_target_pairs={{0,4},{4,0},{8,12},{12,8},{16,20},{20,16},{24,28},{28,24},{1,5},{5... | collective-permute-start | bytes 835592 | tf_op jit(solution)/shard_map/ppermute | solution.py:358
  36.1 1.3 %shard_map.89 = (bf16[7,1024,1024]{2,1,0:T(8,128)(2,1)S(1)}, f32[8,1024,256]{2,1,0:T(8,128)S(1)}, f32[8,1024,128]{2,1,0:T(8,128)S(1)}, bf16[8,2,768,256]{3,2,1,0:T(8,128)(2,1)S(1)}, f32[16,128]{1,0:T(8,128)S(1)}) custom-call(f32[1,1024]{1,0:T(1,128)S(1)} %bitcast.257, ...), custom_call_target="tpu_custom_call", output_to_operand_aliasing={{0}: (3, {}), {1}: (4, {}), {2}: (5, {}), {3}: (6, {})} | custom-call | flops 268435456 | bytes 1048576 | tf_op jit(solution)/shard_map/pallas_call | solution.py:334
  37.4 1.3 %shard_map.90 = (bf16[7,1024,1024]{2,1,0:T(8,128)(2,1)S(1)}, f32[8,1024,256]{2,1,0:T(8,128)S(1)}, f32[8,1024,128]{2,1,0:T(8,128)S(1)}, bf16[8,2,768,256]{3,2,1,0:T(8,128)(2,1)S(1)}, f32[16,128]{1,0:T(8,128)S(1)}) custom-call(f32[1,1024]{1,0:T(1,128)S(1)} %bitcast.258, ...), custom_call_target="tpu_custom_call", output_to_operand_aliasing={{0}: (3, {}), {1}: (4, {}), {2}: (5, {}), {3}: (6, {})} | custom-call | flops 268435456 | bytes 1048576 | tf_op jit(solution)/shard_map/pallas_call | solution.py:334
  38.8 3.7 %collective-permute-start.13 = (f32[16,128]{1,0:T(8,128)S(1)}, f32[16,128]{1,0:T(8,128)S(1)}, u32[]{:S(2)}, u32[]{:S(2)}) collective-permute-start(f32[16,128]{1,0:T(8,128)S(1)} %add.492.refs_1_), channel_id=1, source_target_pairs={{0,2},{1,3},{2,0},{3,1},{4,6},{5,7},{6,4},{7,5},{8,10},{9,11},{10,... | collective-permute-start | bytes 24584 | tf_op jit(solution)/shard_map/ppermute | solution.py:460
  42.5 0.4 collective-permute-start.12
  42.9 1.0 %collective-permute-start.11 = (f32[16,128]{1,0:T(8,128)S(1)}, f32[16,128]{1,0:T(8,128)S(1)}, u32[]{:S(2)}, u32[]{:S(2)}) collective-permute-start(f32[16,128]{1,0:T(8,128)S(1)} %add.492.refs_1_), channel_id=1, source_target_pairs={{0,1},{1,2},{2,3},{3,0},{4,5},{5,6},{6,7},{7,4},{8,9},{9,10},{10,1... | collective-permute-start | bytes 24584 | tf_op jit(solution)/shard_map/ppermute | solution.py:460
  43.9 2.6 %shard_map.91 = (bf16[7,1024,1024]{2,1,0:T(8,128)(2,1)S(1)}, f32[8,1024,256]{2,1,0:T(8,128)S(1)}, f32[8,1024,128]{2,1,0:T(8,128)S(1)}, bf16[8,2,768,256]{3,2,1,0...) custom-call(f32[1,1024]{1,0:T(1,128)S(1)} %bitcast.259, ...), custom_call_target="tpu_custom_call", output_to_operand_aliasing={{0}: (2, {}), {1}: (3, {}), {2}: (4, {}), {3}: (5, {})} | custom-call | flops 268435456 | bytes 1048576 | tf_op jit(solution)/shard_map/pallas_call | solution.py:334
  46.5 0.1 collective-permute-done.11
  46.6 2.6 %shard_map.92 = (bf16[7,1024,1024]{2,1,0:T(8,128)(2,1)S(1)}, f32[8,1024,256]{2,1,0:T(8,128)S(1)}, f32[8,1024,128]{2,1,0:T(8,128)S(1)}, bf16[8,2,768,256]{3,2,1,0...) custom-call(f32[1,1024]{1,0:T(1,128)S(1)} %bitcast.260, ...), custom_call_target="tpu_custom_call", output_to_operand_aliasing={{0}: (4, {}), {1}: (5, {}), {2}: (6, {}), {3}: (7, {})} | custom-call | flops 536870912 | bytes 1048576 | tf_op jit(solution)/shard_map/pallas_call | solution.py:334
  49.3 2.0 %collective-permute-start.14 = (f32[4,136,128]{2,1,0:T(8,128)S(1)}, f32[4,136,128]{2,1,0:T(8,128)S(1)}, u32[]{:S(2)}, u32[]{:S(2)}) collective-permute-start(f32[4,136,128]{2,1,0:T(8,128)S(1)} %slice.445), channel_id=1, source_target_pairs={{0,4},{4,0},{8,12},{12,8},{16,20},{20,16},{24,28},{28,24},{1,5},{5... | collective-permute-start | bytes 835592 | tf_op jit(solution)/shard_map/ppermute | solution.py:358
  51.4 1.9 %shard_map.93 = (bf16[7,1024,1024]{2,1,0:T(8,128)(2,1)S(1)}, f32[8,1024,256]{2,1,0:T(8,128)S(1)}, f32[8,1024,128]{2,1,0:T(8,128)S(1)}, bf16[8,2,768,256]{3,2,1,0...) custom-call(f32[1,1024]{1,0:T(1,128)S(1)} %bitcast.261, ...), custom_call_target="tpu_custom_call", output_to_operand_aliasing={{0}: (6, {}), {1}: (7, {}), {2}: (8, {}), {3}: (9, {})} | custom-call | flops 536870912 | bytes 1048576 | tf_op jit(solution)/shard_map/pallas_call | solution.py:334
  53.5 0.4 collective-permute-start.15
  53.9 1.8 %collective-permute-start.16 = (f32[136,128]{1,0:T(8,128)S(1)}, f32[136,128]{1,0:T(8,128)S(1)}, u32[]{:S(2)}, u32[]{:S(2)}) collective-permute-start(f32[136,128]{1,0:T(8,128)S(1)} %get-tuple-element.199), channel_id=1, source_target_pairs={{0,8},{4,12},{8,16},{12,20},{16,24},{20,28},{24,0},{28,4},{1,9},{5... | collective-permute-start | bytes 208904 | tf_op jit(solution)/shard_map/ppermute | solution.py:350
  55.7 0.9 %collective-permute-start.17 = (f32[136,128]{1,0:T(8,128)S(1)}, f32[136,128]{1,0:T(8,128)S(1)}, u32[]{:S(2)}, u32[]{:S(2)}) collective-permute-start(f32[136,128]{1,0:T(8,128)S(1)} %get-tuple-element.197), channel_id=1, source_target_pairs={{0,24},{4,28},{8,0},{12,4},{16,8},{20,12},{24,16},{28,20},{1,25},{... | collective-permute-start | bytes 208904 | tf_op jit(solution)/shard_map/ppermute | solution.py:350
  56.5 3.0 %shard_map.94 = (bf16[7,1024,1024]{2,1,0:T(8,128)(2,1)S(1)}, f32[8,1024,256]{2,1,0:T(8,128)S(1)}, f32[8,1024,128]{2,1,0:T(8,128)S(1)}, bf16[8,2,768,256]{3,2,1,0...) custom-call(f32[1,1024]{1,0:T(1,128)S(1)} %bitcast.262, ...), custom_call_target="tpu_custom_call", output_to_operand_aliasing={{0}: (6, {}), {1}: (7, {}), {2}: (8, {}), {3}: (9, {}), {4}... | custom-call | flops 1073741824 | bytes 1048576 | tf_op jit(solution)/shard_map/pallas_call | solution.py:334
  59.6 1.1 %collective-permute-done.16 = f32[136,128]{1,0:T(8,128)S(1)} collective-permute-done((f32[136,128]{1,0:T(8,128)S(1)}, f32[136,128]{1,0:T(8,128)S(1)}, u32[]{:S(2)}, u32[]{:S(2)}) %collective-permute-start.16) | collective-permute-done | bytes 69664 | tf_op jit(solution)/shard_map/ppermute | solution.py:350
  60.7 0.3 collective-permute-start.20
  61.0 0.1 collective-permute-start.19
  61.1 2.6 %collective-permute-start.18 = (f32[136,128]{1,0:T(8,128)S(1)}, f32[136,128]{1,0:T(8,128)S(1)}, u32[]{:S(2)}, u32[]{:S(2)}) collective-permute-start(f32[136,128]{1,0:T(8,128)S(1)} %add_add_fusion.7.refs_5_), channel_id=1, source_target_pairs={{0,96},{32,0},{64,32},{96,64},{1,97},{33,1},{65,33},{97,65},{2,98}... | collective-permute-start | bytes 208904 | tf_op jit(solution)/shard_map/ppermute | solution.py:354
  63.7 4.2 %shard_map.95 = (bf16[7,1024,1024]{2,1,0:T(8,128)(2,1)S(1)}, f32[8,1024,256]{2,1,0:T(8,128)S(1)}, f32[8,1024,128]{2,1,0:T(8,128)S(1)}, bf16[8,2,768,256]{3,2,1,0...) custom-call(f32[1,1024]{1,0:T(1,128)S(1)} %bitcast.263, ...), custom_call_target="tpu_custom_call", output_to_operand_aliasing={{0}: (6, {}), {1}: (7, {}), {2}: (8, {}), {3}: (9, {}), {4}... | custom-call | flops 1610612736 | bytes 1048576 | tf_op jit(solution)/shard_map/pallas_call | solution.py:334
  67.9 0.4 collective-permute-start.21
  68.4 1.4 %collective-permute-start.22 = (f32[136,128]{1,0:T(8,128)S(1)}, f32[136,128]{1,0:T(8,128)S(1)}, u32[]{:S(2)}, u32[]{:S(2)}) collective-permute-start(f32[136,128]{1,0:T(8,128)S(1)} %get-tuple-element.184), channel_id=1, source_target_pairs={{0,8},{4,12},{8,16},{12,20},{16,24},{20,28},{24,0},{28,4},{1,9},{5... | collective-permute-start | bytes 208904 | tf_op jit(solution)/shard_map/ppermute | solution.py:350
  69.8 1.3 %collective-permute-start.23 = (f32[136,128]{1,0:T(8,128)S(1)}, f32[136,128]{1,0:T(8,128)S(1)}, u32[]{:S(2)}, u32[]{:S(2)}) collective-permute-start(f32[136,128]{1,0:T(8,128)S(1)} %get-tuple-element.185), channel_id=1, source_target_pairs={{0,24},{4,28},{8,0},{12,4},{16,8},{20,12},{24,16},{28,20},{1,25},{... | collective-permute-start | bytes 208904 | tf_op jit(solution)/shard_map/ppermute | solution.py:350
  71.2 3.0 %shard_map.96 = (bf16[7,1024,1024]{2,1,0:T(8,128)(2,1)S(1)}, f32[8,1024,256]{2,1,0:T(8,128)S(1)}, f32[8,1024,128]{2,1,0:T(8,128)S(1)}, bf16[8,2,768,256]{3,2,1,0...) custom-call(f32[1,1024]{1,0:T(1,128)S(1)} %bitcast.264, ...), custom_call_target="tpu_custom_call", output_to_operand_aliasing={{0}: (6, {}), {1}: (7, {}), {2}: (8, {}), {3}: (9, {}), {4}... | custom-call | flops 1073741824 | bytes 1048576 | tf_op jit(solution)/shard_map/pallas_call | solution.py:334
  74.2 0.1 add_bitcast_fusion.2
  74.4 3.1 %collective-permute-start.24 = (f32[4,136,128]{2,1,0:T(8,128)S(1)}, f32[4,136,128]{2,1,0:T(8,128)S(1)}, u32[]{:S(2)}, u32[]{:S(2)}) collective-permute-start(f32[4,136,128]{2,1,0:T(8,128)S(1)} %get-tuple-element.195), channel_id=1, source_target_pairs={{0,4},{4,0},{8,12},{12,8},{16,20},{20,16},{24,28},{28,24},{1,5},{5... | collective-permute-start | bytes 835592 | tf_op jit(solution)/shard_map/ppermute | solution.py:358
  77.5 2.4 %shard_map.97 = (bf16[7,1024,1024]{2,1,0:T(8,128)(2,1)S(1)}, f32[8,1024,256]{2,1,0:T(8,128)S(1)}, f32[8,1024,128]{2,1,0:T(8,128)S(1)}, bf16[8,2,768,256]{3,2,1,0...) custom-call(f32[4,136,128]{2,1,0:T(8,128)S(1)} %get-tuple-element.19, ...), custom_call_target="tpu_custom_call", output_to_operand_aliasing={{0}: (2, {}), {1}: (3, {}), {2}: (4, {}), {3}: (5, {})} | custom-call | flops 268435456 | bytes 1048576 | tf_op jit(solution)/shard_map/pallas_call | solution.py:334
  79.9 2.4 %shard_map.98 = (bf16[7,1024,1024]{2,1,0:T(8,128)(2,1)S(1)}, f32[8,1024,256]{2,1,0:T(8,128)S(1)}, f32[8,1024,128]{2,1,0:T(8,128)S(1)}, bf16[8,2,768,256]{3,2,1,0...) custom-call(f32[4,136,128]{2,1,0:T(8,128)S(1)} %collective-permute-d, ...), custom_call_target="tpu_custom_call", output_to_operand_aliasing={{0}: (2, {}), {1}: (3, {}), {2}: (4, {}), {3}: (5, {}), {4}... | custom-call | flops 268435456 | bytes 1048576 | tf_op jit(solution)/shard_map/pallas_call | solution.py:334
  (58 shorter events, 1.2 us)
Async XLA Ops:
  5.1 3.2 %collective-permute-start = (f32[4,136,128]{2,1,0:T(8,128)S(1)}, f32[4,136,128]{2,1,0:T(8,128)S(1)}, u32[]{:S(2)}, u32[]{:S(2)}) collective-permute-start(f32[4,136,128]{2,1,0:T(8,128)S(1)} %slice.437), channel_id=1, source_target_pairs={{0,4},{4,0},{8,12},{12,8},{16,20},{20,16},{24,28},{28,24},{1,5},{5... | collective-permute-start | bytes 835592 | tf_op jit(solution)/shard_map/ppermute | solution.py:358
  8.4 7.3 %collective-permute-start.1 = (f32[136,128]{1,0:T(8,128)S(1)}, f32[136,128]{1,0:T(8,128)S(1)}, u32[]{:S(2)}, u32[]{:S(2)}) collective-permute-start(f32[136,128]{1,0:T(8,128)S(1)} %get-tuple-element.204), channel_id=1, source_target_pairs={{0,16},{4,20},{8,24},{12,28},{16,0},{20,4},{24,8},{28,12},{1,17},{... | collective-permute-start | bytes 208904 | tf_op jit(solution)/shard_map/ppermute | solution.py:350
  11.3 4.4 %collective-permute-start.2 = (f32[136,128]{1,0:T(8,128)S(1)}, f32[136,128]{1,0:T(8,128)S(1)}, u32[]{:S(2)}, u32[]{:S(2)}) collective-permute-start(f32[136,128]{1,0:T(8,128)S(1)} %get-tuple-element.205), channel_id=1, source_target_pairs={{0,8},{4,12},{8,16},{12,20},{16,24},{20,28},{24,0},{28,4},{1,9},{5... | collective-permute-start | bytes 208904 | tf_op jit(solution)/shard_map/ppermute | solution.py:350
  11.7 4.1 %collective-permute-start.3 = (f32[136,128]{1,0:T(8,128)S(1)}, f32[136,128]{1,0:T(8,128)S(1)}, u32[]{:S(2)}, u32[]{:S(2)}) collective-permute-start(f32[136,128]{1,0:T(8,128)S(1)} %get-tuple-element.203), channel_id=1, source_target_pairs={{0,24},{4,28},{8,0},{12,4},{16,8},{20,12},{24,16},{28,20},{1,25},{... | collective-permute-start | bytes 208904 | tf_op jit(solution)/shard_map/ppermute | solution.py:350
  15.8 6.1 %collective-permute-start.6 = (f32[136,128]{1,0:T(8,128)S(1)}, f32[136,128]{1,0:T(8,128)S(1)}, u32[]{:S(2)}, u32[]{:S(2)}) collective-permute-start(f32[136,128]{1,0:T(8,128)S(1)} %add_add_fusion.13.refs_0_), channel_id=1, source_target_pairs={{0,64},{32,96},{64,0},{96,32},{1,65},{33,97},{65,1},{97,33},{2,66}... | collective-permute-start | bytes 208904 | tf_op jit(solution)/shard_map/ppermute | solution.py:354
  18.8 3.5 %collective-permute-start.5 = (f32[136,128]{1,0:T(8,128)S(1)}, f32[136,128]{1,0:T(8,128)S(1)}, u32[]{:S(2)}, u32[]{:S(2)}) collective-permute-start(f32[136,128]{1,0:T(8,128)S(1)} %add_add_fusion.13.refs_0_), channel_id=1, source_target_pairs={{0,96},{32,0},{64,32},{96,64},{1,97},{33,1},{65,33},{97,65},{2,98}... | collective-permute-start | bytes 208904 | tf_op jit(solution)/shard_map/ppermute | solution.py:354
  19.5 4.4 %collective-permute-start.4 = (f32[136,128]{1,0:T(8,128)S(1)}, f32[136,128]{1,0:T(8,128)S(1)}, u32[]{:S(2)}, u32[]{:S(2)}) collective-permute-start(f32[136,128]{1,0:T(8,128)S(1)} %add_add_fusion.13.refs_0_), channel_id=1, source_target_pairs={{0,32},{32,64},{64,96},{96,0},{1,33},{33,65},{65,97},{97,1},{2,34}... | collective-permute-start | bytes 208904 | tf_op jit(solution)/shard_map/ppermute | solution.py:354
  24.0 6.0 %collective-permute-start.7 = (f32[136,128]{1,0:T(8,128)S(1)}, f32[136,128]{1,0:T(8,128)S(1)}, u32[]{:S(2)}, u32[]{:S(2)}) collective-permute-start(f32[136,128]{1,0:T(8,128)S(1)} %get-tuple-element.182), channel_id=1, source_target_pairs={{0,16},{4,20},{8,24},{12,28},{16,0},{20,4},{24,8},{28,12},{1,17},{... | collective-permute-start | bytes 208904 | tf_op jit(solution)/shard_map/ppermute | solution.py:350
  25.6 4.4 %collective-permute-start.8 = (f32[136,128]{1,0:T(8,128)S(1)}, f32[136,128]{1,0:T(8,128)S(1)}, u32[]{:S(2)}, u32[]{:S(2)}) collective-permute-start(f32[136,128]{1,0:T(8,128)S(1)} %get-tuple-element.186), channel_id=1, source_target_pairs={{0,8},{4,12},{8,16},{12,20},{16,24},{20,28},{24,0},{28,4},{1,9},{5... | collective-permute-start | bytes 208904 | tf_op jit(solution)/shard_map/ppermute | solution.py:350
  27.6 3.2 %collective-permute-start.9 = (f32[136,128]{1,0:T(8,128)S(1)}, f32[136,128]{1,0:T(8,128)S(1)}, u32[]{:S(2)}, u32[]{:S(2)}) collective-permute-start(f32[136,128]{1,0:T(8,128)S(1)} %get-tuple-element.187), channel_id=1, source_target_pairs={{0,24},{4,28},{8,0},{12,4},{16,8},{20,12},{24,16},{28,20},{1,25},{... | collective-permute-start | bytes 208904 | tf_op jit(solution)/shard_map/ppermute | solution.py:350
  28.4 7.7 %copy-start = (f32[1024]{0:T(1024)S(1)}, f32[1024]{0:T(1024)}, u32[]{:S(2)}) copy-start(f32[1024]{0:T(1024)} %param.8) | copy-start | bytes 12292
  31.0 6.5 %collective-permute-start.10 = (f32[4,136,128]{2,1,0:T(8,128)S(1)}, f32[4,136,128]{2,1,0:T(8,128)S(1)}, u32[]{:S(2)}, u32[]{:S(2)}) collective-permute-start(f32[4,136,128]{2,1,0:T(8,128)S(1)} %get-tuple-element.200), channel_id=1, source_target_pairs={{0,4},{4,0},{8,12},{12,8},{16,20},{20,16},{24,28},{28,24},{1,5},{5... | collective-permute-start | bytes 835592 | tf_op jit(solution)/shard_map/ppermute | solution.py:358
  38.8 7.7 %collective-permute-start.13 = (f32[16,128]{1,0:T(8,128)S(1)}, f32[16,128]{1,0:T(8,128)S(1)}, u32[]{:S(2)}, u32[]{:S(2)}) collective-permute-start(f32[16,128]{1,0:T(8,128)S(1)} %add.492.refs_1_), channel_id=1, source_target_pairs={{0,2},{1,3},{2,0},{3,1},{4,6},{5,7},{6,4},{7,5},{8,10},{9,11},{10,... | collective-permute-start | bytes 24584 | tf_op jit(solution)/shard_map/ppermute | solution.py:460
  42.5 4.0 %collective-permute-start.12 = (f32[16,128]{1,0:T(8,128)S(1)}, f32[16,128]{1,0:T(8,128)S(1)}, u32[]{:S(2)}, u32[]{:S(2)}) collective-permute-start(f32[16,128]{1,0:T(8,128)S(1)} %add.492.refs_1_), channel_id=1, source_target_pairs={{0,3},{1,0},{2,1},{3,2},{4,7},{5,4},{6,5},{7,6},{8,11},{9,8},{10,9... | collective-permute-start | bytes 24584 | tf_op jit(solution)/shard_map/ppermute | solution.py:460
  42.9 3.7 %collective-permute-start.11 = (f32[16,128]{1,0:T(8,128)S(1)}, f32[16,128]{1,0:T(8,128)S(1)}, u32[]{:S(2)}, u32[]{:S(2)}) collective-permute-start(f32[16,128]{1,0:T(8,128)S(1)} %add.492.refs_1_), channel_id=1, source_target_pairs={{0,1},{1,2},{2,3},{3,0},{4,5},{5,6},{6,7},{7,4},{8,9},{9,10},{10,1... | collective-permute-start | bytes 24584 | tf_op jit(solution)/shard_map/ppermute | solution.py:460
  49.3 4.0 %collective-permute-start.14 = (f32[4,136,128]{2,1,0:T(8,128)S(1)}, f32[4,136,128]{2,1,0:T(8,128)S(1)}, u32[]{:S(2)}, u32[]{:S(2)}) collective-permute-start(f32[4,136,128]{2,1,0:T(8,128)S(1)} %slice.445), channel_id=1, source_target_pairs={{0,4},{4,0},{8,12},{12,8},{16,20},{20,16},{24,28},{28,24},{1,5},{5... | collective-permute-start | bytes 835592 | tf_op jit(solution)/shard_map/ppermute | solution.py:358
  53.5 6.1 %collective-permute-start.15 = (f32[136,128]{1,0:T(8,128)S(1)}, f32[136,128]{1,0:T(8,128)S(1)}, u32[]{:S(2)}, u32[]{:S(2)}) collective-permute-start(f32[136,128]{1,0:T(8,128)S(1)} %get-tuple-element.198), channel_id=1, source_target_pairs={{0,16},{4,20},{8,24},{12,28},{16,0},{20,4},{24,8},{28,12},{1,17},{... | collective-permute-start | bytes 208904 | tf_op jit(solution)/shard_map/ppermute | solution.py:350
  53.9 6.8 %collective-permute-start.16 = (f32[136,128]{1,0:T(8,128)S(1)}, f32[136,128]{1,0:T(8,128)S(1)}, u32[]{:S(2)}, u32[]{:S(2)}) collective-permute-start(f32[136,128]{1,0:T(8,128)S(1)} %get-tuple-element.199), channel_id=1, source_target_pairs={{0,8},{4,12},{8,16},{12,20},{16,24},{20,28},{24,0},{28,4},{1,9},{5... | collective-permute-start | bytes 208904 | tf_op jit(solution)/shard_map/ppermute | solution.py:350
  55.7 5.0 %collective-permute-start.17 = (f32[136,128]{1,0:T(8,128)S(1)}, f32[136,128]{1,0:T(8,128)S(1)}, u32[]{:S(2)}, u32[]{:S(2)}) collective-permute-start(f32[136,128]{1,0:T(8,128)S(1)} %get-tuple-element.197), channel_id=1, source_target_pairs={{0,24},{4,28},{8,0},{12,4},{16,8},{20,12},{24,16},{28,20},{1,25},{... | collective-permute-start | bytes 208904 | tf_op jit(solution)/shard_map/ppermute | solution.py:350
  60.7 7.1 %collective-permute-start.20 = (f32[136,128]{1,0:T(8,128)S(1)}, f32[136,128]{1,0:T(8,128)S(1)}, u32[]{:S(2)}, u32[]{:S(2)}) collective-permute-start(f32[136,128]{1,0:T(8,128)S(1)} %add_add_fusion.7.refs_5_), channel_id=1, source_target_pairs={{0,64},{32,96},{64,0},{96,32},{1,65},{33,97},{65,1},{97,33},{2,66}... | collective-permute-start | bytes 208904 | tf_op jit(solution)/shard_map/ppermute | solution.py:354
  61.0 6.9 %collective-permute-start.19 = (f32[136,128]{1,0:T(8,128)S(1)}, f32[136,128]{1,0:T(8,128)S(1)}, u32[]{:S(2)}, u32[]{:S(2)}) collective-permute-start(f32[136,128]{1,0:T(8,128)S(1)} %add_add_fusion.7.refs_5_), channel_id=1, source_target_pairs={{0,32},{32,64},{64,96},{96,0},{1,33},{33,65},{65,97},{97,1},{2,34}... | collective-permute-start | bytes 208904 | tf_op jit(solution)/shard_map/ppermute | solution.py:354
  61.1 6.8 %collective-permute-start.18 = (f32[136,128]{1,0:T(8,128)S(1)}, f32[136,128]{1,0:T(8,128)S(1)}, u32[]{:S(2)}, u32[]{:S(2)}) collective-permute-start(f32[136,128]{1,0:T(8,128)S(1)} %add_add_fusion.7.refs_5_), channel_id=1, source_target_pairs={{0,96},{32,0},{64,32},{96,64},{1,97},{33,1},{65,33},{97,65},{2,98}... | collective-permute-start | bytes 208904 | tf_op jit(solution)/shard_map/ppermute | solution.py:354
  67.9 6.2 %collective-permute-start.21 = (f32[136,128]{1,0:T(8,128)S(1)}, f32[136,128]{1,0:T(8,128)S(1)}, u32[]{:S(2)}, u32[]{:S(2)}) collective-permute-start(f32[136,128]{1,0:T(8,128)S(1)} %get-tuple-element.178), channel_id=1, source_target_pairs={{0,16},{4,20},{8,24},{12,28},{16,0},{20,4},{24,8},{28,12},{1,17},{... | collective-permute-start | bytes 208904 | tf_op jit(solution)/shard_map/ppermute | solution.py:350
  68.4 5.8 %collective-permute-start.22 = (f32[136,128]{1,0:T(8,128)S(1)}, f32[136,128]{1,0:T(8,128)S(1)}, u32[]{:S(2)}, u32[]{:S(2)}) collective-permute-start(f32[136,128]{1,0:T(8,128)S(1)} %get-tuple-element.184), channel_id=1, source_target_pairs={{0,8},{4,12},{8,16},{12,20},{16,24},{20,28},{24,0},{28,4},{1,9},{5... | collective-permute-start | bytes 208904 | tf_op jit(solution)/shard_map/ppermute | solution.py:350
  69.8 4.3 %collective-permute-start.23 = (f32[136,128]{1,0:T(8,128)S(1)}, f32[136,128]{1,0:T(8,128)S(1)}, u32[]{:S(2)}, u32[]{:S(2)}) collective-permute-start(f32[136,128]{1,0:T(8,128)S(1)} %get-tuple-element.185), channel_id=1, source_target_pairs={{0,24},{4,28},{8,0},{12,4},{16,8},{20,12},{24,16},{28,20},{1,25},{... | collective-permute-start | bytes 208904 | tf_op jit(solution)/shard_map/ppermute | solution.py:350
  74.4 5.5 %collective-permute-start.24 = (f32[4,136,128]{2,1,0:T(8,128)S(1)}, f32[4,136,128]{2,1,0:T(8,128)S(1)}, u32[]{:S(2)}, u32[]{:S(2)}) collective-permute-start(f32[4,136,128]{2,1,0:T(8,128)S(1)} %get-tuple-element.195), channel_id=1, source_target_pairs={{0,4},{4,0},{8,12},{12,8},{16,20},{20,16},{24,28},{28,24},{1,5},{5... | collective-permute-start | bytes 835592 | tf_op jit(solution)/shard_map/ppermute | solution.py:358
